TPU v7x, 32 devices: a whole 2x2x4 slice. The times are simulated.
32 devices in a mesh: seq: 8 (over z, y), mp: 4 (over x, core).
Axes of the slice: x: 2, y: 2, z: 4, core: 2. Of those that a mesh axis runs over, the one named last changes fastest.
Arguments:
- tokens: bfloat16 [4608, 2048], P('seq'), may hold values from -6 to 6
- attn_gain: bfloat16 [2048], replicated, may hold values from 0.5 to 1.5
- w_input: bfloat16 [2048, 2048], P(None, 'mp'), may hold values from -0.125 to 0.125
- w_forget: bfloat16 [2048, 2048], P(None, 'mp'), may hold values from -0.125 to 0.125
- w_rgate: bfloat16 [2048, 2048], P(None, 'mp'), may hold values from -0.125 to 0.125
- gnorm_gain: bfloat16 [2048], P('mp'), may hold values from 0.5 to 1.5
- lower_bound: float32 [2048], P('mp'), may hold values from 0.4 to 0.99999
- w_out: bfloat16 [2048, 2048], P('mp'), may hold values from -0.125 to 0.125
- mlp_gain: bfloat16 [2048], replicated, may hold values from 0.5 to 1.5
- w_gate: bfloat16 [2048, 5632], P(None, 'mp'), may hold values from -0.125 to 0.125
- w_up: bfloat16 [2048, 5632], P(None, 'mp'), may hold values from -0.125 to 0.125
- w_down: bfloat16 [5632, 2048], P('mp'), may hold values from -0.078125 to 0.078125
- local_lengths: int32 [8, 3], P('seq'), may hold values from 1 to 240, 320 in all within a row
- cotangent: bfloat16 [4608, 2048], P('seq'), may hold values from -6 to 6
Outputs:
- mixed_out: bfloat16 [4608, 2048], P('seq')
- grad_tokens: bfloat16 [4608, 2048], P('seq')
- grad_attn_gain: float32 [2048], P('seq')
- grad_w_input: float32 [2048, 2048], P('seq', 'mp')
- grad_w_forget: float32 [2048, 2048], P('seq', 'mp')
- grad_w_rgate: float32 [2048, 2048], P('seq', 'mp')
- grad_gnorm_gain: float32 [4, 512], P('mp', 'seq')
- grad_lower_bound: float32 [4, 512], P('mp', 'seq')
- grad_w_out: float32 [2048, 2048], P('mp', 'seq')
- grad_mlp_gain: float32 [2048], P('seq')
- grad_w_gate: float32 [2048, 5632], P('seq', 'mp')
- grad_w_up: float32 [2048, 5632], P('seq', 'mp')
- grad_w_down: float32 [5632, 2048], P('mp', 'seq')
Inputs may be any that keep to these rules, and one draw needn't show every extreme that they name: `local_lengths`: each row holds the lengths of the 3 short sequences of one block, in order; they sum to 320, the longest is 240.
All inputs are finite; a program needn't handle non-finite values.
Results may differ from a plain program's by a relative error of at most 0.008.
Values sent between devices are 32-bit elements; how exact they have to be, the bound alone decides.
No kernel may reach another device: no remote copies, remote signals or barrier semaphores. Data moves between devices by JAX's collectives and lax.ppermute only.
A program may use at most 256 MiB of HBM per device.

v0:
```python
import jax
import jax.numpy as jnp
from jax import lax
from jax.sharding import PartitionSpec as P

LCHUNK = 256


norm_eps = 1e-06


def prefix(value, axis, join, neutral, backward):
    count, mine = (lax.axis_size(axis), lax.axis_index(axis))
    pieces = jax.tree.map(lambda part: lax.all_gather(part, axis), value)
    if backward:
        pieces = jax.tree.map(lambda part: part[::-1], pieces)
        mine = count - 1 - mine
    subtotal = jax.tree.map(
        lambda part, zero: jnp.full_like(part, 0) + jnp.asarray(zero, part.dtype), value, neutral
    )

    def hop(position, subtotal):
        longer = join(subtotal, jax.tree.map(lambda part: part[position], pieces))
        return jax.tree.map(lambda new, old: jnp.where(position < mine, new, old), longer, subtotal)

    return lax.fori_loop(0, count - 1, hop, subtotal)


def compose(earlier, later):
    return (earlier[0] * later[0], later[0] * earlier[1] + later[1])


def linear_scan(decay, source):
    return lax.associative_scan(compose, (decay, source), axis=0)


def reverse_scan(decay, source):
    flipped_decay, flipped_state = linear_scan(jnp.flip(decay, 0), jnp.flip(source, 0))
    return (jnp.flip(flipped_decay, 0), jnp.flip(flipped_state, 0))


def left_dot(left, right):
    return lax.dot_general(
        left, right, (((0,), (0,)), ((), ())), preferred_element_type=jnp.float32
    )


def right_dot(left, right):
    return lax.dot_general(
        left, right, (((1,), (1,)), ((), ())), preferred_element_type=jnp.float32
    )


def silu_slope(values):
    sigmoid_values = jax.nn.sigmoid(values)
    return sigmoid_values * (1.0 + values * (1.0 - sigmoid_values))


def per_device(
    tokens,
    attn_gain,
    w_input,
    w_forget,
    w_rgate,
    gnorm_gain,
    lower_bound,
    w_out,
    mlp_gain,
    w_gate,
    w_up,
    w_down,
    local_lengths,
    cotangent,
):
    width = tokens.shape[1]
    lengths_row = local_lengths[0]
    offsets = jnp.cumsum(lengths_row) - lengths_row
    short_rows = tokens.shape[0] - LCHUNK
    starts = jnp.any(jnp.arange(short_rows, dtype=jnp.int32)[:, None] == offsets[None, :], axis=1)[
        :, None
    ]
    stream = tokens.astype(jnp.float32)
    first_gain = attn_gain.astype(jnp.float32)
    first_scale = lax.rsqrt(jnp.mean(stream * stream, axis=1, keepdims=True) + norm_eps)
    first_hat = stream * first_scale
    normed_one = (first_hat * first_gain).astype(jnp.bfloat16)
    pre_input = jnp.dot(normed_one, w_input, preferred_element_type=jnp.float32)
    pre_forget = jnp.dot(normed_one, w_forget, preferred_element_type=jnp.float32)
    pre_rgate = jnp.dot(normed_one, w_rgate, preferred_element_type=jnp.float32)
    forget_sig = jax.nn.sigmoid(pre_forget)
    forget = lower_bound + (1.0 - lower_bound) * forget_sig
    input_act = jax.nn.silu(pre_input)
    drive = input_act * (1.0 - forget)
    long_forget = forget[:LCHUNK]
    short_forget = forget[LCHUNK:]
    long_decay, long_local = linear_scan(long_forget, drive[:LCHUNK])
    identity = (jnp.ones_like(long_decay[0]), jnp.zeros_like(long_decay[0]))
    prefix_decay, carry_in = prefix(
        (long_decay[-1], long_local[-1]), "seq", compose, identity, False
    )
    long_state = long_local + long_decay * carry_in[None, :]
    short_decay = jnp.where(starts, jnp.zeros_like(short_forget), short_forget)
    short_prod, short_state = linear_scan(short_decay, drive[LCHUNK:])
    states = jnp.concatenate([long_state, short_state], axis=0)
    squares = lax.psum(jnp.sum(states * states, axis=1), "mp")
    state_scale = lax.rsqrt(squares / width + norm_eps)[:, None]
    normed_state = states * state_scale
    state_gain = gnorm_gain.astype(jnp.float32)
    rgate_act = jax.nn.silu(pre_rgate)
    gated = (normed_state * state_gain * rgate_act).astype(jnp.bfloat16)
    branch = lax.psum(jnp.dot(gated, w_out, preferred_element_type=jnp.float32), "mp")
    middle = stream + branch
    second_gain = mlp_gain.astype(jnp.float32)
    second_scale = lax.rsqrt(jnp.mean(middle * middle, axis=1, keepdims=True) + norm_eps)
    second_hat = middle * second_scale
    normed_two = (second_hat * second_gain).astype(jnp.bfloat16)
    gate = jnp.dot(normed_two, w_gate, preferred_element_type=jnp.float32)
    up_values = jnp.dot(normed_two, w_up, preferred_element_type=jnp.float32)
    gate_act = jax.nn.silu(gate)
    hidden = (gate_act * up_values).astype(jnp.bfloat16)
    feed = lax.psum(jnp.dot(hidden, w_down, preferred_element_type=jnp.float32), "mp")
    mixed_out = (middle + feed).astype(jnp.bfloat16)
    out_grad = cotangent.astype(jnp.float32)
    grad_w_down = left_dot(hidden, cotangent)
    d_hidden = right_dot(cotangent, w_down)
    d_gate = (d_hidden * up_values * silu_slope(gate)).astype(jnp.bfloat16)
    d_up = (d_hidden * gate_act).astype(jnp.bfloat16)
    grad_w_gate = left_dot(normed_two, d_gate)
    grad_w_up = left_dot(normed_two, d_up)
    d_normed_two = lax.psum(right_dot(d_gate, w_gate) + right_dot(d_up, w_up), "mp")
    grad_mlp_gain = jnp.sum(d_normed_two * second_hat, axis=0)
    second_term = d_normed_two * second_gain
    d_middle = out_grad + second_scale * (
        second_term - second_hat * jnp.mean(second_term * second_hat, axis=1, keepdims=True)
    )
    d_branch = d_middle.astype(jnp.bfloat16)
    grad_w_out = left_dot(gated, d_branch)
    d_gated = right_dot(d_branch, w_out)
    grad_gnorm = jnp.sum(d_gated * normed_state * rgate_act, axis=0)
    d_rgate = (d_gated * normed_state * state_gain * silu_slope(pre_rgate)).astype(jnp.bfloat16)
    d_normed = d_gated * state_gain * rgate_act
    inner = lax.psum(jnp.sum(d_normed * normed_state, axis=1), "mp")
    d_states = state_scale * (d_normed - normed_state * (inner / width)[:, None])
    long_links = jnp.concatenate([long_forget[1:], jnp.ones_like(long_forget[:1])], axis=0)
    back_decay, back_local = reverse_scan(long_links, d_states[:LCHUNK])
    alpha_map = long_forget[0] * back_decay[0]
    beta_map = long_forget[0] * back_local[0]
    suffix_decay, carried_in = prefix((alpha_map, beta_map), "seq", compose, identity, True)
    long_carried = back_local + back_decay * carried_in[None, :]
    short_next = jnp.where(starts[1:], jnp.zeros_like(short_forget[1:]), short_forget[1:])
    short_links = jnp.concatenate([short_next, jnp.zeros_like(short_forget[:1])], axis=0)
    short_back_prod, short_carried = reverse_scan(short_links, d_states[LCHUNK:])
    carried = jnp.concatenate([long_carried, short_carried], axis=0)
    long_prev = jnp.concatenate([carry_in[None, :], long_state[:-1]], axis=0)
    short_shift = jnp.concatenate([jnp.zeros_like(short_state[:1]), short_state[:-1]], axis=0)
    short_prev = jnp.where(starts, jnp.zeros_like(short_shift), short_shift)
    states_prev = jnp.concatenate([long_prev, short_prev], axis=0)
    d_forget = carried * states_prev - carried * input_act
    d_input = (carried * (1.0 - forget) * silu_slope(pre_input)).astype(jnp.bfloat16)
    d_pforget = (d_forget * (1.0 - lower_bound) * forget_sig * (1.0 - forget_sig)).astype(
        jnp.bfloat16
    )
    grad_bound = jnp.sum(d_forget * (1.0 - forget_sig), axis=0)
    grad_w_input = left_dot(normed_one, d_input)
    grad_w_forget = left_dot(normed_one, d_pforget)
    grad_w_rgate = left_dot(normed_one, d_rgate)
    d_normed_one = lax.psum(
        right_dot(d_input, w_input) + right_dot(d_pforget, w_forget) + right_dot(d_rgate, w_rgate),
        "mp",
    )
    grad_first = jnp.sum(d_normed_one * first_hat, axis=0)
    first_term = d_normed_one * first_gain
    d_stream = d_middle + first_scale * (
        first_term - first_hat * jnp.mean(first_term * first_hat, axis=1, keepdims=True)
    )
    grad_tokens = d_stream.astype(jnp.bfloat16)
    gathered = (
        lax.psum_scatter(grad_first, "seq", scatter_dimension=0, tiled=True),
        lax.psum_scatter(grad_w_input, "seq", scatter_dimension=0, tiled=True),
        lax.psum_scatter(grad_w_forget, "seq", scatter_dimension=0, tiled=True),
        lax.psum_scatter(grad_w_rgate, "seq", scatter_dimension=0, tiled=True),
        lax.psum_scatter(grad_gnorm[None, :], "seq", scatter_dimension=1, tiled=True),
        lax.psum_scatter(grad_bound[None, :], "seq", scatter_dimension=1, tiled=True),
        lax.psum_scatter(grad_w_out, "seq", scatter_dimension=1, tiled=True),
        lax.psum_scatter(grad_mlp_gain, "seq", scatter_dimension=0, tiled=True),
        lax.psum_scatter(grad_w_gate, "seq", scatter_dimension=0, tiled=True),
        lax.psum_scatter(grad_w_up, "seq", scatter_dimension=0, tiled=True),
        lax.psum_scatter(grad_w_down, "seq", scatter_dimension=1, tiled=True),
    )
    return (
        mixed_out,
        grad_tokens,
        gathered[0],
        gathered[1],
        gathered[2],
        gathered[3],
        gathered[4],
        gathered[5],
        gathered[6],
        gathered[7],
        gathered[8],
        gathered[9],
        gathered[10],
    )


def solution(mesh):
    in_specs = (
        P("seq", None),
        P(),
        P(None, "mp"),
        P(None, "mp"),
        P(None, "mp"),
        P("mp"),
        P("mp"),
        P("mp", None),
        P(),
        P(None, "mp"),
        P(None, "mp"),
        P("mp", None),
        P("seq", None),
        P("seq", None),
    )
    out_specs = (
        P("seq", None),
        P("seq", None),
        P("seq"),
        P("seq", "mp"),
        P("seq", "mp"),
        P("seq", "mp"),
        P("mp", "seq"),
        P("mp", "seq"),
        P("mp", "seq"),
        P("seq"),
        P("seq", "mp"),
        P("seq", "mp"),
        P("mp", "seq"),
    )
    return jax.shard_map(
        per_device, mesh=mesh, in_specs=in_specs, out_specs=out_specs, check_vma=False
    )
```

profile of v0, /device:TPU:0, one launch (start us, length us, event | category | flops | bytes accessed | tf_op | source)
XLA Modules:
  0.0 2039.9 jit_solution(8637172442298498642)
XLA Ops:
  164.7 27.8 %all-gather.1 = f32[8,1,512]{2,1,0:T(1,128)S(1)} all-gather(f32[1,1,512]{2,1,0:T(1,128)S(1)} %add_bitcast_fusion), channel_id=1, replica_groups=mesh['seq'=8,'mp'=4] {'seq'}, dimensions={0}, use_global_device_ids=true | all-gather | bytes 18432 | tf_op jit(solution)/shard_map/all_gather | solution.py:14
  195.5 26.0 %all-gather = f32[8,1,512]{2,1,0:T(1,128)S(1)} all-gather(f32[1,1,512]{2,1,0:T(1,128)S(1)} %add_bitcast_fusion.1), channel_id=1, replica_groups=mesh['seq'=8,'mp'=4] {'seq'}, dimensions={0}, use_global_device_ids=true | all-gather | bytes 18432 | tf_op jit(solution)/shard_map/all_gather | solution.py:14
  221.5 12.6 while.28
  272.1 5.9 psum.42
  278.0 5.3 multiply_convert_fusion.7
  288.4 91.7 %all-reduce.108.cloned.1.call-done = f32[576,2048]{1,0:T(8,128)} async-done(((f32[576,2048]{1,0:T(8,128)}), f32[576,2048]{1,0:T(8,128)}) %all-reduce.108.cloned.1.call-update) | async-done | bytes 4718608 | tf_op jit(solution)/shard_map/psum | solution.py:111
  380.1 3.8 multiply_reduce_fusion.2
  386.3 7.6 fusion.102
  394.0 5.5 fusion.101
  399.5 9.7 multiply_convert_fusion.1
  409.3 5.4 fusion.104
  414.7 5.6 convolution_add_fusion
  446.4 4.4 slice.1145
  450.8 4.6 slice.1135
  455.4 4.5 slice.1137
  462.4 8.3 fusion.103
  470.7 44.0 %all-reduce.110.cloned.1.call-done = f32[576,2048]{1,0:T(8,128)} async-done(((f32[576,2048]{1,0:T(8,128)}), f32[576,2048]{1,0:T(8,128)}) %all-reduce.110.cloned.1.call-update) | async-done | bytes 4718608 | tf_op jit(solution)/shard_map/psum | solution.py:130
  514.7 5.6 multiply_reduce_fusion
  520.6 3.8 multiply_add_fusion
  524.4 3.7 multiply_reduce_fusion.4
  528.2 6.0 psum.46
  677.7 4.4 slice.1140
  682.1 4.4 slice.1142
  722.6 4.7 rev.21
  727.4 4.7 rev.22
  732.1 26.3 %all-gather.3 = f32[8,1,512]{2,1,0:T(1,128)S(1)} all-gather(f32[1,1,512]{2,1,0:T(1,128)S(1)} %copy-done.67), channel_id=1, replica_groups=mesh['seq'=8,'mp'=4] {'seq'}, dimensions={0}, use_global_device_ids=true | all-gather | bytes 18432 | tf_op jit(solution)/shard_map/all_gather | solution.py:14
  758.5 26.0 %all-gather.2 = f32[8,1,512]{2,1,0:T(1,128)S(1)} all-gather(f32[1,1,512]{2,1,0:T(1,128)S(1)} %copy-done.66), channel_id=1, replica_groups=mesh['seq'=8,'mp'=4] {'seq'}, dimensions={0}, use_global_device_ids=true | all-gather | bytes 18432 | tf_op jit(solution)/shard_map/all_gather | solution.py:14
  785.0 4.6 slice.1197
  823.0 6.6 rev.25
  844.0 8.0 add_add_fusion
  853.1 6.2 fusion.17
  860.0 5.7 fusion.63
  866.8 5.7 fusion.65
  873.6 5.8 fusion.61
  879.7 11.1 fusion.109
  890.9 9.5 fusion.108
  900.5 9.8 fusion.107
  914.9 159.2 %all-reduce.112.cloned.1.call-done = (f32[576,2048]{1,0:T(8,128)}, f32[576,2048]{1,0:T(8,128)}) async-done(((f32[576,2048]{1,0:T(8,128)}, f32[576,2048]{1,0:T(8,128)}), (f32[576,2048]{1,0:T(8,128)}, f32[576,2048]{1,0:T(8,128)})) %all-reduce.112.cloned.1.call-update) | async-done | bytes 9437200 | tf_op jit(solution)/shard_map/psum | solution.py:121
  1074.1 4.4 fusion.10
  1078.5 39.2 %all-reduce.102 = (f32[2048]{0:T(1024)S(1)}, f32[2048]{0:T(1024)S(1)}) all-reduce(f32[2048]{0:T(1024)S(1)} %get-tuple-element.241, f32[2048]{0:T(1024)S(1)} %copy-done.49), channel_id=2, replica_groups=mesh['seq'=8,'mp'=4] {'seq'}, use_global_device_ids=true, to_apply=%region_19.20.clone | all-reduce | flops 4096 | bytes 32768
  1118.9 6.2 add_convert_fusion
  1129.8 37.3 %reduce-scatter.20.cloned.1.call-done = f32[512,256]{1,0:T(8,128)} async-done(((f32[512,2048]{1,0:T(8,128)}), f32[512,256]{1,0:T(8,128)}) %reduce-scatter.20.cloned.1.call-update) | async-done | bytes 524304 | tf_op jit(solution)/shard_map/reduce_scatter | solution.py:184
  1167.1 92.3 %reduce-scatter.16.cloned.1.call-done = f32[256,512]{1,0:T(8,128)} async-done(((f32[2048,512]{1,0:T(8,128)}), f32[256,512]{1,0:T(8,128)}) %reduce-scatter.16.cloned.1.call-update) | async-done | bytes 524304 | tf_op jit(solution)/shard_map/reduce_scatter | solution.py:180
  1259.4 91.9 %reduce-scatter.14.cloned.1.call-done = f32[256,512]{1,0:T(8,128)} async-done(((f32[2048,512]{1,0:T(8,128)}), f32[256,512]{1,0:T(8,128)}) %reduce-scatter.14.cloned.1.call-update) | async-done | bytes 524304 | tf_op jit(solution)/shard_map/reduce_scatter | solution.py:179
  1351.3 92.5 %reduce-scatter.18.cloned.1.call-done = f32[256,512]{1,0:T(8,128)} async-done(((f32[2048,512]{1,0:T(8,128)}), f32[256,512]{1,0:T(8,128)}) %reduce-scatter.18.cloned.1.call-update) | async-done | bytes 524304 | tf_op jit(solution)/shard_map/reduce_scatter | solution.py:181
  1443.8 196.9 %reduce-scatter.26.cloned.1.call-done = f32[1408,256]{1,0:T(8,128)} async-done(((f32[1408,2048]{1,0:T(8,128)}), f32[1408,256]{1,0:T(8,128)}) %reduce-scatter.26.cloned.1.call-update) | async-done | bytes 1441808 | tf_op jit(solution)/shard_map/reduce_scatter | solution.py:188
  1640.7 196.0 %reduce-scatter.24.cloned.1.call-done = f32[256,1408]{1,0:T(8,128)} async-done(((f32[2048,1408]{1,0:T(8,128)}), f32[256,1408]{1,0:T(8,128)}) %reduce-scatter.24.cloned.1.call-update) | async-done | bytes 1441808 | tf_op jit(solution)/shard_map/reduce_scatter | solution.py:187
  1836.7 195.8 %reduce-scatter.22.cloned.1.call-done = f32[256,1408]{1,0:T(8,128)} async-done(((f32[2048,1408]{1,0:T(8,128)}), f32[256,1408]{1,0:T(8,128)}) %reduce-scatter.22.cloned.1.call-update) | async-done | bytes 1441808 | tf_op jit(solution)/shard_map/reduce_scatter | solution.py:186
  (717 shorter events, 488.8 us)
Async XLA Ops:
  7.2 372.9 %all-reduce.108.cloned.1.call-start = ((), (), s32[]{:S(2)}) async-start(), calls=%async_computation.9 | async-start | bytes 9437184 | tf_op jit(solution)/shard_map/psum | solution.py:111
  68.9 11.2 copy-start.71
  104.0 17.9 copy-start.68
  118.3 7.9 copy-start.57
  120.3 17.6 copy-start.56
  121.9 17.6 copy-start.55
  141.1 12.6 copy-start.54
  148.1 8.9 copy-start.64
  153.7 39.3 %copy-start.26 = (f32[128,512]{1,0:T(8,128)S(1)}, f32[128,512]{1,0:T(8,128)}, u32[]{:S(2)}) copy-start(f32[128,512]{1,0:T(8,128)} %add.731) | copy-start | bytes 786436
  194.7 48.1 %copy-start.36 = (f32[9,512]{1,0:T(8,128)S(1)}, f32[9,512]{1,0:T(8,128)}, u32[]{:S(2)}) copy-start(f32[9,512]{1,0:T(8,128)} %slice.1015) | copy-start | bytes 55300
  194.7 48.1 %copy-start.37 = (f32[9,512]{1,0:T(8,128)S(1)}, f32[9,512]{1,0:T(8,128)}, u32[]{:S(2)}) copy-start(f32[9,512]{1,0:T(8,128)} %slice.1039) | copy-start | bytes 55300
  194.7 50.2 %copy-start.34 = (f32[19,512]{1,0:T(8,128)S(1)}, f32[19,512]{1,0:T(8,128)}, u32[]{:S(2)}) copy-start(f32[19,512]{1,0:T(8,128)} %slice.1009) | copy-start | bytes 116740
  221.5 26.5 %copy-start.32 = (f32[39,512]{1,0:T(8,128)S(1)}, f32[39,512]{1,0:T(8,128)}, u32[]{:S(2)}) copy-start(f32[39,512]{1,0:T(8,128)} %slice.1003) | copy-start | bytes 239620
  253.4 8.9 copy-start.63
  263.0 14.9 copy-start.44
  263.1 14.9 copy-start.47
  263.1 14.9 copy-start.52
  287.7 226.9 %all-reduce.110.cloned.1.call-start = ((), (), s32[]{:S(2)}) async-start(), calls=%async_computation.10 | async-start | bytes 9437184 | tf_op jit(solution)/shard_map/psum | solution.py:130
  383.9 10.0 slice-start.2
  394.0 20.7 %slice-start.4 = ((s8[5767168]{0:T(1024)(128)(4,1)}), s8[4194304]{0:T(1024)(128)(4,1)S(1)}, s32[]{:S(2)}) async-start(s8[5767168]{0:T(1024)(128)(4,1)} %bitcast.97), calls=%async_computation.25 | async-start | bytes 8388608
  399.5 15.2 slice-start.5
  420.3 491.9 %reduce-scatter.28.cloned.1.call-start = ((), (), s32[]{:S(2)}) async-start(), calls=%async_computation.18 | async-start | bytes 294912
  446.4 15.0 copy-start.73
  560.3 51.9 %copy-start.25 = (f32[127,512]{1,0:T(8,128)S(1)}, f32[127,512]{1,0:T(8,128)}, u32[]{:S(2)}) copy-start(f32[127,512]{1,0:T(8,128)} %slice.1113) | copy-start | bytes 780292
  612.2 14.2 copy-start.61
  612.2 14.3 copy-start.60
  620.6 17.4 copy-start.59
  622.8 16.9 copy-start.58
  646.0 8.0 copy-start.65
  653.2 9.3 copy-start.27
  716.7 67.9 %copy-start.40 = (f32[512]{0:T(512)S(1)}, f32[512]{0:T(512)}, u32[]{:S(2)}) copy-start(f32[512]{0:T(512)} %custom-call.1) | copy-start | bytes 6148
  718.5 13.6 copy-start.67
  721.0 37.5 %copy-start.66 = (f32[1,1,512]{2,1,0:T(1,128)S(1)}, f32[1,1,512]{2,1,0:T(1,128)}, u32[]{:S(2)}) copy-start(f32[1,1,512]{2,1,0:T(1,128)} %get-tuple-element.285) | copy-start | bytes 6148
  721.0 76.1 %copy-start.35 = (f32[19,512]{1,0:T(8,128)S(1)}, f32[19,512]{1,0:T(8,128)}, u32[]{:S(2)}) copy-start(f32[19,512]{1,0:T(8,128)} %slice.1158) | copy-start | bytes 116740
  722.6 191.0 %reduce-scatter.30.cloned.1.call-start = ((), (), s32[]{:S(2)}) async-start(), calls=%async_computation.19 | async-start | bytes 294912
  805.6 8.9 copy-start.62
  818.0 11.6 copy-start.42
  820.8 10.3 copy-start.39
  843.8 230.3 %all-reduce.112.cloned.1.call-start = ((), (), s32[]{:S(2)}) async-start(), calls=%async_computation.20 | async-start | bytes 18874368 | tf_op jit(solution)/shard_map/psum | solution.py:121
  852.1 315.0 %reduce-scatter.20.cloned.1.call-start = ((), (), s32[]{:S(2)}) async-start(), calls=%async_computation.14 | async-start | bytes 4718592 | tf_op jit(solution)/shard_map/reduce_scatter | solution.py:184
  859.4 400.1 %reduce-scatter.16.cloned.1.call-start = ((), (), s32[]{:S(2)}) async-start(), calls=%async_computation.12 | async-start | bytes 4718592 | tf_op jit(solution)/shard_map/reduce_scatter | solution.py:180
  865.8 485.5 %reduce-scatter.14.cloned.1.call-start = ((), (), s32[]{:S(2)}) async-start(), calls=%async_computation.11 | async-start | bytes 4718592 | tf_op jit(solution)/shard_map/reduce_scatter | solution.py:179
  872.6 571.2 %reduce-scatter.18.cloned.1.call-start = ((), (), s32[]{:S(2)}) async-start(), calls=%async_computation.13 | async-start | bytes 4718592 | tf_op jit(solution)/shard_map/reduce_scatter | solution.py:181
  879.4 761.3 %reduce-scatter.26.cloned.1.call-start = ((), (), s32[]{:S(2)}) async-start(), calls=%async_computation.17 | async-start | bytes 12976128 | tf_op jit(solution)/shard_map/reduce_scatter | solution.py:188
  890.9 945.9 %reduce-scatter.24.cloned.1.call-start = ((), (), s32[]{:S(2)}) async-start(), calls=%async_computation.16 | async-start | bytes 12976128 | tf_op jit(solution)/shard_map/reduce_scatter | solution.py:187
  900.4 1132.2 %reduce-scatter.22.cloned.1.call-start = ((), (), s32[]{:S(2)}) async-start(), calls=%async_computation.15 | async-start | bytes 12976128 | tf_op jit(solution)/shard_map/reduce_scatter | solution.py:186
  1074.1 51.1 %slice-start = ((s8[4718592]{0:T(1024)(128)(4,1)}), s8[524288]{0:T(1024)(128)(4,1)S(1)}, s32[]{:S(2)}) async-start(s8[4718592]{0:T(1024)(128)(4,1)} %bitcast.77), calls=%async_computation.21 | async-start | bytes 1048576
  1118.9 8.1 copy-start.6
  (48 other events, 154.2 us)
Sparse Core Ops, SparseCore 0:
  287.9 92.2 all-reduce.107
  420.4 94.1 all-reduce.109
  722.7 61.7 reduce-scatter.27
  843.9 58.4 reduce-scatter.29
  904.8 169.2 all-reduce.111
  1078.2 88.9 reduce-scatter.19
  1171.8 87.6 reduce-scatter.15
  1263.6 87.6 reduce-scatter.13
  1356.0 87.7 reduce-scatter.17
  1447.8 192.8 reduce-scatter.25
  1644.9 191.7 reduce-scatter.23
  1840.8 191.7 reduce-scatter.21
where the time goes:
time: 2060 us; the launch traced here: 2040 us
  waiting for transfers between devices  1200 us (58%)
  local copies, waits for them, and re-layouts  357 us (17%)
  other arithmetic  180 us (9%)
  blocking collectives  157 us (8%)
  matrix products  130 us (6%)
    slice x211, local copies, waits for them, and re-layouts, linear_scan(): return lax.associative_scan(compose, (decay, source), axis=0)  226 us
    reduce_scatter x1, waiting for transfers between devices, per_device(): lax.psum_scatter(grad_w_down, 'seq', scatter_dimension=1, tiled=True)  197 us
    reduce_scatter x1, waiting for transfers between devices, per_device(): lax.psum_scatter(grad_w_up, 'seq', scatter_dimension=0, tiled=True)  196 us
    reduce_scatter x1, waiting for transfers between devices, per_device(): lax.psum_scatter(grad_w_gate, 'seq', scatter_dimension=0, tiled=True)  196 us
    psum x1, waiting for transfers between devices, per_device(): lax.psum(jnp.dot(hidden, w_down, preferred_element_type=jnp.float32), 'mp')  159 us
    all_gather x4, blocking collectives, prefix(): pieces = jax.tree.map(lambda part: lax.all_gather(part, axis), value)  106 us
    reduce_scatter x1, waiting for transfers between devices, per_device(): lax.psum_scatter(grad_w_rgate, 'seq', scatter_dimension=0, tiled=True)  92.5 us
    reduce_scatter x1, waiting for transfers between devices, per_device(): lax.psum_scatter(grad_w_forget, 'seq', scatter_dimension=0, tiled=True)  92.3 us
  transfers between devices with their start and end apart: 12, of which 10 were waited for; matrix products, arithmetic and copies ran while one was open for 10% of the time, Pallas kernels for 0%

commit v1 on v0

v1 whole, which is shorter than its diff:
```python
import jax
import jax.numpy as jnp
from jax import lax
from jax.experimental import pallas as pl
from jax.experimental.pallas import tpu as pltpu
from jax.sharding import PartitionSpec as P

LCHUNK = 256
norm_eps = 1e-06
F32 = jnp.float32
BF16 = jnp.bfloat16

CORE_PAIRS = [(i, i ^ 1) for i in range(4)]
X_PAIRS = [(i, i ^ 2) for i in range(4)]
Y_PAIRS = [(i, i ^ 1) for i in range(8)]


def dot(left, right):
    return jnp.dot(left, right, preferred_element_type=F32)


def left_dot(left, right):
    return lax.dot_general(left, right, (((0,), (0,)), ((), ())), preferred_element_type=F32)


def right_dot(left, right):
    return lax.dot_general(left, right, (((1,), (1,)), ((), ())), preferred_element_type=F32)


def silu_slope(values):
    sig = jax.nn.sigmoid(values)
    return sig * (1.0 + values * (1.0 - sig))


def after(value, *others):
    return lax.optimization_barrier((value, *others))[0]


def round_kernel(flip_ref, first_ref, second_ref, out_ref):
    size = first_ref.shape[0]

    @pl.when(flip_ref[0] == 0)
    def _():
        out_ref[:size, :] = first_ref[...].astype(BF16)
        out_ref[size:, :] = second_ref[...].astype(BF16)

    @pl.when(flip_ref[0] != 0)
    def _():
        out_ref[:size, :] = second_ref[...].astype(BF16)
        out_ref[size:, :] = first_ref[...].astype(BF16)


def rounded(first, second, flip):
    size, width = first.shape
    block = 512
    spec = pl.BlockSpec((size, block), lambda i: (0, i))
    return pl.pallas_call(
        round_kernel,
        grid=(width // block,),
        in_specs=[pl.BlockSpec(memory_space=pltpu.SMEM), spec, spec],
        out_specs=pl.BlockSpec((2 * size, block), lambda i: (0, i)),
        out_shape=jax.ShapeDtypeStruct((2 * size, width), BF16),
        compiler_params=pltpu.CompilerParams(vmem_limit_bytes=16 * 1024 * 1024),
        cost_estimate=pl.CostEstimate(
            flops=size * width * 2, bytes_accessed=size * width * 12, transcendentals=0
        ),
        name="rounded",
    )(jnp.full((1,), flip, jnp.int32), first, second)


def scan_kernel(backward, a_ref, b_ref, x_ref, p_ref):
    rows, width = a_ref.shape
    place = lax.broadcasted_iota(jnp.int32, (8, width), 0)

    def group(start, carry_x, carry_p, with_product):
        a = a_ref[pl.ds(start, 8), :]
        b = b_ref[pl.ds(start, 8), :]
        for step in (1, 2, 4):
            shift = 8 - step if backward else step
            inside = place < 8 - step if backward else place >= step
            a_shift = jnp.where(inside, pltpu.roll(a, shift, 0), 1.0)
            b_shift = jnp.where(inside, pltpu.roll(b, shift, 0), 0.0)
            b = a * b_shift + b
            a = a * a_shift
        x = b + a * carry_x
        x_ref[pl.ds(start, 8), :] = x
        last = 0 if backward else 7
        carry_x = jnp.broadcast_to(x[last : last + 1, :], (8, width))
        if with_product:
            product = a * carry_p
            p_ref[pl.ds(start, 8), :] = product
            carry_p = jnp.broadcast_to(product[last : last + 1, :], (8, width))
        return carry_x, carry_p

    def run(first, count, with_product):
        def body(step, carry):
            place_of = count - 1 - step if backward else step
            start = pl.multiple_of(first + place_of * 8, 8)
            return group(start, *carry, with_product)

        lax.fori_loop(
            0,
            count,
            body,
            (jnp.zeros((8, width), F32), jnp.ones((8, width), F32)),
            unroll=4,
        )

    run(0, LCHUNK // 8, True)
    run(LCHUNK, (rows - LCHUNK) // 8, False)


def scan(a, b, backward):
    rows, width = a.shape
    block = 256
    spec = pl.BlockSpec((rows, block), lambda i: (0, i))
    return pl.pallas_call(
        lambda *refs: scan_kernel(backward, *refs),
        grid=(width // block,),
        in_specs=[spec, spec],
        out_specs=[spec, pl.BlockSpec((LCHUNK, block), lambda i: (0, i))],
        out_shape=[
            jax.ShapeDtypeStruct((rows, width), F32),
            jax.ShapeDtypeStruct((LCHUNK, width), F32),
        ],
        compiler_params=pltpu.CompilerParams(vmem_limit_bytes=16 * 1024 * 1024),
        cost_estimate=pl.CostEstimate(
            flops=rows * width * 12, bytes_accessed=rows * width * 14, transcendentals=0
        ),
        name="scan_back" if backward else "scan_forth",
    )(a, b)


def carry_of(decay, local, backward):
    count, mine = lax.axis_size("seq"), lax.axis_index("seq")
    ends = jnp.stack([decay, local])
    if count != 8:
        pieces = lax.all_gather(ends, "seq")
        order = jnp.arange(count)
        total = jnp.zeros_like(local)
        for step in range(count):
            i = count - 1 - step if backward else step
            use = (order[i] > mine) if backward else (order[i] < mine)
            total = jnp.where(use, pieces[i, 0] * total + pieces[i, 1], total)
        return total
    partner = lax.ppermute(ends, "seq", Y_PAIRS)
    first = (mine % 2 == 1) if backward else (mine % 2 == 0)
    early = jnp.where(first, ends, partner)
    late = jnp.where(first, partner, ends)
    pair = jnp.stack([early[0] * late[0], late[0] * early[1] + late[1]])
    total = jnp.zeros_like(local)
    got = []
    for hops in (3, 2, 1):
        if backward:
            pairs = [(i + 2 * hops, i) for i in range(8 - 2 * hops)]
        else:
            pairs = [(i, i + 2 * hops) for i in range(8 - 2 * hops)]
        got.append(lax.ppermute(pair, "seq", pairs))
    for piece in got:
        total = piece[0] * total + piece[1]
    return jnp.where(first, total, partner[0] * total + partner[1])


def small_psum(value):
    value = value + lax.ppermute(value, "mp", CORE_PAIRS)
    return value + lax.ppermute(value, "mp", X_PAIRS)


def summed_half(send, keep):
    value = keep + lax.ppermute(send, "mp", CORE_PAIRS)
    return value + lax.ppermute(value, "mp", X_PAIRS)


def butterfly(value, axis):
    count = lax.axis_size(axis)
    step = 1
    while step < count:
        value = value + lax.ppermute(value, axis, [(i, i ^ step) for i in range(count)])
        step *= 2
    return value


def chain(part):
    plane = lax.axis_index("seq") // 2
    parts = [part(jnp.bitwise_xor(slot, 3 - plane)) for slot in range(4)]

    def move(value, hops):
        pairs = [(2 * a + y, 2 * b + y) for a, b in hops for y in range(2)]
        return lax.ppermute(value, "seq", pairs)

    second = parts[1] + move(parts[0], [(0, 1), (3, 2)])
    up = move(second, [(0, 1), (1, 2)])
    down = move(second, [(3, 2), (2, 1)])
    up = jnp.where(plane == 1, parts[0], parts[2]) + up
    down = jnp.where(plane == 2, parts[0], parts[2]) + down
    up = move(up, [(0, 1), (1, 2), (2, 3)])
    down = move(down, [(3, 2), (2, 1), (1, 0)])
    return parts[3] + up + down


def per_device(
    tokens,
    attn_gain,
    w_input,
    w_forget,
    w_rgate,
    gnorm_gain,
    lower_bound,
    w_out,
    mlp_gain,
    w_gate,
    w_up,
    w_down,
    local_lengths,
    cotangent,
):
    rows, width = tokens.shape
    short_rows = rows - LCHUNK
    count, mine = lax.axis_size("seq"), lax.axis_index("seq")
    fast = count == 8
    core = lax.axis_index("mp") % 2
    side = mine % 2
    chunks = ((LCHUNK, short_rows), (0, LCHUNK))

    def half(value, own, chunk):
        first, size = chunk
        which = core if own else 1 - core
        return lax.dynamic_slice_in_dim(value, first + which * (size // 2), size // 2, 0)

    def swap_core(value):
        return lax.ppermute(value, "mp", CORE_PAIRS)

    def swap_y(value):
        return lax.ppermute(value, "seq", Y_PAIRS)

    def canonical(parts):
        out = []
        for own, other in (parts[1], parts[0]):
            out.append(jnp.where(core == 0, own, other))
            out.append(jnp.where(core == 0, other, own))
        return jnp.concatenate(out, axis=0)

    def side_columns(value, which):
        wide = value.reshape(value.shape[0], 4, 2, width // 8)
        return lax.dynamic_index_in_dim(wide, which, 2, keepdims=False).reshape(
            value.shape[0], width // 2
        )

    lengths_row = local_lengths[0]
    offsets = jnp.cumsum(lengths_row) - lengths_row
    starts = jnp.any(
        jnp.arange(short_rows, dtype=jnp.int32)[:, None] == offsets[None, :], axis=1
    )[:, None]

    cot_own = [(half(cotangent, True, c), half(cotangent, False, c)) for c in chunks]
    cot_rows = jnp.concatenate([part for pair in cot_own for part in pair], axis=0)
    d_hidden = right_dot(cot_rows, w_down)

    stream = tokens.astype(F32)
    first_gain = attn_gain.astype(F32)
    first_scale = lax.rsqrt(jnp.mean(stream * stream, axis=1, keepdims=True) + norm_eps)
    normed_one_wide = stream * first_scale * first_gain
    normed_one = normed_one_wide.astype(BF16)
    pre_forget = dot(normed_one, w_forget)
    pre_input = dot(normed_one, w_input)
    pre_rgate = dot(normed_one, w_rgate)
    forget_sig = jax.nn.sigmoid(pre_forget)
    forget = lower_bound + (1.0 - lower_bound) * forget_sig
    input_act = jax.nn.silu(pre_input)
    drive = input_act * (1.0 - forget)
    is_start = jnp.concatenate([jnp.zeros((LCHUNK, 1), bool), starts], axis=0)
    states_local, long_decay = scan(jnp.where(is_start, 0.0, forget), drive, False)
    carry_in = carry_of(long_decay[-1], states_local[LCHUNK - 1], False)

    state_gain = gnorm_gain.astype(F32)
    rgate_act = jax.nn.silu(pre_rgate)
    second_gain = mlp_gain.astype(F32)

    def row_scale(values):
        return lax.rsqrt(jnp.mean(values * values, axis=1, keepdims=True) + norm_eps)

    def glu(middle, d_hid):
        scale = row_scale(middle)
        hat = middle * scale
        normed = (hat * second_gain).astype(BF16)
        gate = dot(normed, w_gate)
        up = dot(normed, w_up)
        act = jax.nn.silu(gate)
        hidden = (act * up).astype(BF16)
        d_gate = (d_hid * up * silu_slope(gate)).astype(BF16)
        d_up = (d_hid * act).astype(BF16)
        return scale, hat, normed, hidden, d_gate, d_up

    states_of, scale_of, gated_of, middle_own, middle_other = [], [], [], [], []
    for index, (first, size) in enumerate(chunks):
        local = states_local[first : first + size]
        if index == 1:
            local = local + long_decay * carry_in[None, :]
        squares = small_psum(jnp.sum(local * local, axis=1))
        scale = lax.rsqrt(squares / width + norm_eps)[:, None]
        gated = local * scale * state_gain * rgate_act[first : first + size]
        gated16 = gated.astype(BF16)
        states_of.append(local)
        scale_of.append(scale)
        gated_of.append(gated)
        h = size // 2
        send = dot(lax.dynamic_slice_in_dim(gated16, (1 - core) * h, h, 0), w_out)
        keep = dot(lax.dynamic_slice_in_dim(gated16, core * h, h, 0), w_out)
        own = half(tokens, True, (first, size)).astype(F32) + summed_half(send, keep)
        middle_own.append(own)
        middle_other.append(swap_core(own))

    states = jnp.concatenate([states_of[1], states_of[0]], axis=0)
    state_scale = jnp.concatenate([scale_of[1], scale_of[0]], axis=0)
    gated_wide = jnp.concatenate([gated_of[1], gated_of[0]], axis=0)
    gated = gated_wide.astype(BF16)
    normed_state = states * state_scale

    offset = 0
    main, d_mid_own, d_mid_other, hat_grad, feeds = [], [], [], [], []
    for index, (first, size) in enumerate(chunks):
        h = size // 2
        middle = jnp.concatenate([middle_own[index], middle_other[index]], axis=0)
        scale, hat, normed, hidden, d_gate, d_up = glu(middle, d_hidden[offset : offset + size])
        offset += size
        main.append((normed, hidden, d_gate, d_up))
        send = right_dot(d_gate[h:], w_gate) + right_dot(d_up[h:], w_up)
        keep = right_dot(d_gate[:h], w_gate) + right_dot(d_up[:h], w_up)
        d_normed = summed_half(send, keep)
        hat, scale = hat[:h], scale[:h]
        hat_grad.append(jnp.sum(d_normed * hat, axis=0))
        e = d_normed * second_gain
        turn = scale * (e - hat * jnp.mean(e * hat, axis=1, keepdims=True))
        d_mid_own.append(cot_own[index][0].astype(F32) + turn)
        d_mid_other.append(cot_own[index][1].astype(F32) + swap_core(turn))
        hid = after(hidden, d_normed)
        feeds.append((dot(hid[h:], w_down), dot(hid[:h], w_down)))

    d_branch_wide = canonical(list(zip(d_mid_own, d_mid_other)))
    d_branch = d_branch_wide.astype(BF16)
    d_gated = right_dot(d_branch, w_out)
    grad_gnorm = jnp.sum(d_gated * normed_state * rgate_act, axis=0)
    d_rgate_wide = d_gated * normed_state * state_gain * silu_slope(pre_rgate)
    d_normed = d_gated * state_gain * rgate_act
    inner = small_psum(jnp.sum(d_normed * normed_state, axis=1))
    d_states = state_scale * (d_normed - normed_state * (inner / width)[:, None])
    shifted = jnp.concatenate([forget[1:], jnp.zeros_like(forget[:1])], axis=0)
    next_start = jnp.concatenate([is_start[1:], jnp.ones((1, 1), bool)], axis=0)
    links = jnp.where(next_start, 0.0, shifted)
    row = lax.broadcasted_iota(jnp.int32, (rows, 1), 0)
    links = jnp.where(row == LCHUNK - 1, 1.0, links)
    back_local, back_decay = scan(links, d_states, True)
    carried_in = carry_of(forget[0] * back_decay[0], forget[0] * back_local[0], True)
    carried = jnp.concatenate(
        [back_local[:LCHUNK] + back_decay * carried_in[None, :], back_local[LCHUNK:]], axis=0
    )
    states_prev = jnp.concatenate([carry_in[None, :], states[:-1]], axis=0)
    states_prev = jnp.where(is_start, 0.0, states_prev)
    d_forget = carried * (states_prev - input_act)
    d_input_wide = carried * (1.0 - forget) * silu_slope(pre_input)
    d_pforget_wide = d_forget * (1.0 - lower_bound) * forget_sig * (1.0 - forget_sig)
    grad_bound = jnp.sum(d_forget * (1.0 - forget_sig), axis=0)
    d_input = d_input_wide.astype(BF16)
    d_pforget = d_pforget_wide.astype(BF16)
    d_rgate = d_rgate_wide.astype(BF16)

    d_stream, first_grad = [], []
    for index, chunk in enumerate(chunks):
        both = []
        for own in (False, True):
            both.append(
                right_dot(half(d_input, own, chunk), w_input)
                + right_dot(half(d_pforget, own, chunk), w_forget)
                + right_dot(half(d_rgate, own, chunk), w_rgate)
            )
        d_normed_one = summed_half(*both)
        part = half(tokens, True, chunk).astype(F32)
        scale = row_scale(part)
        hat = part * scale
        first_grad.append(jnp.sum(d_normed_one * hat, axis=0))
        e = d_normed_one * first_gain
        turn = scale * (e - hat * jnp.mean(e * hat, axis=1, keepdims=True))
        d_stream.append((d_mid_own[index] + turn, d_mid_other[index] + swap_core(turn)))
    grad_tokens = canonical(d_stream).astype(BF16)

    mixed = []
    for own, other, feed in zip(middle_own, middle_other, feeds):
        value = summed_half(*feed)
        mixed.append((own + value, other + swap_core(value)))
    mixed_out = canonical(mixed).astype(BF16)

    pieces = jnp.concatenate([sum(first_grad), sum(hat_grad)])
    pieces = pieces + swap_core(pieces)
    vectors = butterfly(jnp.concatenate([pieces, grad_gnorm, grad_bound]), "seq")
    part = width // count
    grad_attn = lax.dynamic_slice_in_dim(vectors[:width], mine * part, part)
    grad_mlp = lax.dynamic_slice_in_dim(vectors[width : 2 * width], mine * part, part)
    channels = grad_gnorm.shape[0]
    small = channels // count
    grad_gnorm = lax.dynamic_slice_in_dim(
        vectors[2 * width : 2 * width + channels], mine * small, small
    )[None, :]
    grad_bound = lax.dynamic_slice_in_dim(vectors[2 * width + channels :], mine * small, small)[
        None, :
    ]

    normed_two, hidden, d_gate, d_up = (
        jnp.concatenate([main[0][i], main[1][i]], axis=0) for i in range(4)
    )

    if not fast:

        def scattered(value, dim):
            return lax.psum_scatter(value, "seq", scatter_dimension=dim, tiled=True)

        grads = (
            scattered(left_dot(normed_one, d_input), 0),
            scattered(left_dot(normed_one, d_pforget), 0),
            scattered(left_dot(normed_one, d_rgate), 0),
            scattered(left_dot(gated, d_branch), 1),
            scattered(left_dot(normed_two, d_gate), 0),
            scattered(left_dot(normed_two, d_up), 0),
            scattered(left_dot(hidden, cot_rows), 1),
        )
    else:
        cot_mine = jnp.concatenate([pair[0] for pair in cot_own], axis=0).astype(F32)
        cot_near = swap_y(cot_mine)
        cot_near = rounded(cot_near, swap_core(cot_near), 0)
        got = [swap_y(own) for own in middle_own]
        got_other = [swap_core(value) for value in got]
        middle_near = jnp.concatenate(got + got_other, axis=0)
        _, _, normed_near, hidden_near, d_gate_near, d_up_near = glu(
            middle_near, right_dot(cot_near, w_down)
        )
        both_cot = jnp.concatenate([cot_rows, cot_near], axis=0)
        both_normed = jnp.concatenate([normed_two, normed_near], axis=0)
        both_hidden = jnp.concatenate([hidden, hidden_near], axis=0)
        both_gate = jnp.concatenate([d_gate, d_gate_near], axis=0)
        both_up = jnp.concatenate([d_up, d_up_near], axis=0)
        block = width // 8

        def features(value, q):
            return lax.dynamic_slice_in_dim(value, q * 2 * block + side * block, block, 1)

        grad_w_down = chain(lambda q: left_dot(both_hidden, features(both_cot, q)))
        grad_w_gate = chain(lambda q: left_dot(features(both_normed, q), both_gate))
        grad_w_up = chain(lambda q: left_dot(features(both_normed, q), both_up))

        def near_half(value, order):
            value, _ = lax.optimization_barrier((value, order))
            columns = side_columns(value, 1 - side)
            h = rows // 2
            own = lax.dynamic_slice_in_dim(columns, core * h, h, 0)
            own = swap_y(own)
            return rounded(own, swap_core(own), core)

        one_near = near_half(normed_one_wide, middle_near)
        branch_near = near_half(d_branch_wide, middle_near)

        def near(value):
            value = swap_y(value)
            return rounded(value[: rows // 2], value[rows // 2 :], 0)

        gated_near = near(after(gated_wide, middle_near))
        joined = jnp.concatenate([d_input_wide, d_pforget_wide, d_rgate_wide], axis=1)
        joined_near = near(joined)
        both_joined = jnp.concatenate([joined.astype(BF16), joined_near], axis=0)
        both_one = jnp.concatenate([side_columns(normed_one, side), one_near], axis=0)
        both_branch = jnp.concatenate([side_columns(d_branch, side), branch_near], axis=0)
        both_gated = jnp.concatenate([gated, gated_near], axis=0)

        def own_features(value, q):
            return lax.dynamic_slice_in_dim(value, q * block, block, 1)

        grad_w_out = chain(lambda q: left_dot(both_gated, own_features(both_branch, q)))
        grad_joined = chain(lambda q: left_dot(own_features(both_one, q), both_joined))
        grads = (
            grad_joined[:, :channels],
            grad_joined[:, channels : 2 * channels],
            grad_joined[:, 2 * channels :],
            grad_w_out,
            grad_w_gate,
            grad_w_up,
            grad_w_down,
        )

    return (
        mixed_out,
        grad_tokens,
        grad_attn,
        grads[0],
        grads[1],
        grads[2],
        grad_gnorm,
        grad_bound,
        grads[3],
        grad_mlp,
        grads[4],
        grads[5],
        grads[6],
    )


def solution(mesh):
    in_specs = (
        P("seq", None),
        P(),
        P(None, "mp"),
        P(None, "mp"),
        P(None, "mp"),
        P("mp"),
        P("mp"),
        P("mp", None),
        P(),
        P(None, "mp"),
        P(None, "mp"),
        P("mp", None),
        P("seq", None),
        P("seq", None),
    )
    out_specs = (
        P("seq", None),
        P("seq", None),
        P("seq"),
        P("seq", "mp"),
        P("seq", "mp"),
        P("seq", "mp"),
        P("mp", "seq"),
        P("mp", "seq"),
        P("mp", "seq"),
        P("seq"),
        P("seq", "mp"),
        P("seq", "mp"),
        P("mp", "seq"),
    )
    return jax.shard_map(
        per_device, mesh=mesh, in_specs=in_specs, out_specs=out_specs, check_vma=False
    )
```

time: 2060 us -> 792 us (0.38)
  waiting for transfers between devices: 1200 us -> 321 us
  local copies, waits for them, and re-layouts: 357 us -> 110 us
  blocking collectives: 157 us -> 0 us
  starting transfers between devices: 1.37 us -> 123 us
  other arithmetic: 180 us -> 60.6 us
  matrix products: 130 us -> 159 us
    reduce_scatter x7 -> x0, waiting for transfers between devices: 903 us -> none  [the longest x1 197 us: per_device(): lax.psum_scatter(grad_w_down, 'seq', scatter_dimension=1, tiled=True)]
    ppermute x0 -> x79, waiting for transfers between devices: none -> 321 us  [the longest x25 178 us: move(): return lax.ppermute(value, 'seq', pairs)]
    psum x3 -> x0, waiting for transfers between devices: 295 us -> none  [the longest x1 159 us: per_device(): lax.psum(jnp.dot(hidden, w_down, preferred_element_type=jnp.float32), 'mp')]
    slice x218 -> x14, local copies, waits for them, and re-layouts: 231 us -> 4.03 us  [the longest x2 1.56 us: near(): return rounded(value[:rows // 2], value[rows // 2:], 0)]
    ppermute x0 -> x79, starting transfers between devices: none -> 123 us  [the longest x25 78.2 us: move(): return lax.ppermute(value, 'seq', pairs)]
    all_gather x4 -> x0, blocking collectives: 106 us -> none  [prefix(): pieces = jax.tree.map(lambda part: lax.all_gather(part, axis), value)]
    pad x84 -> x0, local copies, waits for them, and re-layouts: 77.5 us -> none  [linear_scan(): return lax.associative_scan(compose, (decay, source), axis=0)]
    add x76 -> x12, other arithmetic: 70.2 us -> 1.36 us  [the longest x2 1.22 us: summed_half(): return value + lax.ppermute(value, 'mp', X_PAIRS)]
  transfers between devices with their start and end apart: 12 -> 79, of which waited for: 10 -> 26; matrix products, arithmetic and copies ran while one was open for 10% -> 38% of each run, Pallas kernels for 0% -> 1%
where the time goes in v1:
time: 792 us; the launch traced here: 784 us
  waiting for transfers between devices  321 us (41%)
  matrix products  159 us (20%)
  starting transfers between devices  123 us (16%)
  local copies, waits for them, and re-layouts  110 us (14%)
  other arithmetic  60.6 us (8%)
    ppermute x25, waiting for transfers between devices, move(): return lax.ppermute(value, 'seq', pairs)  178 us
    ppermute x25, starting transfers between devices, move(): return lax.ppermute(value, 'seq', pairs)  78.2 us
    ppermute x7, waiting for transfers between devices, swap_y(): return lax.ppermute(value, 'seq', Y_PAIRS)  60.9 us
    dot_general x20, matrix products, left_dot(): lax.dot_general(left, right, (((0,), (0,)), ((), ())), preferred_element_...  55.7 us
    dot_general x17, matrix products, dot(): return jnp.dot(left, right, preferred_element_type=F32)  52.4 us
    dot_general x23, matrix products, right_dot(): lax.dot_general(left, right, (((1,), (1,)), ((), ())), preferred_element_...  50.8 us
    ppermute x8, waiting for transfers between devices, summed_half(): return value + lax.ppermute(value, 'mp', X_PAIRS)  45.4 us
    unnamed x307, local copies, waits for them, and re-layouts  32.3 us
  transfers between devices with their start and end apart: 79, of which 26 were waited for; matrix products, arithmetic and copies ran while one was open for 38% of the time, Pallas kernels for 1%

profile of v1, /device:TPU:0, one launch (start us, length us, event | category | flops | bytes accessed | tf_op | source)
XLA Modules:
  0.0 784.0 jit_solution(16403461707431614968)
XLA Ops:
  4.1 4.6 fusion.1
  35.4 4.5 collective-permute-start.2
  55.7 8.2 %fusion.9 = f32[576,1408]{1,0:T(8,128)} fusion(bf16[1408,2048]{1,0:T(8,128)(2,1)} %param.25, bf16[128,2048]{1,0:T(8,128)(2,1)S(1)} %copy-done.56, bf16[128,2048]{1,0:T(8,128)(2,1)S(1)} %copy-done.38, bf16[160,2048]{1,0:T(8,128)(2,1)S(1)} %copy-done.49, bf16[160,2048]{1,0:T(8,128)(2,1)S(1)} %copy-done.27), kind=kOutput, calls=%fused_computation.65 | convolution fusion | flops 3331325952 | bytes 11370496 | tf_op jit(solution)/shard_map/dot_general | solution.py:27
  63.9 7.0 reshape.173
  73.6 8.5 %dynamic-slice_reduce_fusion.2 = bf16[576,4,256]{2,1,0:T(4,128)(2,1)} fusion(bf16[576,4,2,256]{3,2,1,0:T(2,128)(2,1)S(1)} %copy-done.32, s32[]{:T(128)S(6)} %select_n.331), kind=kLoop, calls=%fused_computation.81 | loop fusion | bytes 2359300 | tf_op jit(solution)/shard_map/jit(dynamic_index_in_dim)/dynamic_slice | solution.py:245
  91.5 7.1 collective-permute-done.7
  106.1 20.0 %collective-permute-done.17 = f32[160,2048]{1,0:T(8,128)} collective-permute-done((f32[160,2048]{1,0:T(8,128)}, f32[160,2048]{1,0:T(8,128)}, u32[]{:S(2)}, u32[]{:S(2)}) %collective-permute-start.17) | collective-permute-done | bytes 1310752 | tf_op jit(solution)/shard_map/ppermute | solution.py:171
  149.5 3.8 multiply_convert_fusion.6
  174.0 5.5 fusion.212
  184.7 5.5 fusion.213
  190.3 4.5 fusion.7
  196.6 7.1 multiply_convert_fusion.1
  219.2 7.4 reshape.175
  231.4 3.8 fusion.195
  245.1 4.2 convolution_add_fusion.15
  260.2 3.9 convolution_add_fusion.3
  264.0 27.0 %collective-permute-done.69 = f32[256,1408]{1,0:T(8,128)} collective-permute-done((f32[256,1408]{1,0:T(8,128)}, f32[256,1408]{1,0:T(8,128)}, u32[]{:S(2)}, u32[]{:S(2)}) %collective-permute-start.69) | collective-permute-done | bytes 1441824 | tf_op jit(solution)/shard_map/ppermute | solution.py:189
  291.0 5.5 collective-permute-start.65
  296.5 3.8 convolution_add_fusion.2
  300.4 21.5 %collective-permute-done.74 = f32[1408,256]{1,0:T(8,128)S(1)} collective-permute-done((f32[1408,256]{1,0:T(8,128)}, f32[1408,256]{1,0:T(8,128)S(1)}, u32[]{:S(2)}, u32[]{:S(2)}) %collective-permute-start.74) | collective-permute-done | bytes 1441824 | tf_op jit(solution)/shard_map/ppermute | solution.py:189
  331.4 3.6 fusion.197
  337.8 7.6 reshape.178
  345.3 5.6 convolution_add_fusion.19
  350.9 19.4 %dynamic-slice_reduce_fusion = (f32[576,4,256]{2,1,0:T(4,128)}, f32[576,4,256]{2,1,0:T(4,128)}) fusion(f32[576,4,2,256]{3,2,1,0:T(2,128)S(1)} %copy-done.23, s32[]{:T(128)S(6)} %select_n.332, f32[576,4,2,256]{3,2,1,0:T(2,128)} %reshape.175), kind=kLoop, calls=%fused_computation.79 | loop fusion | bytes 9437188 | tf_op jit(solution)/shard_map/jit(dynamic_index_in_dim)/dynamic_slice | solution.py:245
  396.9 5.6 collective-permute-start.70
  404.2 3.6 collective-permute-start.75
  423.6 9.8 %collective-permute-done.70 = f32[256,1408]{1,0:T(8,128)} collective-permute-done((f32[256,1408]{1,0:T(8,128)S(1)}, f32[256,1408]{1,0:T(8,128)}, u32[]{:S(2)}, u32[]{:S(2)}) %collective-permute-start.70) | collective-permute-done | bytes 1441824 | tf_op jit(solution)/shard_map/ppermute | solution.py:189
  435.1 26.7 %collective-permute-done.75 = f32[1408,256]{1,0:T(8,128)} collective-permute-done((f32[1408,256]{1,0:T(8,128)}, f32[1408,256]{1,0:T(8,128)}, u32[]{:S(2)}, u32[]{:S(2)}) %collective-permute-start.75) | collective-permute-done | bytes 1441824 | tf_op jit(solution)/shard_map/ppermute | solution.py:189
  463.0 5.7 select_add_fusion.7
  470.3 6.5 collective-permute-start.66
  476.8 5.2 select_add_fusion.3
  482.0 5.1 collective-permute-done.46.first_ref
  488.5 7.0 collective-permute-start.76
  495.5 5.2 select_add_fusion.5
  507.9 5.7 collective-permute-start.71
  515.9 21.2 %collective-permute-done.78 = f32[1408,256]{1,0:T(8,128)} collective-permute-done((f32[1408,256]{1,0:T(8,128)}, f32[1408,256]{1,0:T(8,128)}, u32[]{:S(2)}, u32[]{:S(2)}) %collective-permute-start.78) | collective-permute-done | bytes 1441824 | tf_op jit(solution)/shard_map/ppermute | solution.py:189
  540.0 4.1 add_add_fusion.1
  544.1 4.4 fusion.3
  548.6 54.7 %collective-permute-done.55.first_ref = f32[288,1024]{1,0:T(8,128)S(1)} collective-permute-done((f32[288,1024]{1,0:T(8,128)S(1)}, f32[288,1024]{1,0:T(8,128)S(1)}, u32[]{:S(2)}, u32[]{:S(2)}) %collective-permute-start.55) | collective-permute-done | bytes 1179680 | tf_op jit(solution)/shard_map/ppermute | solution.py:234
  604.9 4.1 add_add_fusion
  612.3 3.5 collective-permute-start.57
  616.3 18.2 %collective-permute-done.36 = f32[160,2048]{1,0:T(8,128)S(1)} collective-permute-done((f32[160,2048]{1,0:T(8,128)S(1)}, f32[160,2048]{1,0:T(8,128)S(1)}, u32[]{:S(2)}, u32[]{:S(2)}) %collective-permute-start.36) | collective-permute-done | bytes 1310752 | tf_op jit(solution)/shard_map/ppermute | solution.py:171
  645.8 30.2 %collective-permute-done.40 = f32[5120]{0:T(1024)S(1)} collective-permute-done((f32[5120]{0:T(1024)S(1)}, f32[5120]{0:T(1024)S(1)}, u32[]{:S(2)}, u32[]{:S(2)}) %collective-permute-start.40) | collective-permute-done | bytes 20512 | tf_op jit(solution)/shard_map/ppermute | solution.py:178
  676.0 4.8 collective-permute-start.41
  691.2 36.7 %collective-permute-done.58 = f32[512,256]{1,0:T(8,128)S(1)} collective-permute-done((f32[512,256]{1,0:T(8,128)S(1)}, f32[512,256]{1,0:T(8,128)S(1)}, u32[]{:S(2)}, u32[]{:S(2)}) %collective-permute-start.58) | collective-permute-done | bytes 524320 | tf_op jit(solution)/shard_map/ppermute | solution.py:189
  729.9 8.0 %collective-permute-start.59 = (f32[512,256]{1,0:T(8,128)S(1)}, f32[512,256]{1,0:T(8,128)S(1)}, u32[]{:S(2)}, u32[]{:S(2)}) collective-permute-start(f32[512,256]{1,0:T(8,128)S(1)} %get-tuple-element.129), channel_id=1, source_target_pairs={{0,8},{4,12},{8,16},{12,20},{16,24},{20,28},{1,9},{5,13},{9,17},{1... | collective-permute-start | bytes 1572872 | tf_op jit(solution)/shard_map/ppermute | solution.py:189
  740.5 4.6 collective-permute-start.51
  754.0 26.0 %collective-permute-done.53 = f32[256,1536]{1,0:T(8,128)S(1)} collective-permute-done((f32[256,1536]{1,0:T(8,128)S(1)}, f32[256,1536]{1,0:T(8,128)S(1)}, u32[]{:S(2)}, u32[]{:S(2)}) %collective-permute-start.53) | collective-permute-done | bytes 1572896 | tf_op jit(solution)/shard_map/ppermute | solution.py:189
  (618 shorter events, 274.2 us)
Async XLA Ops:
  28.0 78.2 %collective-permute-start.62 = (f32[288,2048]{1,0:T(8,128)}, f32[288,2048]{1,0:T(8,128)}, u32[]{:S(2)}, u32[]{:S(2)}) collective-permute-start(f32[288,2048]{1,0:T(8,128)} %maximum_convert_fusion), channel_id=1, source_target_pairs={{0,4},{4,0},{8,12},{12,8},{16,20},{20,16},{24,28},{28,24},{1,5},{5... | collective-permute-start | bytes 7077896 | tf_op jit(solution)/shard_map/ppermute | solution.py:234
  85.1 41.1 %collective-permute-start.17 = (f32[160,2048]{1,0:T(8,128)}, f32[160,2048]{1,0:T(8,128)}, u32[]{:S(2)}, u32[]{:S(2)}) collective-permute-start(f32[160,2048]{1,0:T(8,128)} %convolution_add_fusion.10), channel_id=1, source_target_pairs={{0,2},{1,3},{2,0},{3,1},{4,6},{5,7},{6,4},{7,5},{8,10},{9,11},{10,... | collective-permute-start | bytes 3932168 | tf_op jit(solution)/shard_map/ppermute | solution.py:171
  104.5 38.1 %collective-permute-start.43 = (f32[128,2048]{1,0:T(8,128)S(1)}, f32[128,2048]{1,0:T(8,128)}, u32[]{:S(2)}, u32[]{:S(2)}) collective-permute-start(f32[128,2048]{1,0:T(8,128)S(1)} %get-tuple-element.115), channel_id=1, source_target_pairs={{0,4},{4,0},{8,12},{12,8},{16,20},{20,16},{24,28},{28,24},{1,5},{5... | collective-permute-start | bytes 3145736 | tf_op jit(solution)/shard_map/ppermute | solution.py:234
  106.1 63.6 %collective-permute-start.63 = (f32[288,2048]{1,0:T(8,128)}, f32[288,2048]{1,0:T(8,128)S(1)}, u32[]{:S(2)}, u32[]{:S(2)}) collective-permute-start(f32[288,2048]{1,0:T(8,128)} %collective-permute-done.62.first_ref), channel_id=1, source_target_pairs={{0,1},{1,0},{2,3},{3,2},{4,5},{5,4},{6,7},{7,6},{8,9},{9,8},{10,11... | collective-permute-start | bytes 7077896 | tf_op jit(solution)/shard_map/ppermute | solution.py:231
  128.3 31.3 %collective-permute-start.42 = (f32[160,2048]{1,0:T(8,128)S(1)}, f32[160,2048]{1,0:T(8,128)}, u32[]{:S(2)}, u32[]{:S(2)}) collective-permute-start(f32[160,2048]{1,0:T(8,128)S(1)} %get-tuple-element.119), channel_id=1, source_target_pairs={{0,4},{4,0},{8,12},{12,8},{16,20},{20,16},{24,28},{28,24},{1,5},{5... | collective-permute-start | bytes 3932168 | tf_op jit(solution)/shard_map/ppermute | solution.py:234
  142.7 38.2 %collective-permute-start.45 = (f32[128,2048]{1,0:T(8,128)}, f32[128,2048]{1,0:T(8,128)}, u32[]{:S(2)}, u32[]{:S(2)}) collective-permute-start(f32[128,2048]{1,0:T(8,128)} %collective-permute-done.43), channel_id=1, source_target_pairs={{0,1},{1,0},{2,3},{3,2},{4,5},{5,4},{6,7},{7,6},{8,9},{9,8},{10,11... | collective-permute-start | bytes 3145736 | tf_op jit(solution)/shard_map/ppermute | solution.py:231
  158.4 31.9 %collective-permute-start.19 = (f32[160,2048]{1,0:T(8,128)}, f32[160,2048]{1,0:T(8,128)}, u32[]{:S(2)}, u32[]{:S(2)}) collective-permute-start(f32[160,2048]{1,0:T(8,128)} %convolution_add_fusion.20), channel_id=1, source_target_pairs={{0,1},{1,0},{2,3},{3,2},{4,5},{5,4},{6,7},{7,6},{8,9},{9,8},{10,11... | collective-permute-start | bytes 3932168 | tf_op jit(solution)/shard_map/ppermute | solution.py:170
  168.5 35.3 %collective-permute-start.10 = (f32[128,2048]{1,0:T(8,128)}, f32[128,2048]{1,0:T(8,128)}, u32[]{:S(2)}, u32[]{:S(2)}) collective-permute-start(f32[128,2048]{1,0:T(8,128)} %fusion.8), channel_id=1, source_target_pairs={{0,2},{1,3},{2,0},{3,1},{4,6},{5,7},{6,4},{7,5},{8,10},{9,11},{10,... | collective-permute-start | bytes 3145736 | tf_op jit(solution)/shard_map/ppermute | solution.py:171
  194.7 58.2 %collective-permute-start.20 = (f32[160,2048]{1,0:T(8,128)}, f32[160,2048]{1,0:T(8,128)}, u32[]{:S(2)}, u32[]{:S(2)}) collective-permute-start(f32[160,2048]{1,0:T(8,128)} %fusion.7), channel_id=1, source_target_pairs={{0,2},{1,3},{2,0},{3,1},{4,6},{5,7},{6,4},{7,5},{8,10},{9,11},{10,... | collective-permute-start | bytes 3932168 | tf_op jit(solution)/shard_map/ppermute | solution.py:171
  195.6 53.7 %collective-permute-start.54 = (f32[576,512]{1,0:T(8,128)}, f32[576,512]{1,0:T(8,128)}, u32[]{:S(2)}, u32[]{:S(2)}) collective-permute-start(f32[576,512]{1,0:T(8,128)} %pad_maximum_fusion.13), channel_id=1, source_target_pairs={{0,4},{4,0},{8,12},{12,8},{16,20},{20,16},{24,28},{28,24},{1,5},{5... | collective-permute-start | bytes 3538952 | tf_op jit(solution)/shard_map/ppermute | solution.py:234
  226.6 33.6 %collective-permute-start.64 = (f32[256,1408]{1,0:T(8,128)}, f32[256,1408]{1,0:T(8,128)}, u32[]{:S(2)}, u32[]{:S(2)}) collective-permute-start(f32[256,1408]{1,0:T(8,128)} %fusion.87), channel_id=1, source_target_pairs={{0,8},{4,12},{24,16},{28,20},{1,9},{5,13},{25,17},{29,21},{2,10},{... | collective-permute-start | bytes 4325384 | tf_op jit(solution)/shard_map/ppermute | solution.py:189
  229.0 62.1 %collective-permute-start.69 = (f32[256,1408]{1,0:T(8,128)}, f32[256,1408]{1,0:T(8,128)}, u32[]{:S(2)}, u32[]{:S(2)}) collective-permute-start(f32[256,1408]{1,0:T(8,128)} %fusion.85), channel_id=1, source_target_pairs={{0,8},{4,12},{24,16},{28,20},{1,9},{5,13},{25,17},{29,21},{2,10},{... | collective-permute-start | bytes 4325384 | tf_op jit(solution)/shard_map/ppermute | solution.py:189
  243.7 78.2 %collective-permute-start.74 = (f32[1408,256]{1,0:T(8,128)}, f32[1408,256]{1,0:T(8,128)S(1)}, u32[]{:S(2)}, u32[]{:S(2)}) collective-permute-start(f32[1408,256]{1,0:T(8,128)} %fusion.76), channel_id=1, source_target_pairs={{0,8},{4,12},{24,16},{28,20},{1,9},{5,13},{25,17},{29,21},{2,10},{... | collective-permute-start | bytes 4325384 | tf_op jit(solution)/shard_map/ppermute | solution.py:189
  249.3 77.7 %collective-permute-start.12 = (f32[128,2048]{1,0:T(8,128)S(1)}, f32[128,2048]{1,0:T(8,128)S(1)}, u32[]{:S(2)}, u32[]{:S(2)}) collective-permute-start(f32[128,2048]{1,0:T(8,128)S(1)} %convolution_add_fusion.15), channel_id=1, source_target_pairs={{0,2},{1,3},{2,0},{3,1},{4,6},{5,7},{6,4},{7,5},{8,10},{9,11},{10,... | collective-permute-start | bytes 3145736 | tf_op jit(solution)/shard_map/ppermute | solution.py:171
  257.6 87.7 %collective-permute-start.21 = (f32[160,2048]{1,0:T(8,128)}, f32[160,2048]{1,0:T(8,128)}, u32[]{:S(2)}, u32[]{:S(2)}) collective-permute-start(f32[160,2048]{1,0:T(8,128)} %fusion.103), channel_id=1, source_target_pairs={{0,1},{1,0},{2,3},{3,2},{4,5},{5,4},{6,7},{7,6},{8,9},{9,8},{10,11... | collective-permute-start | bytes 3932168 | tf_op jit(solution)/shard_map/ppermute | solution.py:170
  260.1 68.0 %collective-permute-start.25 = (f32[160,2048]{1,0:T(8,128)S(1)}, f32[160,2048]{1,0:T(8,128)S(1)}, u32[]{:S(2)}, u32[]{:S(2)}) collective-permute-start(f32[160,2048]{1,0:T(8,128)S(1)} %subtract_multiply_fusion), channel_id=1, source_target_pairs={{0,1},{1,0},{2,3},{3,2},{4,5},{5,4},{6,7},{7,6},{8,9},{9,8},{10,11... | collective-permute-start | bytes 3932168 | tf_op jit(solution)/shard_map/ppermute | solution.py:231
  291.0 129.7 %collective-permute-start.65 = (f32[256,1408]{1,0:T(8,128)}, f32[256,1408]{1,0:T(8,128)}, u32[]{:S(2)}, u32[]{:S(2)}) collective-permute-start(f32[256,1408]{1,0:T(8,128)} %convolution_add_fusion.3), channel_id=1, source_target_pairs={{0,8},{4,12},{8,16},{12,20},{1,9},{5,13},{9,17},{13,21},{2,10},{6,... | collective-permute-start | bytes 4325384 | tf_op jit(solution)/shard_map/ppermute | solution.py:189
  321.9 101.5 %collective-permute-start.67 = (f32[256,1408]{1,0:T(8,128)}, f32[256,1408]{1,0:T(8,128)}, u32[]{:S(2)}, u32[]{:S(2)}) collective-permute-start(f32[256,1408]{1,0:T(8,128)} %convolution_add_fusion.3), channel_id=1, source_target_pairs={{24,16},{28,20},{16,8},{20,12},{25,17},{29,21},{17,9},{21,13},{26,... | collective-permute-start | bytes 4325384 | tf_op jit(solution)/shard_map/ppermute | solution.py:189
  335.0 45.3 %collective-permute-start.26 = (f32[576]{0:T(1024)S(1)}, f32[576]{0:T(1024)S(1)}, u32[]{:S(2)}, u32[]{:S(2)}) collective-permute-start(f32[576]{0:T(1024)S(1)} %get-tuple-element.97), channel_id=1, source_target_pairs={{0,1},{1,0},{2,3},{3,2},{4,5},{5,4},{6,7},{7,6},{8,9},{9,8},{10,11... | collective-permute-start | bytes 6920 | tf_op jit(solution)/shard_map/ppermute | solution.py:165
  396.9 36.5 %collective-permute-start.70 = (f32[256,1408]{1,0:T(8,128)S(1)}, f32[256,1408]{1,0:T(8,128)}, u32[]{:S(2)}, u32[]{:S(2)}) collective-permute-start(f32[256,1408]{1,0:T(8,128)S(1)} %copy-done.126), channel_id=1, source_target_pairs={{0,8},{4,12},{8,16},{12,20},{1,9},{5,13},{9,17},{13,21},{2,10},{6,... | collective-permute-start | bytes 4325384 | tf_op jit(solution)/shard_map/ppermute | solution.py:189
  402.5 31.7 %collective-permute-start.72 = (f32[256,1408]{1,0:T(8,128)S(1)}, f32[256,1408]{1,0:T(8,128)}, u32[]{:S(2)}, u32[]{:S(2)}) collective-permute-start(f32[256,1408]{1,0:T(8,128)S(1)} %copy-done.126), channel_id=1, source_target_pairs={{24,16},{28,20},{16,8},{20,12},{25,17},{29,21},{17,9},{21,13},{26,... | collective-permute-start | bytes 4325384 | tf_op jit(solution)/shard_map/ppermute | solution.py:189
  404.2 57.5 %collective-permute-start.75 = (f32[1408,256]{1,0:T(8,128)}, f32[1408,256]{1,0:T(8,128)}, u32[]{:S(2)}, u32[]{:S(2)}) collective-permute-start(f32[1408,256]{1,0:T(8,128)} %convolution_add_fusion), channel_id=1, source_target_pairs={{0,8},{4,12},{8,16},{12,20},{1,9},{5,13},{9,17},{13,21},{2,10},{6,... | collective-permute-start | bytes 4325384 | tf_op jit(solution)/shard_map/ppermute | solution.py:189
  420.7 48.0 %collective-permute-start.77 = (f32[1408,256]{1,0:T(8,128)}, f32[1408,256]{1,0:T(8,128)}, u32[]{:S(2)}, u32[]{:S(2)}) collective-permute-start(f32[1408,256]{1,0:T(8,128)} %convolution_add_fusion), channel_id=1, source_target_pairs={{24,16},{28,20},{16,8},{20,12},{25,17},{29,21},{17,9},{21,13},{26,... | collective-permute-start | bytes 4325384 | tf_op jit(solution)/shard_map/ppermute | solution.py:189
  423.5 45.2 %collective-permute-start.13 = (f32[128,2048]{1,0:T(8,128)S(1)}, f32[128,2048]{1,0:T(8,128)}, u32[]{:S(2)}, u32[]{:S(2)}) collective-permute-start(f32[128,2048]{1,0:T(8,128)S(1)} %copy-done.66), channel_id=1, source_target_pairs={{0,1},{1,0},{2,3},{3,2},{4,5},{5,4},{6,7},{7,6},{8,9},{9,8},{10,11... | collective-permute-start | bytes 3145736 | tf_op jit(solution)/shard_map/ppermute | solution.py:231
  433.4 36.9 %collective-permute-start.32 = (f32[128,2048]{1,0:T(8,128)}, f32[128,2048]{1,0:T(8,128)}, u32[]{:S(2)}, u32[]{:S(2)}) collective-permute-start(f32[128,2048]{1,0:T(8,128)} %convolution_add_fusion.11), channel_id=1, source_target_pairs={{0,1},{1,0},{2,3},{3,2},{4,5},{5,4},{6,7},{7,6},{8,9},{9,8},{10,11... | collective-permute-start | bytes 3145736 | tf_op jit(solution)/shard_map/ppermute | solution.py:170
  434.2 54.2 %collective-permute-start.22 = (f32[160,2048]{1,0:T(8,128)S(1)}, f32[160,2048]{1,0:T(8,128)S(1)}, u32[]{:S(2)}, u32[]{:S(2)}) collective-permute-start(f32[160,2048]{1,0:T(8,128)S(1)} %copy-done.54), channel_id=1, source_target_pairs={{0,2},{1,3},{2,0},{3,1},{4,6},{5,7},{6,4},{7,5},{8,10},{9,11},{10,... | collective-permute-start | bytes 3932168 | tf_op jit(solution)/shard_map/ppermute | solution.py:171
  468.7 33.7 %collective-permute-start.35 = (f32[160,2048]{1,0:T(8,128)S(1)}, f32[160,2048]{1,0:T(8,128)S(1)}, u32[]{:S(2)}, u32[]{:S(2)}) collective-permute-start(f32[160,2048]{1,0:T(8,128)S(1)} %convolution_add_fusion.6), channel_id=1, source_target_pairs={{0,1},{1,0},{2,3},{3,2},{4,5},{5,4},{6,7},{7,6},{8,9},{9,8},{10,11... | collective-permute-start | bytes 3932168 | tf_op jit(solution)/shard_map/ppermute | solution.py:170
  468.7 37.5 %collective-permute-start.68 = (f32[256,1408]{1,0:T(8,128)}, f32[256,1408]{1,0:T(8,128)}, u32[]{:S(2)}, u32[]{:S(2)}) collective-permute-start(f32[256,1408]{1,0:T(8,128)} %get-tuple-element.111), channel_id=1, source_target_pairs={{24,16},{28,20},{16,8},{20,12},{8,0},{12,4},{25,17},{29,21},{17,9}... | collective-permute-start | bytes 4325384 | tf_op jit(solution)/shard_map/ppermute | solution.py:189
  470.3 37.6 %collective-permute-start.66 = (f32[256,1408]{1,0:T(8,128)}, f32[256,1408]{1,0:T(8,128)}, u32[]{:S(2)}, u32[]{:S(2)}) collective-permute-start(f32[256,1408]{1,0:T(8,128)} %get-tuple-element.110), channel_id=1, source_target_pairs={{0,8},{4,12},{8,16},{12,20},{16,24},{20,28},{1,9},{5,13},{9,17},{1... | collective-permute-start | bytes 4325384 | tf_op jit(solution)/shard_map/ppermute | solution.py:189
  487.2 49.9 %collective-permute-start.78 = (f32[1408,256]{1,0:T(8,128)}, f32[1408,256]{1,0:T(8,128)}, u32[]{:S(2)}, u32[]{:S(2)}) collective-permute-start(f32[1408,256]{1,0:T(8,128)} %get-tuple-element.107), channel_id=1, source_target_pairs={{24,16},{28,20},{16,8},{20,12},{8,0},{12,4},{25,17},{29,21},{17,9}... | collective-permute-start | bytes 4325384 | tf_op jit(solution)/shard_map/ppermute | solution.py:189
  488.5 50.6 %collective-permute-start.76 = (f32[1408,256]{1,0:T(8,128)}, f32[1408,256]{1,0:T(8,128)}, u32[]{:S(2)}, u32[]{:S(2)}) collective-permute-start(f32[1408,256]{1,0:T(8,128)} %get-tuple-element.106), channel_id=1, source_target_pairs={{0,8},{4,12},{8,16},{12,20},{16,24},{20,28},{1,9},{5,13},{9,17},{1... | collective-permute-start | bytes 4325384 | tf_op jit(solution)/shard_map/ppermute | solution.py:189
  502.4 132.8 %collective-permute-start.48 = (f32[576,1536]{1,0:T(8,128)S(1)}, f32[576,1536]{1,0:T(8,128)S(1)}, u32[]{:S(2)}, u32[]{:S(2)}) collective-permute-start(f32[576,1536]{1,0:T(8,128)S(1)} %pad_maximum_fusion.2), channel_id=1, source_target_pairs={{0,4},{4,0},{8,12},{12,8},{16,20},{20,16},{24,28},{28,24},{1,5},{5... | collective-permute-start | bytes 10616840 | tf_op jit(solution)/shard_map/ppermute | solution.py:234
  506.2 97.1 %collective-permute-start.73 = (f32[256,1408]{1,0:T(8,128)}, f32[256,1408]{1,0:T(8,128)}, u32[]{:S(2)}, u32[]{:S(2)}) collective-permute-start(f32[256,1408]{1,0:T(8,128)} %get-tuple-element.109), channel_id=1, source_target_pairs={{24,16},{28,20},{16,8},{20,12},{8,0},{12,4},{25,17},{29,21},{17,9}... | collective-permute-start | bytes 4325384 | tf_op jit(solution)/shard_map/ppermute | solution.py:189
  507.9 95.9 %collective-permute-start.71 = (f32[256,1408]{1,0:T(8,128)}, f32[256,1408]{1,0:T(8,128)}, u32[]{:S(2)}, u32[]{:S(2)}) collective-permute-start(f32[256,1408]{1,0:T(8,128)} %get-tuple-element.108), channel_id=1, source_target_pairs={{0,8},{4,12},{8,16},{12,20},{16,24},{20,28},{1,9},{5,13},{9,17},{1... | collective-permute-start | bytes 4325384 | tf_op jit(solution)/shard_map/ppermute | solution.py:189
  537.1 66.1 %collective-permute-start.55 = (f32[288,1024]{1,0:T(8,128)S(1)}, f32[288,1024]{1,0:T(8,128)S(1)}, u32[]{:S(2)}, u32[]{:S(2)}) collective-permute-start(f32[288,1024]{1,0:T(8,128)S(1)} %constant_dynamic-slice_fusion), channel_id=1, source_target_pairs={{0,4},{4,0},{8,12},{12,8},{16,20},{20,16},{24,28},{28,24},{1,5},{5... | collective-permute-start | bytes 3538952 | tf_op jit(solution)/shard_map/ppermute | solution.py:234
  539.0 70.0 %collective-permute-start.33 = (f32[128,2048]{1,0:T(8,128)S(1)}, f32[128,2048]{1,0:T(8,128)S(1)}, u32[]{:S(2)}, u32[]{:S(2)}) collective-permute-start(f32[128,2048]{1,0:T(8,128)S(1)} %fusion.6), channel_id=1, source_target_pairs={{0,2},{1,3},{2,0},{3,1},{4,6},{5,7},{6,4},{7,5},{8,10},{9,11},{10,... | collective-permute-start | bytes 3145736 | tf_op jit(solution)/shard_map/ppermute | solution.py:171
  603.8 30.8 %collective-permute-start.36 = (f32[160,2048]{1,0:T(8,128)S(1)}, f32[160,2048]{1,0:T(8,128)S(1)}, u32[]{:S(2)}, u32[]{:S(2)}) collective-permute-start(f32[160,2048]{1,0:T(8,128)S(1)} %fusion.5), channel_id=1, source_target_pairs={{0,2},{1,3},{2,0},{3,1},{4,6},{5,7},{6,4},{7,5},{8,10},{9,11},{10,... | collective-permute-start | bytes 3932168 | tf_op jit(solution)/shard_map/ppermute | solution.py:171
  609.0 32.3 %collective-permute-start.23 = (f32[160,2048]{1,0:T(8,128)S(1)}, f32[160,2048]{1,0:T(8,128)S(1)}, u32[]{:S(2)}, u32[]{:S(2)}) collective-permute-start(f32[160,2048]{1,0:T(8,128)S(1)} %add.617), channel_id=1, source_target_pairs={{0,1},{1,0},{2,3},{3,2},{4,5},{5,4},{6,7},{7,6},{8,9},{9,8},{10,11... | collective-permute-start | bytes 3932168 | tf_op jit(solution)/shard_map/ppermute | solution.py:231
  609.9 130.6 %collective-permute-start.34 = (f32[128,2048]{1,0:T(8,128)S(1)}, f32[128,2048]{1,0:T(8,128)S(1)}, u32[]{:S(2)}, u32[]{:S(2)}) collective-permute-start(f32[128,2048]{1,0:T(8,128)S(1)} %fusion.49), channel_id=1, source_target_pairs={{0,1},{1,0},{2,3},{3,2},{4,5},{5,4},{6,7},{7,6},{8,9},{9,8},{10,11... | collective-permute-start | bytes 3145736 | tf_op jit(solution)/shard_map/ppermute | solution.py:231
  612.3 72.4 %collective-permute-start.57 = (f32[512,256]{1,0:T(8,128)S(1)}, f32[512,256]{1,0:T(8,128)S(1)}, u32[]{:S(2)}, u32[]{:S(2)}) collective-permute-start(f32[512,256]{1,0:T(8,128)S(1)} %fusion.58), channel_id=1, source_target_pairs={{0,8},{4,12},{24,16},{28,20},{1,9},{5,13},{25,17},{29,21},{2,10},{... | collective-permute-start | bytes 1572872 | tf_op jit(solution)/shard_map/ppermute | solution.py:189
  638.0 42.8 %collective-permute-start.49 = (f32[256,1536]{1,0:T(8,128)S(1)}, f32[256,1536]{1,0:T(8,128)S(1)}, u32[]{:S(2)}, u32[]{:S(2)}) collective-permute-start(f32[256,1536]{1,0:T(8,128)S(1)} %fusion.68), channel_id=1, source_target_pairs={{0,8},{4,12},{24,16},{28,20},{1,9},{5,13},{25,17},{29,21},{2,10},{... | collective-permute-start | bytes 4718600 | tf_op jit(solution)/shard_map/ppermute | solution.py:189
  645.8 30.2 %collective-permute-start.40 = (f32[5120]{0:T(1024)S(1)}, f32[5120]{0:T(1024)S(1)}, u32[]{:S(2)}, u32[]{:S(2)}) collective-permute-start(f32[5120]{0:T(1024)S(1)} %fusion.188), channel_id=1, source_target_pairs={{0,8},{4,12},{8,0},{12,4},{16,24},{20,28},{24,16},{28,20},{1,9},{5... | collective-permute-start | bytes 61448 | tf_op jit(solution)/shard_map/ppermute | solution.py:178
  682.0 47.9 %collective-permute-start.50 = (f32[256,1536]{1,0:T(8,128)S(1)}, f32[256,1536]{1,0:T(8,128)S(1)}, u32[]{:S(2)}, u32[]{:S(2)}) collective-permute-start(f32[256,1536]{1,0:T(8,128)S(1)} %convolution_add_fusion.4), channel_id=1, source_target_pairs={{0,8},{4,12},{8,16},{12,20},{1,9},{5,13},{9,17},{13,21},{2,10},{6,... | collective-permute-start | bytes 4718600 | tf_op jit(solution)/shard_map/ppermute | solution.py:189
  683.5 54.3 %collective-permute-start.52 = (f32[256,1536]{1,0:T(8,128)S(1)}, f32[256,1536]{1,0:T(8,128)S(1)}, u32[]{:S(2)}, u32[]{:S(2)}) collective-permute-start(f32[256,1536]{1,0:T(8,128)S(1)} %convolution_add_fusion.4), channel_id=1, source_target_pairs={{24,16},{28,20},{16,8},{20,12},{25,17},{29,21},{17,9},{21,13},{26,... | collective-permute-start | bytes 4718600 | tf_op jit(solution)/shard_map/ppermute | solution.py:189
  685.3 42.7 %collective-permute-start.58 = (f32[512,256]{1,0:T(8,128)S(1)}, f32[512,256]{1,0:T(8,128)S(1)}, u32[]{:S(2)}, u32[]{:S(2)}) collective-permute-start(f32[512,256]{1,0:T(8,128)S(1)} %convolution_add_fusion.22), channel_id=1, source_target_pairs={{0,8},{4,12},{8,16},{12,20},{1,9},{5,13},{9,17},{13,21},{2,10},{6,... | collective-permute-start | bytes 1572872 | tf_op jit(solution)/shard_map/ppermute | solution.py:189
  688.6 39.3 %collective-permute-start.60 = (f32[512,256]{1,0:T(8,128)S(1)}, f32[512,256]{1,0:T(8,128)S(1)}, u32[]{:S(2)}, u32[]{:S(2)}) collective-permute-start(f32[512,256]{1,0:T(8,128)S(1)} %convolution_add_fusion.22), channel_id=1, source_target_pairs={{24,16},{28,20},{16,8},{20,12},{25,17},{29,21},{17,9},{21,13},{26,... | collective-permute-start | bytes 1572872 | tf_op jit(solution)/shard_map/ppermute | solution.py:189
  739.2 40.8 %collective-permute-start.53 = (f32[256,1536]{1,0:T(8,128)S(1)}, f32[256,1536]{1,0:T(8,128)S(1)}, u32[]{:S(2)}, u32[]{:S(2)}) collective-permute-start(f32[256,1536]{1,0:T(8,128)S(1)} %get-tuple-element.102), channel_id=1, source_target_pairs={{24,16},{28,20},{16,8},{20,12},{8,0},{12,4},{25,17},{29,21},{17,9}... | collective-permute-start | bytes 4718600 | tf_op jit(solution)/shard_map/ppermute | solution.py:189
  740.5 40.8 %collective-permute-start.51 = (f32[256,1536]{1,0:T(8,128)S(1)}, f32[256,1536]{1,0:T(8,128)S(1)}, u32[]{:S(2)}, u32[]{:S(2)}) collective-permute-start(f32[256,1536]{1,0:T(8,128)S(1)} %get-tuple-element.101), channel_id=1, source_target_pairs={{0,8},{4,12},{8,16},{12,20},{16,24},{20,28},{1,9},{5,13},{9,17},{1... | collective-permute-start | bytes 4718600 | tf_op jit(solution)/shard_map/ppermute | solution.py:189
  (181 other events, 2180.4 us)

commit v2 on v1

v2 whole, which is shorter than its diff:
```python
import jax
import jax.numpy as jnp
from jax import lax
from jax.experimental import pallas as pl
from jax.experimental.pallas import tpu as pltpu
from jax.sharding import PartitionSpec as P

LCHUNK = 256
norm_eps = 1e-06
FL = {'cot': (0,), 'cot_ready': (0, 1), 'prefix': (0,), 'glu': (), 'branch': (), 'inner': (0,), 'feed': (1,), 'one': (), 'one_ready': (0,), 'gated': (), 'gated_ready': (0,), 'kernel': 0, 'kernel_rec': 0, 'gate': (0,), 'far_down': (0,), 'far_gate': (), 'far_up': (0,), 'joined': (), 'near_branch': (), 'branch_ready': (), 'out': (), 'far_joined': (), 'far_out': (), 'own_down': (2,), 'own_gate': (2,), 'own_up': (2,), 'own_joined': (), 'own_out': (), 'end_down': (1, 2), 'end_gate': (1, 2), 'end_up': (1, 2), 'end_joined': (), 'end_out': (), 'sends': 7, 'direct': 0, 'steps': (1, 2, 4)}
F32 = jnp.float32
BF16 = jnp.bfloat16

CORE_PAIRS = [(i, i ^ 1) for i in range(4)]
X_PAIRS = [(i, i ^ 2) for i in range(4)]
Y_PAIRS = [(i, i ^ 1) for i in range(8)]
Z_PAIRS = [(i, i ^ 2) for i in range(8)]
FAR_PAIRS = [(i, i ^ 4) for i in range(8)]


def dot(left, right):
    return jnp.dot(left, right, preferred_element_type=F32)


def left_dot(left, right):
    return lax.dot_general(left, right, (((0,), (0,)), ((), ())), preferred_element_type=F32)


def right_dot(left, right):
    return lax.dot_general(left, right, (((1,), (1,)), ((), ())), preferred_element_type=F32)


def silu_slope(values):
    sig = jax.nn.sigmoid(values)
    return sig * (1.0 + values * (1.0 - sig))


def pick(name, options):
    return [options[i] for i in FL[name]]


def spark(*others):
    firsts = [
        lax.reshape(lax.slice(other, (0,) * other.ndim, (1,) * other.ndim), ()).astype(F32)
        for other in others
    ]
    return sum(firsts) * 0.0


def after(value, *others):
    return value + spark(*others) if others else value


def later(index, *others):
    return index + spark(*others).astype(jnp.int32) if others else index


def place_kernel(moves, flip_ref, *refs):
    out_ref = refs[-1]
    for flip, plan in enumerate(moves):

        @pl.when((flip_ref[0] != 0) == bool(flip))
        def _():
            for index, source, size, target in plan:
                out_ref[target : target + size, :] = refs[index][source : source + size, :].astype(
                    BF16
                )


def placed(values, rows, plan, other_plan=None, flip=0):
    width = values[0].shape[1]
    block = 256
    moves = (plan,) if other_plan is None else (plan, other_plan)
    return pl.pallas_call(
        lambda *refs: place_kernel(moves, *refs),
        grid=(width // block,),
        in_specs=[pl.BlockSpec(memory_space=pltpu.SMEM)]
        + [pl.BlockSpec((value.shape[0], block), lambda i: (0, i)) for value in values],
        out_specs=pl.BlockSpec((rows, block), lambda i: (0, i)),
        out_shape=jax.ShapeDtypeStruct((rows, width), BF16),
        compiler_params=pltpu.CompilerParams(vmem_limit_bytes=24 * 1024 * 1024),
        cost_estimate=pl.CostEstimate(
            flops=rows * width, bytes_accessed=rows * width * 6, transcendentals=0
        ),
        name="placed",
    )(jnp.full((1,), flip, jnp.int32), *values)


def norm_kernel(gain_ref, *refs):
    out_ref = refs[-1]
    target = 0
    for ref in refs[:-1]:
        values = ref[...]
        scale = lax.rsqrt(jnp.mean(values * values, axis=1, keepdims=True) + norm_eps)
        size = values.shape[0]
        out_ref[target : target + size, :] = (values * scale * gain_ref[...]).astype(BF16)
        target += size


def normed_rows(values, gain):
    width = gain.shape[0]
    rows = sum(value.shape[0] for value in values)
    return pl.pallas_call(
        norm_kernel,
        out_shape=jax.ShapeDtypeStruct((rows, width), BF16),
        compiler_params=pltpu.CompilerParams(vmem_limit_bytes=32 * 1024 * 1024),
        cost_estimate=pl.CostEstimate(
            flops=rows * width * 5, bytes_accessed=rows * width * 6, transcendentals=rows
        ),
        name="normed_rows",
    )(gain[None, :], *values)


def block_kernel(depth, at_ref, left_ref, right_ref, *refs):
    out_ref = refs[-1]
    step = pl.program_id(0)
    product = lax.dot_general(
        left_ref[...], right_ref[...], (((0,), (0,)), ((), ())), preferred_element_type=F32
    )

    @pl.when(step == 0)
    def _():
        total = product
        for ref in refs[:-1]:
            total += ref[...]
        out_ref[...] = total

    @pl.when(step > 0)
    def _():
        out_ref[...] += product


def block_product(left, left_at, right, right_at, *adds):
    block = 256
    rows = left.shape[0]
    steps = 3
    depth = rows // steps
    height = left.shape[1] if left_at is None else block
    width = right.shape[1] if right_at is None else block
    at = jnp.stack([jnp.int32(0) if p is None else p for p in (left_at, right_at)])

    def spec(wide, which, picked):
        def place(step, at_ref):
            return step, (at_ref[which] if picked else 0)

        return pl.BlockSpec((depth, wide), place)

    whole = pl.BlockSpec((height, width), lambda step, at_ref: (0, 0))
    return pl.pallas_call(
        lambda *refs: block_kernel(depth, *refs),
        grid_spec=pltpu.PrefetchScalarGridSpec(
            num_scalar_prefetch=1,
            grid=(steps,),
            in_specs=[
                spec(height, 0, left_at is not None),
                spec(width, 1, right_at is not None),
                *[whole] * len(adds),
            ],
            out_specs=whole,
        ),
        out_shape=jax.ShapeDtypeStruct((height, width), F32),
        compiler_params=pltpu.CompilerParams(vmem_limit_bytes=32 * 1024 * 1024),
        name="block_product",
    )(at, left, right, *adds)


def group_scan(a, b, backward):
    place = lax.broadcasted_iota(jnp.int32, a.shape, 0)
    for step in (1, 2, 4):
        shift = 8 - step if backward else step
        inside = place < 8 - step if backward else place >= step
        a_shift = jnp.where(inside, pltpu.roll(a, shift, 0), 1.0)
        b_shift = jnp.where(inside, pltpu.roll(b, shift, 0), 0.0)
        b = a * b_shift + b
        a = a * a_shift
    return a, b


def forth_kernel(a_ref, b_ref, x_ref, p_ref, before_ref, p_before_ref):
    rows, width = a_ref.shape
    first = lax.broadcasted_iota(jnp.int32, (8, width), 0) == 0

    def last(value):
        return jnp.broadcast_to(value[7:8, :], (8, width))

    def run(begin, count, long):
        def body(step, carry):
            carry_x, carry_p = carry
            here = pl.ds(pl.multiple_of(begin + step * 8, 8), 8)
            decay = a_ref[here, :]
            a, b = group_scan(decay, b_ref[here, :], False)
            x = b + a * carry_x
            x_ref[here, :] = x
            before = jnp.where(first, carry_x, pltpu.roll(x, 1, 0))
            before_ref[here, :] = jnp.where(decay == 0.0, 0.0, before)
            if long:
                product = a * carry_p
                p_ref[here, :] = product
                p_before_ref[here, :] = jnp.where(first, carry_p, pltpu.roll(product, 1, 0))
                carry_p = last(product)
            return last(x), carry_p

        start = (jnp.zeros((8, width), F32), jnp.ones((8, width), F32))
        lax.fori_loop(0, count, body, start, unroll=4)

    run(0, LCHUNK // 8, True)
    run(LCHUNK, (rows - LCHUNK) // 8, False)


def back_kernel(a_ref, b_ref, x_ref, p_ref):
    rows, width = a_ref.shape
    end = lax.broadcasted_iota(jnp.int32, (8, width), 0) == 7

    def top(value):
        return jnp.broadcast_to(value[0:1, :], (8, width))

    def run(begin, count, long):
        def body(step, carry):
            carry_x, carry_p, carry_a = carry
            here = pl.ds(pl.multiple_of(begin + (count - 1 - step) * 8, 8), 8)
            decay = a_ref[here, :]
            link = jnp.where(end, carry_a, pltpu.roll(decay, 7, 0))
            a, b = group_scan(link, b_ref[here, :], True)
            x = b + a * carry_x
            x_ref[here, :] = x
            if long:
                product = a * carry_p
                p_ref[here, :] = product
                carry_p = top(product)
            return top(x), carry_p, top(decay)

        one = jnp.ones((8, width), F32)
        lax.fori_loop(0, count, body, (jnp.zeros((8, width), F32), one, one), unroll=4)

    run(0, LCHUNK // 8, True)
    run(LCHUNK, (rows - LCHUNK) // 8, False)


def scan(a, b, backward):
    rows, width = a.shape
    block = 256
    spec = pl.BlockSpec((rows, block), lambda i: (0, i))
    long_spec = pl.BlockSpec((LCHUNK, block), lambda i: (0, i))
    shape = jax.ShapeDtypeStruct((rows, width), F32)
    long_shape = jax.ShapeDtypeStruct((LCHUNK, width), F32)
    times = 1 if backward else 2
    return pl.pallas_call(
        back_kernel if backward else forth_kernel,
        grid=(width // block,),
        in_specs=[spec, spec],
        out_specs=[spec, long_spec] * times,
        out_shape=[shape, long_shape] * times,
        compiler_params=pltpu.CompilerParams(vmem_limit_bytes=24 * 1024 * 1024),
        cost_estimate=pl.CostEstimate(
            flops=rows * width * 12, bytes_accessed=rows * width * 14, transcendentals=0
        ),
        name="scan_back" if backward else "scan_forth",
    )(a, b)


def carry_of(decay, local, backward, *before):
    count, mine = lax.axis_size("seq"), lax.axis_index("seq")
    ends = jnp.stack([decay, local])
    if count != 8:
        pieces = lax.all_gather(ends, "seq")
        order = jnp.arange(count)
        total = jnp.zeros_like(local)
        for step in range(count):
            i = count - 1 - step if backward else step
            use = (order[i] > mine) if backward else (order[i] < mine)
            total = jnp.where(use, pieces[i, 0] * total + pieces[i, 1], total)
        return total, total
    partner = lax.ppermute(ends, "seq", Y_PAIRS)
    first = (mine % 2 == 1) if backward else (mine % 2 == 0)
    early = jnp.where(first, ends, partner)
    late = jnp.where(first, partner, ends)
    pair = after(jnp.stack([early[0] * late[0], late[0] * early[1] + late[1]]), *before)
    total = jnp.zeros_like(local)
    got = []
    for hops in (3, 2, 1):
        if backward:
            pairs = [(i + 2 * hops, i) for i in range(8 - 2 * hops)]
        else:
            pairs = [(i, i + 2 * hops) for i in range(8 - 2 * hops)]
        got.append(lax.ppermute(pair, "seq", pairs))
    for piece in got:
        total = piece[0] * total + piece[1]
    return jnp.where(first, total, partner[0] * total + partner[1]), partner


def small_psum(value):
    value = value + lax.ppermute(value, "mp", CORE_PAIRS)
    return value + lax.ppermute(value, "mp", X_PAIRS)


def summed_half(send, keep):
    value = keep + lax.ppermute(send, "mp", CORE_PAIRS)
    return value + lax.ppermute(value, "mp", X_PAIRS), value


def per_device(
    tokens,
    attn_gain,
    w_input,
    w_forget,
    w_rgate,
    gnorm_gain,
    lower_bound,
    w_out,
    mlp_gain,
    w_gate,
    w_up,
    w_down,
    local_lengths,
    cotangent,
):
    rows, width = tokens.shape
    short_rows = rows - LCHUNK
    count, mine = lax.axis_size("seq"), lax.axis_index("seq")
    fast = count == 8
    core = lax.axis_index("mp") % 2
    side = mine % 2
    chunks = ((LCHUNK, short_rows), (0, LCHUNK))

    def half(value, own, chunk):
        first, size = chunk
        which = core if own else 1 - core
        return lax.dynamic_slice_in_dim(value, first + which * (size // 2), size // 2, 0)

    def swap_core(value):
        return lax.ppermute(value, "mp", CORE_PAIRS)

    def swap_y(value):
        return lax.ppermute(value, "seq", Y_PAIRS)

    def canonical(parts):
        out = []
        for own, other in (parts[1], parts[0]):
            out.append(jnp.where(core == 0, own, other))
            out.append(jnp.where(core == 0, other, own))
        return jnp.concatenate(out, axis=0)

    lengths_row = local_lengths[0]
    offsets = jnp.cumsum(lengths_row) - lengths_row
    starts = jnp.any(
        jnp.arange(short_rows, dtype=jnp.int32)[:, None] == offsets[None, :], axis=1
    )[:, None]

    sizes = [size // 2 for _, size in chunks]
    cot_own = [(half(cotangent, True, c), half(cotangent, False, c)) for c in chunks]

    def near_rows(value, *ready):
        own = after(lax.ppermute(value, "seq", Z_PAIRS), *ready)
        return [own, swap_core(own)]

    def near_cot(index, *before):
        value = near_rows(
            after(cot_own[index][0].astype(F32), *before),
            *pick("cot_ready", (middle_own[0], middle_own[1])),
        )
        h = sizes[index]
        return placed(value, 2 * h, [(0, 0, h, 0), (1, 0, h, h)])

    if fast:
        near_cots = [None, None]

    stream = tokens.astype(F32)
    first_gain = attn_gain.astype(F32)
    first_scale = lax.rsqrt(jnp.mean(stream * stream, axis=1, keepdims=True) + norm_eps)
    normed_one_wide = stream * first_scale * first_gain
    normed_one = normed_one_wide.astype(BF16)
    pre_forget = dot(normed_one, w_forget)
    pre_input = dot(normed_one, w_input)
    pre_rgate = dot(normed_one, w_rgate)
    forget_sig = jax.nn.sigmoid(pre_forget)
    forget = lower_bound + (1.0 - lower_bound) * forget_sig
    input_act = jax.nn.silu(pre_input)
    drive = input_act * (1.0 - forget)
    is_start = jnp.concatenate([jnp.zeros((LCHUNK, 1), bool), starts], axis=0)
    decay = jnp.where(is_start, 0.0, forget)
    states_local, long_decay, before_local, before_decay = scan(decay, drive, False)

    def entered(local, product, carry):
        return jnp.concatenate(
            [local[:LCHUNK] + product * carry[None, :], local[LCHUNK:]], axis=0
        )

    state_gain = gnorm_gain.astype(F32)
    rgate_act = jax.nn.silu(pre_rgate)
    second_gain = mlp_gain.astype(F32)

    def row_scale(values):
        return lax.rsqrt(jnp.mean(values * values, axis=1, keepdims=True) + norm_eps)

    def glu(normed, d_hid):
        gate = dot(normed, w_gate)
        up = dot(normed, w_up)
        act = jax.nn.silu(gate)
        hidden = (act * up).astype(BF16)
        d_gate = (d_hid * up * silu_slope(gate)).astype(BF16)
        d_up = (d_hid * act).astype(BF16)
        return hidden, d_gate, d_up

    states_of, scale_of, gated_of, middle_own, middle_other = [], [], [], [], []
    for index, (first, size) in enumerate(chunks):
        local = states_local[first : first + size]
        if index == 1:
            carry_in, _ = carry_of(
                long_decay[-1], states_local[LCHUNK - 1], False, *pick("prefix", (short_sent,))
            )
            local = local + long_decay * carry_in[None, :]
        squares = small_psum(jnp.sum(local * local, axis=1))
        scale = lax.rsqrt(squares / width + norm_eps)[:, None]
        gated = local * scale * state_gain * rgate_act[first : first + size]
        gated16 = gated.astype(BF16)
        states_of.append(local)
        scale_of.append(scale)
        gated_of.append(gated)
        h = size // 2
        send = dot(lax.dynamic_slice_in_dim(gated16, (1 - core) * h, h, 0), w_out)
        keep = dot(lax.dynamic_slice_in_dim(gated16, core * h, h, 0), w_out)
        if index == 0:
            short_sent = send
        total, kept = summed_half(send, keep)
        own = half(tokens, True, (first, size)).astype(F32) + total
        middle_own.append(own)
        middle_other.append(swap_core(own))

    if fast:
        near_cots = [near_cot(i, *pick("cot", (carry_in, short_sent))) for i in (0, 1)]
    cot_rows = jnp.concatenate(
        [part for pair in cot_own for part in pair], axis=0
    )
    d_hidden = right_dot(cot_rows, w_down)
    states = jnp.concatenate([states_of[1], states_of[0]], axis=0)
    state_scale = jnp.concatenate([scale_of[1], scale_of[0]], axis=0)
    gated_wide = jnp.concatenate([gated_of[1], gated_of[0]], axis=0)
    gated = gated_wide.astype(BF16)
    normed_state = states * state_scale

    offset = 0
    main, d_mid_own, d_mid_other, hat_grad, feeds = [], [], [], [], []
    for index, (first, size) in enumerate(chunks):
        h = size // 2
        middle = jnp.concatenate([middle_own[index], middle_other[index]], axis=0)
        scale = row_scale(middle)
        hat = middle * scale
        normed = (hat * second_gain).astype(BF16)
        hidden, d_gate, d_up = glu(normed, d_hidden[offset : offset + size])
        offset += size
        main.append((normed, hidden, d_gate, d_up))
        send = right_dot(d_gate[h:], w_gate) + right_dot(d_up[h:], w_up)
        keep = right_dot(d_gate[:h], w_gate) + right_dot(d_up[:h], w_up)
        d_normed, glu_kept = summed_half(send, keep)
        hat, scale = hat[:h], scale[:h]
        hat_grad.append(jnp.sum(d_normed * hat, axis=0))
        e = d_normed * second_gain
        turn = scale * (e - hat * jnp.mean(e * hat, axis=1, keepdims=True))
        d_mid_own.append(cot_own[index][0].astype(F32) + turn)
        d_mid_other.append(cot_own[index][1].astype(F32) + swap_core(turn))

    normed_two, hidden, d_gate, d_up = (
        jnp.concatenate([main[0][i], main[1][i]], axis=0) for i in range(4)
    )

    if fast:
        sets = [(cot_rows, normed_two, hidden, d_gate, d_up)]
        for own, cot in zip(middle_own, near_cots):
            normed = normed_rows(near_rows(own), after(second_gain, *pick("glu", (glu_kept,))))
            sets.append((cot, normed, *glu(normed, right_dot(cot, w_down))))
        arrived = sets[-1][1]
        cots, normed, hiddens, gates, ups = (
            jnp.concatenate(parts, axis=0) for parts in zip(*sets)
        )
        block = width // 8
        plane = mine // 2
        planes = (plane, jnp.bitwise_xor(plane, 2))
        h = rows // 2

        def columns(value, start):
            return lax.dynamic_slice_in_dim(value, start * block, block, 1)

        def part_down(i, y):
            return left_dot(hiddens, columns(cots, 2 * planes[i] + y))

        down_sent = part_down(1, 1 - side)
        down_got = swap_y(down_sent)

    d_branch_wide = canonical(list(zip(d_mid_own, d_mid_other)))
    if fast:
        d_branch_wide = after(d_branch_wide, *pick("branch", (down_sent, down_got)))
    d_branch = d_branch_wide.astype(BF16)
    d_gated = right_dot(d_branch, w_out)
    grad_gnorm = jnp.sum(d_gated * normed_state * rgate_act, axis=0)
    d_rgate_wide = d_gated * normed_state * state_gain * silu_slope(pre_rgate)
    d_normed = d_gated * state_gain * rgate_act
    inner = small_psum(jnp.sum(d_normed * normed_state, axis=1))
    d_normed_last = d_mid_own[1]
    for index, (first, size) in enumerate(chunks):
        size = size // 2
        start = later(0, *pick("feed", (d_normed_last, inner)))
        feeds.append(
            [
                dot(lax.dynamic_slice_in_dim(main[index][1], start + i * size, size, 0), w_down)
                for i in (1, 0)
            ]
        )
    if fast:
        inner = after(inner, *pick("inner", (down_got,)))
    d_states = state_scale * (d_normed - normed_state * (inner / width)[:, None])
    back_local, back_decay = scan(decay, d_states, True)
    carried_in, carry_sent = carry_of(forget[0] * back_decay[0], forget[0] * back_local[0], True)
    carried = entered(back_local, back_decay, carried_in)
    states_prev = entered(before_local, before_decay, carry_in)
    d_forget = carried * (states_prev - input_act)
    d_input_wide = carried * (1.0 - forget) * silu_slope(pre_input)
    d_pforget_wide = d_forget * (1.0 - lower_bound) * forget_sig * (1.0 - forget_sig)
    grad_bound = jnp.sum(d_forget * (1.0 - forget_sig), axis=0)
    d_input = d_input_wide.astype(BF16)
    d_pforget = d_pforget_wide.astype(BF16)
    d_rgate = d_rgate_wide.astype(BF16)

    d_stream, first_grad = [], []
    for index, chunk in enumerate(chunks):
        both = []
        for own in (False, True):
            both.append(
                right_dot(half(d_input, own, chunk), w_input)
                + right_dot(half(d_pforget, own, chunk), w_forget)
                + right_dot(half(d_rgate, own, chunk), w_rgate)
            )
        d_normed_one, _ = summed_half(*both)
        part = half(tokens, True, chunk).astype(F32)
        scale = row_scale(part)
        hat = part * scale
        first_grad.append(jnp.sum(d_normed_one * hat, axis=0))
        e = d_normed_one * first_gain
        turn = scale * (e - hat * jnp.mean(e * hat, axis=1, keepdims=True))
        d_stream.append((d_mid_own[index] + turn, d_mid_other[index] + swap_core(turn)))
    grad_tokens = canonical(d_stream).astype(BF16)

    mixed = []
    for own, other, feed in zip(middle_own, middle_other, feeds):
        value, _ = summed_half(*feed)
        mixed.append((own + value, other + swap_core(value)))
    mixed_out = canonical(mixed).astype(BF16)

    channels = grad_gnorm.shape[0]
    sends = []
    if not fast:

        def scattered(value, dim):
            return lax.psum_scatter(value, "seq", scatter_dimension=dim, tiled=True)

        grads = (
            scattered(left_dot(normed_one, d_input), 0),
            scattered(left_dot(normed_one, d_pforget), 0),
            scattered(left_dot(normed_one, d_rgate), 0),
            scattered(left_dot(gated, d_branch), 1),
            scattered(left_dot(normed_two, d_gate), 0),
            scattered(left_dot(normed_two, d_up), 0),
            scattered(left_dot(hidden, cot_rows), 1),
        )
    else:
        def near_columns(value, before, *ready):
            parts = [
                lax.dynamic_slice(
                    value,
                    (later(core * h, *before), 2 * jnp.bitwise_xor(q, 1) * block),
                    (h, 2 * block),
                )
                for q in planes
            ]
            low, high = [(0, 0, h, 0), (1, 0, h, h)], [(0, 0, h, h), (1, 0, h, 0)]
            return placed(near_rows(jnp.concatenate(parts, axis=1)), rows, low, high, later(core, *ready))

        def near_whole(value, *ready):
            near = lax.ppermute(value, "seq", Z_PAIRS)
            return placed([near], rows, [(0, 0, rows, 0)], flip=later(0, *ready))

        def pair_columns(value):
            return jnp.concatenate(
                [lax.dynamic_slice_in_dim(value, 2 * q * block, 2 * block, 1) for q in planes],
                axis=1,
            )

        joined_wide = jnp.concatenate([d_input_wide, d_pforget_wide, d_rgate_wide], axis=1)
        near_one = near_columns(
            normed_one_wide, pick("one", (arrived, carried_in)), *pick("one_ready", (joined_wide,))
        )
        near_gated = near_whole(
            after(gated_wide, *pick("gated", (arrived, carried_in))),
            *pick("gated_ready", (joined_wide,)),
        )

        def mm(kind, left, left_at, right, right_at):
            if FL[kind]:
                return block_product(left, left_at, right, right_at)
            left = left if left_at is None else columns(left, left_at)
            right = right if right_at is None else columns(right, right_at)
            return left_dot(left, right)

        def part_gate(i, y):
            return mm("kernel", normed, 2 * planes[i] + y, gates, None)

        def part_up(i, y):
            return mm("kernel", normed, 2 * planes[i] + y, ups, None)

        def part_out(i, y):
            return mm("kernel_rec", both_gated, None, both_branch, 2 * i + y)

        def part_joined(i, y):
            return mm("kernel_rec", both_one, 2 * i + y, joined, None)

        def swap_far(value):
            return lax.ppermute(value, "seq", FAR_PAIRS)

        gate_sent = part_gate(1, later(1 - side, *pick("gate", (carry_sent,))))
        up_sent = part_up(1, later(1 - side, *pick("gate", (carry_sent,))))
        far_down = part_down(1, later(side, *pick("far_down", (carry_sent, carried_in)))) + down_got
        far_gate = part_gate(1, later(side, *pick("far_gate", (carried_in, joined_wide)))) + swap_y(gate_sent)
        far_up = part_up(1, later(side, *pick("far_up", (carried_in, joined_wide, far_gate)))) + swap_y(up_sent)
        far_down_got, far_gate_got, far_up_got = (
            swap_far(value) for value in (far_down, far_gate, far_up)
        )
        near_joined = near_whole(
            joined_wide, *pick("joined", (far_down_got, far_gate_got, far_up, far_down))
        )
        near_branch = near_columns(
            d_branch_wide, pick("near_branch", (joined_wide, far_up)), *pick("branch_ready", (near_joined,))
        )
        mine_joined = jnp.concatenate([d_input, d_pforget, d_rgate], axis=1)
        joined = jnp.concatenate([mine_joined, near_joined], axis=0)
        both_one = jnp.concatenate([pair_columns(normed_one), near_one], axis=0)
        both_branch = jnp.concatenate([pair_columns(d_branch), near_branch], axis=0)
        both_gated = jnp.concatenate([gated, near_gated], axis=0)

        joined_sent = part_joined(1, 1 - side)
        out_sent = part_out(1, later(1 - side, *pick("out", (joined_sent,))))
        far_joined = part_joined(1, later(side, *pick("far_joined", (far_up_got, far_gate_got)))) + swap_y(
            joined_sent
        )
        far_out = part_out(1, later(side, *pick("far_out", (far_joined,)))) + swap_y(out_sent)

        def finish(part, got, name):
            sent = part(0, later(1 - side, *pick("own_" + name, (up_sent, joined_sent, far_joined))))
            kept = part(0, later(side, *pick("end_" + name, (joined_sent, far_joined, far_out))))
            ends.append(sent)
            return kept + swap_y(sent) + got

        ends = [far_joined, far_out]
        grad_w_down = finish(part_down, far_down_got, "down")
        grad_w_gate = finish(part_gate, far_gate_got, "gate")
        grad_w_up = finish(part_up, far_up_got, "up")
        grad_joined = finish(part_joined, swap_far(far_joined), "joined")
        grad_w_out = finish(part_out, swap_far(far_out), "out")
        sends = ends[: FL["sends"]]
        grads = (
            grad_joined[:, :channels],
            grad_joined[:, channels : 2 * channels],
            grad_joined[:, 2 * channels :],
            grad_w_out,
            grad_w_gate,
            grad_w_up,
            grad_w_down,
        )

    rowsum = jnp.stack([sum(first_grad), sum(hat_grad)])
    rowsum = rowsum + swap_core(rowsum)
    pieces = jnp.concatenate(
        [
            rowsum.reshape(2, count, width // count).transpose(1, 0, 2).reshape(count, -1),
            grad_gnorm.reshape(count, -1),
            grad_bound.reshape(count, -1),
        ],
        axis=1,
    )
    if not fast:
        vectors = lax.psum_scatter(pieces, "seq", scatter_dimension=0, tiled=True)[0]
    elif FL["direct"]:
        pieces = after(pieces, *sends)
        vectors = lax.dynamic_index_in_dim(pieces, mine, 0, keepdims=False)
        for step in range(1, 8):
            piece = lax.dynamic_index_in_dim(pieces, jnp.bitwise_xor(mine, step), 0, keepdims=False)
            vectors += lax.ppermute(piece, "seq", [(i, i ^ step) for i in range(8)])
    else:
        pieces = after(pieces, *sends)
        for step in FL["steps"]:
            pieces = pieces + lax.ppermute(pieces, "seq", [(i, i ^ step) for i in range(8)])
        vectors = lax.dynamic_index_in_dim(pieces, mine, 0, keepdims=False)
    part, small = width // count, channels // count
    grad_attn, grad_mlp = vectors[:part], vectors[part : 2 * part]
    grad_gnorm = vectors[2 * part : 2 * part + small][None, :]
    grad_bound = vectors[2 * part + small :][None, :]

    return (
        mixed_out,
        grad_tokens,
        grad_attn,
        grads[0],
        grads[1],
        grads[2],
        grad_gnorm,
        grad_bound,
        grads[3],
        grad_mlp,
        grads[4],
        grads[5],
        grads[6],
    )


def solution(mesh):
    in_specs = (
        P("seq", None),
        P(),
        P(None, "mp"),
        P(None, "mp"),
        P(None, "mp"),
        P("mp"),
        P("mp"),
        P("mp", None),
        P(),
        P(None, "mp"),
        P(None, "mp"),
        P("mp", None),
        P("seq", None),
        P("seq", None),
    )
    out_specs = (
        P("seq", None),
        P("seq", None),
        P("seq"),
        P("seq", "mp"),
        P("seq", "mp"),
        P("seq", "mp"),
        P("mp", "seq"),
        P("mp", "seq"),
        P("mp", "seq"),
        P("seq"),
        P("seq", "mp"),
        P("seq", "mp"),
        P("mp", "seq"),
    )
    return jax.shard_map(
        per_device, mesh=mesh, in_specs=in_specs, out_specs=out_specs, check_vma=False
    )
```

time: 792 us -> 699 us (0.88)
  local copies, waits for them, and re-layouts: 110 us -> 38.6 us
  starting transfers between devices: 123 us -> 68.8 us
  waiting for transfers between devices: 321 us -> 349 us
  between operations: 3.25 us -> 15.1 us
  other arithmetic: 60.6 us -> 50.6 us
    ppermute x36 -> x24, starting transfers between devices: 92.3 us -> 34.9 us  [the longest x5 10.3 us: swap_far(): return lax.ppermute(value, 'seq', FAR_PAIRS)]
    ppermute x7 -> x10, waiting for transfers between devices: 60.9 us -> 97.5 us  [swap_y(): return lax.ppermute(value, 'seq', Y_PAIRS)]
    dynamic_slice x6 -> x4, local copies, waits for them, and re-layouts: 29.4 us -> 2.51 us  [the longest x2 2.29 us: pair_columns(): lax.dynamic_slice_in_dim(value, 2 * q * block, 2 * block, 1)]
    reshape x3 -> x2, local copies, waits for them, and re-layouts: 21.9 us -> 0.15 us  [the longest x1 0.08 us: per_device(): grad_bound.reshape(count, -1)]
    concatenate x10 -> x1, local copies, waits for them, and re-layouts: 21.3 us -> 1.12 us  [per_device(): jnp.concatenate(parts, axis=0)]
    unnamed x307 -> x352, local copies, waits for them, and re-layouts: 32.3 us -> 20.8 us
    ppermute x36 -> x24, waiting for transfers between devices: 255 us -> 245 us  [the longest x8 114 us: summed_half(): return (value + lax.ppermute(value, 'mp', X_PAIRS), value)]
    slice x9 -> x22, local copies, waits for them, and re-layouts: 2.85 us -> 12.9 us  [the longest x16 9.7 us: spark(): lax.slice(other, (0,) * other.ndim, (1,) * other.ndim)]
  transfers between devices with their start and end apart: 79 -> 71, of which waited for: 26 -> 26; matrix products, arithmetic and copies ran while one was open for 38% -> 32% of each run, Pallas kernels for 1% -> 2%
where the time goes in v2:
time: 699 us; the launch traced here: 692 us
  waiting for transfers between devices  349 us (50%)
  matrix products  159 us (23%)
  starting transfers between devices  68.8 us (10%)
  other arithmetic  50.6 us (7%)
  local copies, waits for them, and re-layouts  38.6 us (6%)
  between operations  15.1 us (2%)
  Pallas kernels  11.1 us (2%)
    ppermute x8, waiting for transfers between devices, summed_half(): return (value + lax.ppermute(value, 'mp', X_PAIRS), value)  114 us
    ppermute x5, waiting for transfers between devices, swap_far(): return lax.ppermute(value, 'seq', FAR_PAIRS)  98.1 us
    ppermute x10, waiting for transfers between devices, swap_y(): return lax.ppermute(value, 'seq', Y_PAIRS)  97.5 us
    dot_general x19, matrix products, dot(): return jnp.dot(left, right, preferred_element_type=F32)  55.1 us
    dot_general x20, matrix products, left_dot(): lax.dot_general(left, right, (((0,), (0,)), ((), ())), preferred_element_...  52.8 us
    dot_general x24, matrix products, right_dot(): lax.dot_general(left, right, (((1,), (1,)), ((), ())), preferred_element_...  51.4 us
    ppermute x6, waiting for transfers between devices, near_rows(): own = after(lax.ppermute(value, 'seq', Z_PAIRS), *ready)  26.4 us
    unnamed x352, local copies, waits for them, and re-layouts  20.8 us
  transfers between devices with their start and end apart: 71, of which 26 were waited for; matrix products, arithmetic and copies ran while one was open for 32% of the time, Pallas kernels for 2%

profile of v2, /device:TPU:0, one launch (start us, length us, event | category | flops | bytes accessed | tf_op | source)
XLA Modules:
  0.0 692.0 jit_solution(2283802208010582862)
XLA Ops:
  3.1 3.7 fusion.1
  8.0 3.0 collective-permute-start.48
  11.4 4.0 fusion.32
  36.1 4.4 collective-permute-start.5
  41.8 2.9 collective-permute-start.3
  63.2 5.5 fusion.10
  72.4 14.1 %collective-permute-done.9 = f32[128,2048]{1,0:T(8,128)S(1)} collective-permute-done((f32[128,2048]{1,0:T(8,128)S(1)}, f32[128,2048]{1,0:T(8,128)S(1)}, u32[]{:S(2)}, u32[]{:S(2)}) %collective-permute-start.9) | collective-permute-done | bytes 1048608 | tf_op jit(solution)/shard_map/ppermute | solution.py:298
  88.0 25.9 %collective-permute-done.15 = f32[160,2048]{1,0:T(8,128)S(1)} collective-permute-done((f32[160,2048]{1,0:T(8,128)S(1)}, f32[160,2048]{1,0:T(8,128)S(1)}, u32[]{:S(2)}, u32[]{:S(2)}) %collective-permute-start.15) | collective-permute-done | bytes 1310752 | tf_op jit(solution)/shard_map/ppermute | solution.py:298
  122.3 4.6 multiply_convert_fusion.11
  131.9 2.9 convolution_add_fusion.18
  143.3 5.2 multiply_convert_fusion.6
  150.6 3.1 convolution_add_fusion.22
  161.7 3.4 fusion.187
  165.2 17.8 %collective-permute-done.28.refs_0_ = f32[160,2048]{1,0:T(8,128)S(1)} collective-permute-done((f32[160,2048]{1,0:T(8,128)S(1)}, f32[160,2048]{1,0:T(8,128)S(1)}, u32[]{:S(2)}, u32[]{:S(2)}) %collective-permute-start.28) | collective-permute-done | bytes 1310752 | tf_op jit(solution)/shard_map/ppermute | solution.py:353
  183.5 3.2 fusion.9
  190.3 3.4 multiply_convert_fusion.8
  199.2 4.5 multiply_convert_fusion.2
  207.0 5.9 collective-permute-done.12
  213.7 26.3 %collective-permute-done.18 = f32[160,2048]{1,0:T(8,128)S(1)} collective-permute-done((f32[160,2048]{1,0:T(8,128)S(1)}, f32[160,2048]{1,0:T(8,128)S(1)}, u32[]{:S(2)}, u32[]{:S(2)}) %collective-permute-start.18) | collective-permute-done | bytes 1310752 | tf_op jit(solution)/shard_map/ppermute | solution.py:298
  251.6 3.5 fusion.170
  267.3 5.1 fusion.84
  272.4 4.7 fusion.93
  282.6 4.5 fusion.68
  287.1 3.5 convolution_add_fusion
  290.7 3.5 fusion.70
  327.5 4.1 convolution_add_fusion.17
  336.0 4.3 convolution_add_fusion.21
  343.6 6.2 collective-permute-done.53.refs_1_
  351.5 9.3 %collective-permute-done.64 = f32[256,1408]{1,0:T(8,128)S(1)} collective-permute-done((f32[256,1408]{1,0:T(8,128)}, f32[256,1408]{1,0:T(8,128)S(1)}, u32[]{:S(2)}, u32[]{:S(2)}) %collective-permute-start.64) | collective-permute-done | bytes 1441824 | tf_op jit(solution)/shard_map/ppermute | solution.py:334
  360.8 3.4 convolution_add_fusion.4
  364.2 26.3 %collective-permute-done.67 = f32[256,1408]{1,0:T(8,128)S(1)} collective-permute-done((f32[256,1408]{1,0:T(8,128)S(1)}, f32[256,1408]{1,0:T(8,128)S(1)}, u32[]{:S(2)}, u32[]{:S(2)}) %collective-permute-start.67) | collective-permute-done | bytes 1441824 | tf_op jit(solution)/shard_map/ppermute | solution.py:334
  391.8 3.4 convolution_add_fusion.2
  396.1 3.6 collective-permute-start.65
  404.6 17.5 %collective-permute-done.26 = f32[160,2048]{1,0:T(8,128)S(1)} collective-permute-done((f32[160,2048]{1,0:T(8,128)S(1)}, f32[160,2048]{1,0:T(8,128)S(1)}, u32[]{:S(2)}, u32[]{:S(2)}) %collective-permute-start.26) | collective-permute-done | bytes 1310752 | tf_op jit(solution)/shard_map/ppermute | solution.py:298
  423.8 24.3 %collective-permute-done.45 = f32[160,2048]{1,0:T(8,128)S(1)} collective-permute-done((f32[160,2048]{1,0:T(8,128)S(1)}, f32[160,2048]{1,0:T(8,128)S(1)}, u32[]{:S(2)}, u32[]{:S(2)}) %collective-permute-start.45) | collective-permute-done | bytes 1310752 | tf_op jit(solution)/shard_map/ppermute | solution.py:298
  454.1 4.5 collective-permute-done.50.refs_1_
  464.9 3.5 collective-permute-start.68
  468.5 46.5 %collective-permute-done.62 = f32[512,256]{1,0:T(8,128)S(1)} collective-permute-done((f32[512,256]{1,0:T(8,128)S(1)}, f32[512,256]{1,0:T(8,128)S(1)}, u32[]{:S(2)}, u32[]{:S(2)}) %collective-permute-start.62) | collective-permute-done | bytes 524320 | tf_op jit(solution)/shard_map/ppermute | solution.py:616
  524.5 4.2 fusion.74
  531.3 3.9 fusion.76
  562.2 18.4 %collective-permute-done.63 = f32[256,1408]{1,0:T(8,128)} collective-permute-done((f32[256,1408]{1,0:T(8,128)}, f32[256,1408]{1,0:T(8,128)}, u32[]{:S(2)}, u32[]{:S(2)}) %collective-permute-start.63) | collective-permute-done | bytes 1441824 | tf_op jit(solution)/shard_map/ppermute | solution.py:334
  580.7 4.6 fusion.2
  585.3 26.3 %collective-permute-done.66 = f32[256,1408]{1,0:T(8,128)} collective-permute-done((f32[256,1408]{1,0:T(8,128)}, f32[256,1408]{1,0:T(8,128)}, u32[]{:S(2)}, u32[]{:S(2)}) %collective-permute-start.66) | collective-permute-done | bytes 1441824 | tf_op jit(solution)/shard_map/ppermute | solution.py:334
  611.6 4.4 fusion.3
  616.0 39.0 %collective-permute-done.70 = f32[1408,256]{1,0:T(8,128)S(1)} collective-permute-done((f32[1408,256]{1,0:T(8,128)}, f32[1408,256]{1,0:T(8,128)S(1)}, u32[]{:S(2)}, u32[]{:S(2)}) %collective-permute-start.70) | collective-permute-done | bytes 1441824 | tf_op jit(solution)/shard_map/ppermute | solution.py:616
  655.0 3.3 fusion.4
  658.4 17.0 %collective-permute-done.59 = f32[256,1536]{1,0:T(8,128)S(1)} collective-permute-done((f32[256,1536]{1,0:T(8,128)}, f32[256,1536]{1,0:T(8,128)S(1)}, u32[]{:S(2)}, u32[]{:S(2)}) %collective-permute-start.59) | collective-permute-done | bytes 1572896 | tf_op jit(solution)/shard_map/ppermute | solution.py:334
  675.3 12.6 %collective-permute-done.60 = f32[256,1536]{1,0:T(8,128)S(1)} collective-permute-done((f32[256,1536]{1,0:T(8,128)}, f32[256,1536]{1,0:T(8,128)S(1)}, u32[]{:S(2)}, u32[]{:S(2)}) %collective-permute-start.60) | collective-permute-done | bytes 1572896 | tf_op jit(solution)/shard_map/ppermute | solution.py:616
  (652 shorter events, 217.6 us)
Async XLA Ops:
  8.0 62.8 %collective-permute-start.48 = (f32[288,1024]{1,0:T(8,128)}, f32[288,1024]{1,0:T(8,128)}, u32[]{:S(2)}, u32[]{:S(2)}) collective-permute-start(f32[288,1024]{1,0:T(8,128)} %pad_maximum_fusion.14), channel_id=1, source_target_pairs={{0,8},{4,12},{8,0},{12,4},{16,24},{20,28},{24,16},{28,20},{1,9},{5... | collective-permute-start | bytes 3538952 | tf_op jit(solution)/shard_map/ppermute | solution.py:353
  53.9 63.0 %collective-permute-start.34 = (f32[128,2048]{1,0:T(8,128)}, f32[128,2048]{1,0:T(8,128)S(1)}, u32[]{:S(2)}, u32[]{:S(2)}) collective-permute-start(f32[128,2048]{1,0:T(8,128)} %get-tuple-element.47), channel_id=1, source_target_pairs={{0,8},{4,12},{8,0},{12,4},{16,24},{20,28},{24,16},{28,20},{1,9},{5... | collective-permute-start | bytes 3145736 | tf_op jit(solution)/shard_map/ppermute | solution.py:353
  57.6 59.7 %collective-permute-start.32 = (f32[160,2048]{1,0:T(8,128)S(1)}, f32[160,2048]{1,0:T(8,128)S(1)}, u32[]{:S(2)}, u32[]{:S(2)}) collective-permute-start(f32[160,2048]{1,0:T(8,128)S(1)} %get-tuple-element.49), channel_id=1, source_target_pairs={{0,8},{4,12},{8,0},{12,4},{16,24},{20,28},{24,16},{28,20},{1,9},{5... | collective-permute-start | bytes 3932168 | tf_op jit(solution)/shard_map/ppermute | solution.py:353
  60.5 26.1 %collective-permute-start.9 = (f32[128,2048]{1,0:T(8,128)S(1)}, f32[128,2048]{1,0:T(8,128)S(1)}, u32[]{:S(2)}, u32[]{:S(2)}) collective-permute-start(f32[128,2048]{1,0:T(8,128)S(1)} %convolution_add_fusion.20), channel_id=1, source_target_pairs={{0,2},{1,3},{2,0},{3,1},{4,6},{5,7},{6,4},{7,5},{8,10},{9,11},{10,... | collective-permute-start | bytes 3145736 | tf_op jit(solution)/shard_map/ppermute | solution.py:298
  61.8 52.1 %collective-permute-start.15 = (f32[160,2048]{1,0:T(8,128)S(1)}, f32[160,2048]{1,0:T(8,128)S(1)}, u32[]{:S(2)}, u32[]{:S(2)}) collective-permute-start(f32[160,2048]{1,0:T(8,128)S(1)} %convolution_add_fusion.12), channel_id=1, source_target_pairs={{0,2},{1,3},{2,0},{3,1},{4,6},{5,7},{6,4},{7,5},{8,10},{9,11},{10,... | collective-permute-start | bytes 3932168 | tf_op jit(solution)/shard_map/ppermute | solution.py:298
  70.9 249.8 %collective-permute-start.52 = (f32[576,512]{1,0:T(8,128)}, f32[576,512]{1,0:T(8,128)}, u32[]{:S(2)}, u32[]{:S(2)}) collective-permute-start(f32[576,512]{1,0:T(8,128)} %pad_maximum_fusion.15), channel_id=1, source_target_pairs={{0,8},{4,12},{8,0},{12,4},{16,24},{20,28},{24,16},{28,20},{1,9},{5... | collective-permute-start | bytes 3538952 | tf_op jit(solution)/shard_map/ppermute | solution.py:578
  86.6 228.1 %collective-permute-start.49 = (f32[288,1024]{1,0:T(8,128)}, f32[288,1024]{1,0:T(8,128)}, u32[]{:S(2)}, u32[]{:S(2)}) collective-permute-start(f32[288,1024]{1,0:T(8,128)} %collective-permute-done.48.refs_1_), channel_id=1, source_target_pairs={{0,1},{1,0},{2,3},{3,2},{4,5},{5,4},{6,7},{7,6},{8,9},{9,8},{10,11... | collective-permute-start | bytes 3538952 | tf_op jit(solution)/shard_map/ppermute | solution.py:331
  116.9 39.1 %collective-permute-start.30 = (f32[128,2048]{1,0:T(8,128)S(1)}, f32[128,2048]{1,0:T(8,128)S(1)}, u32[]{:S(2)}, u32[]{:S(2)}) collective-permute-start(f32[128,2048]{1,0:T(8,128)S(1)} %get-tuple-element.106), channel_id=1, source_target_pairs={{0,8},{4,12},{8,0},{12,4},{16,24},{20,28},{24,16},{28,20},{1,9},{5... | collective-permute-start | bytes 3145736 | tf_op jit(solution)/shard_map/ppermute | solution.py:353
  117.4 22.6 %collective-permute-start.16 = (f32[160,2048]{1,0:T(8,128)S(1)}, f32[160,2048]{1,0:T(8,128)S(1)}, u32[]{:S(2)}, u32[]{:S(2)}) collective-permute-start(f32[160,2048]{1,0:T(8,128)S(1)} %get-tuple-element.110), channel_id=1, source_target_pairs={{0,1},{1,0},{2,3},{3,2},{4,5},{5,4},{6,7},{7,6},{8,9},{9,8},{10,11... | collective-permute-start | bytes 3932168 | tf_op jit(solution)/shard_map/ppermute | solution.py:331
  117.8 17.0 %collective-permute-start.35 = (f32[128,2048]{1,0:T(8,128)S(1)}, f32[128,2048]{1,0:T(8,128)S(1)}, u32[]{:S(2)}, u32[]{:S(2)}) collective-permute-start(f32[128,2048]{1,0:T(8,128)S(1)} %broadcast_add_fusion.1.refs_1_), channel_id=1, source_target_pairs={{0,1},{1,0},{2,3},{3,2},{4,5},{5,4},{6,7},{7,6},{8,9},{9,8},{10,11... | collective-permute-start | bytes 3145736 | tf_op jit(solution)/shard_map/ppermute | solution.py:331
  134.8 48.2 %collective-permute-start.28 = (f32[160,2048]{1,0:T(8,128)S(1)}, f32[160,2048]{1,0:T(8,128)S(1)}, u32[]{:S(2)}, u32[]{:S(2)}) collective-permute-start(f32[160,2048]{1,0:T(8,128)S(1)} %get-tuple-element.110), channel_id=1, source_target_pairs={{0,8},{4,12},{8,0},{12,4},{16,24},{20,28},{24,16},{28,20},{1,9},{5... | collective-permute-start | bytes 3932168 | tf_op jit(solution)/shard_map/ppermute | solution.py:353
  140.0 16.0 %collective-permute-start.33 = (f32[160,2048]{1,0:T(8,128)S(1)}, f32[160,2048]{1,0:T(8,128)S(1)}, u32[]{:S(2)}, u32[]{:S(2)}) collective-permute-start(f32[160,2048]{1,0:T(8,128)S(1)} %broadcast_add_fusion.refs_1_), channel_id=1, source_target_pairs={{0,1},{1,0},{2,3},{3,2},{4,5},{5,4},{6,7},{7,6},{8,9},{9,8},{10,11... | collective-permute-start | bytes 3932168 | tf_op jit(solution)/shard_map/ppermute | solution.py:331
  156.0 27.0 %collective-permute-start.11 = (f32[128,2048]{1,0:T(8,128)}, f32[128,2048]{1,0:T(8,128)}, u32[]{:S(2)}, u32[]{:S(2)}) collective-permute-start(f32[128,2048]{1,0:T(8,128)} %convolution_add_fusion.18), channel_id=1, source_target_pairs={{0,1},{1,0},{2,3},{3,2},{4,5},{5,4},{6,7},{7,6},{8,9},{9,8},{10,11... | collective-permute-start | bytes 3145736 | tf_op jit(solution)/shard_map/ppermute | solution.py:297
  156.0 30.7 %collective-permute-start.31 = (f32[128,2048]{1,0:T(8,128)S(1)}, f32[128,2048]{1,0:T(8,128)S(1)}, u32[]{:S(2)}, u32[]{:S(2)}) collective-permute-start(f32[128,2048]{1,0:T(8,128)S(1)} %collective-permute-done.30.refs_0_), channel_id=1, source_target_pairs={{0,1},{1,0},{2,3},{3,2},{4,5},{5,4},{6,7},{7,6},{8,9},{9,8},{10,11... | collective-permute-start | bytes 3145736 | tf_op jit(solution)/shard_map/ppermute | solution.py:331
  186.8 26.1 %collective-permute-start.12 = (f32[128,2048]{1,0:T(8,128)S(1)}, f32[128,2048]{1,0:T(8,128)S(1)}, u32[]{:S(2)}, u32[]{:S(2)}) collective-permute-start(f32[128,2048]{1,0:T(8,128)S(1)} %fusion.9), channel_id=1, source_target_pairs={{0,2},{1,3},{2,0},{3,1},{4,6},{5,7},{6,4},{7,5},{8,10},{9,11},{10,... | collective-permute-start | bytes 3145736 | tf_op jit(solution)/shard_map/ppermute | solution.py:298
  198.4 41.6 %collective-permute-start.18 = (f32[160,2048]{1,0:T(8,128)S(1)}, f32[160,2048]{1,0:T(8,128)S(1)}, u32[]{:S(2)}, u32[]{:S(2)}) collective-permute-start(f32[160,2048]{1,0:T(8,128)S(1)} %fusion.8), channel_id=1, source_target_pairs={{0,2},{1,3},{2,0},{3,1},{4,6},{5,7},{6,4},{7,5},{8,10},{9,11},{10,... | collective-permute-start | bytes 3932168 | tf_op jit(solution)/shard_map/ppermute | solution.py:298
  206.3 40.0 %collective-permute-start.36 = (f32[1408,256]{1,0:T(8,128)S(1)}, f32[1408,256]{1,0:T(8,128)S(1)}, u32[]{:S(2)}, u32[]{:S(2)}) collective-permute-start(f32[1408,256]{1,0:T(8,128)S(1)} %fusion.66), channel_id=1, source_target_pairs={{0,4},{4,0},{8,12},{12,8},{16,20},{20,16},{24,28},{28,24},{1,5},{5... | collective-permute-start | bytes 4325384 | tf_op jit(solution)/shard_map/ppermute | solution.py:334
  213.6 31.7 %collective-permute-start.13 = (f32[128,2048]{1,0:T(8,128)S(1)}, f32[128,2048]{1,0:T(8,128)S(1)}, u32[]{:S(2)}, u32[]{:S(2)}) collective-permute-start(f32[128,2048]{1,0:T(8,128)S(1)} %subtract_multiply_fusion.3), channel_id=1, source_target_pairs={{0,1},{1,0},{2,3},{3,2},{4,5},{5,4},{6,7},{7,6},{8,9},{9,8},{10,11... | collective-permute-start | bytes 3145736 | tf_op jit(solution)/shard_map/ppermute | solution.py:331
  278.4 15.8 %collective-permute-start.40 = (f32[2,512]{1,0:T(2,128)S(1)}, f32[2,512]{1,0:T(2,128)S(1)}, u32[]{:S(2)}, u32[]{:S(2)}) collective-permute-start(f32[2,512]{1,0:T(2,128)S(1)} %pad_maximum_fusion.21), channel_id=1, source_target_pairs={{24,0},{28,4},{25,1},{29,5},{26,2},{30,6},{27,3},{31,7}} | collective-permute-start | bytes 12296 | tf_op jit(solution)/shard_map/ppermute | solution.py:285
  279.7 14.5 %collective-permute-start.39 = (f32[2,512]{1,0:T(2,128)S(1)}, f32[2,512]{1,0:T(2,128)S(1)}, u32[]{:S(2)}, u32[]{:S(2)}) collective-permute-start(f32[2,512]{1,0:T(2,128)S(1)} %pad_maximum_fusion.21), channel_id=1, source_target_pairs={{16,0},{20,4},{24,8},{28,12},{17,1},{21,5},{25,9},{29,13},{18,2},{... | collective-permute-start | bytes 12296 | tf_op jit(solution)/shard_map/ppermute | solution.py:285
  294.3 31.7 %collective-permute-start.22 = (f32[128,2048]{1,0:T(8,128)}, f32[128,2048]{1,0:T(8,128)}, u32[]{:S(2)}, u32[]{:S(2)}) collective-permute-start(f32[128,2048]{1,0:T(8,128)} %fusion.93), channel_id=1, source_target_pairs={{0,1},{1,0},{2,3},{3,2},{4,5},{5,4},{6,7},{7,6},{8,9},{9,8},{10,11... | collective-permute-start | bytes 3145736 | tf_op jit(solution)/shard_map/ppermute | solution.py:297
  294.3 40.3 %collective-permute-start.25 = (f32[160,2048]{1,0:T(8,128)}, f32[160,2048]{1,0:T(8,128)}, u32[]{:S(2)}, u32[]{:S(2)}) collective-permute-start(f32[160,2048]{1,0:T(8,128)} %fusion.84), channel_id=1, source_target_pairs={{0,1},{1,0},{2,3},{3,2},{4,5},{5,4},{6,7},{7,6},{8,9},{9,8},{10,11... | collective-permute-start | bytes 3932168 | tf_op jit(solution)/shard_map/ppermute | solution.py:297
  304.9 26.7 %collective-permute-start.41 = (f32[128,2048]{1,0:T(8,128)}, f32[128,2048]{1,0:T(8,128)}, u32[]{:S(2)}, u32[]{:S(2)}) collective-permute-start(f32[128,2048]{1,0:T(8,128)} %convolution_add_fusion.13), channel_id=1, source_target_pairs={{0,1},{1,0},{2,3},{3,2},{4,5},{5,4},{6,7},{7,6},{8,9},{9,8},{10,11... | collective-permute-start | bytes 3145736 | tf_op jit(solution)/shard_map/ppermute | solution.py:297
  314.7 25.7 %collective-permute-start.44 = (f32[160,2048]{1,0:T(8,128)}, f32[160,2048]{1,0:T(8,128)}, u32[]{:S(2)}, u32[]{:S(2)}) collective-permute-start(f32[160,2048]{1,0:T(8,128)} %convolution_add_fusion.8), channel_id=1, source_target_pairs={{0,1},{1,0},{2,3},{3,2},{4,5},{5,4},{6,7},{7,6},{8,9},{9,8},{10,11... | collective-permute-start | bytes 3932168 | tf_op jit(solution)/shard_map/ppermute | solution.py:297
  320.6 29.1 %collective-permute-start.53 = (f32[288,1024]{1,0:T(8,128)}, f32[288,1024]{1,0:T(8,128)S(1)}, u32[]{:S(2)}, u32[]{:S(2)}) collective-permute-start(f32[288,1024]{1,0:T(8,128)} %pad_maximum_fusion.17), channel_id=1, source_target_pairs={{0,8},{4,12},{8,0},{12,4},{16,24},{20,28},{24,16},{28,20},{1,9},{5... | collective-permute-start | bytes 3538952 | tf_op jit(solution)/shard_map/ppermute | solution.py:353
  326.0 34.8 %collective-permute-start.64 = (f32[256,1408]{1,0:T(8,128)}, f32[256,1408]{1,0:T(8,128)S(1)}, u32[]{:S(2)}, u32[]{:S(2)}) collective-permute-start(f32[256,1408]{1,0:T(8,128)} %fusion.70), channel_id=1, source_target_pairs={{0,4},{4,0},{8,12},{12,8},{16,20},{20,16},{24,28},{28,24},{1,5},{5... | collective-permute-start | bytes 4325384 | tf_op jit(solution)/shard_map/ppermute | solution.py:334
  331.6 58.8 %collective-permute-start.67 = (f32[256,1408]{1,0:T(8,128)S(1)}, f32[256,1408]{1,0:T(8,128)S(1)}, u32[]{:S(2)}, u32[]{:S(2)}) collective-permute-start(f32[256,1408]{1,0:T(8,128)S(1)} %copy-done.143), channel_id=1, source_target_pairs={{0,4},{4,0},{8,12},{12,8},{16,20},{20,16},{24,28},{28,24},{1,5},{5... | collective-permute-start | bytes 4325384 | tf_op jit(solution)/shard_map/ppermute | solution.py:334
  334.6 60.5 %collective-permute-start.23 = (f32[128,2048]{1,0:T(8,128)S(1)}, f32[128,2048]{1,0:T(8,128)S(1)}, u32[]{:S(2)}, u32[]{:S(2)}) collective-permute-start(f32[128,2048]{1,0:T(8,128)S(1)} %convolution_add_fusion.17), channel_id=1, source_target_pairs={{0,2},{1,3},{2,0},{3,1},{4,6},{5,7},{6,4},{7,5},{8,10},{9,11},{10,... | collective-permute-start | bytes 3145736 | tf_op jit(solution)/shard_map/ppermute | solution.py:298
  340.3 55.7 %collective-permute-start.42 = (f32[128,2048]{1,0:T(8,128)S(1)}, f32[128,2048]{1,0:T(8,128)S(1)}, u32[]{:S(2)}, u32[]{:S(2)}) collective-permute-start(f32[128,2048]{1,0:T(8,128)S(1)} %fusion.7), channel_id=1, source_target_pairs={{0,2},{1,3},{2,0},{3,1},{4,6},{5,7},{6,4},{7,5},{8,10},{9,11},{10,... | collective-permute-start | bytes 3145736 | tf_op jit(solution)/shard_map/ppermute | solution.py:298
  349.7 108.8 %collective-permute-start.50 = (f32[576,1536]{1,0:T(8,128)S(1)}, f32[576,1536]{1,0:T(8,128)S(1)}, u32[]{:S(2)}, u32[]{:S(2)}) collective-permute-start(f32[576,1536]{1,0:T(8,128)S(1)} %copy-done.65), channel_id=1, source_target_pairs={{0,8},{4,12},{8,0},{12,4},{16,24},{20,28},{24,16},{28,20},{1,9},{5... | collective-permute-start | bytes 10616840 | tf_op jit(solution)/shard_map/ppermute | solution.py:578
  360.8 39.7 %collective-permute-start.54 = (f32[288,1024]{1,0:T(8,128)S(1)}, f32[288,1024]{1,0:T(8,128)S(1)}, u32[]{:S(2)}, u32[]{:S(2)}) collective-permute-start(f32[288,1024]{1,0:T(8,128)S(1)} %collective-permute-done.53.refs_1_), channel_id=1, source_target_pairs={{0,1},{1,0},{2,3},{3,2},{4,5},{5,4},{6,7},{7,6},{8,9},{9,8},{10,11... | collective-permute-start | bytes 3538952 | tf_op jit(solution)/shard_map/ppermute | solution.py:331
  390.4 31.7 %collective-permute-start.26 = (f32[160,2048]{1,0:T(8,128)S(1)}, f32[160,2048]{1,0:T(8,128)S(1)}, u32[]{:S(2)}, u32[]{:S(2)}) collective-permute-start(f32[160,2048]{1,0:T(8,128)S(1)} %convolution_add_fusion.21), channel_id=1, source_target_pairs={{0,2},{1,3},{2,0},{3,1},{4,6},{5,7},{6,4},{7,5},{8,10},{9,11},{10,... | collective-permute-start | bytes 3932168 | tf_op jit(solution)/shard_map/ppermute | solution.py:298
  395.1 52.9 %collective-permute-start.45 = (f32[160,2048]{1,0:T(8,128)S(1)}, f32[160,2048]{1,0:T(8,128)S(1)}, u32[]{:S(2)}, u32[]{:S(2)}) collective-permute-start(f32[160,2048]{1,0:T(8,128)S(1)} %fusion.6), channel_id=1, source_target_pairs={{0,2},{1,3},{2,0},{3,1},{4,6},{5,7},{6,4},{7,5},{8,10},{9,11},{10,... | collective-permute-start | bytes 3932168 | tf_op jit(solution)/shard_map/ppermute | solution.py:298
  396.1 162.8 %collective-permute-start.65 = (f32[256,1408]{1,0:T(8,128)}, f32[256,1408]{1,0:T(8,128)}, u32[]{:S(2)}, u32[]{:S(2)}) collective-permute-start(f32[256,1408]{1,0:T(8,128)} %convolution_add_fusion.4), channel_id=1, source_target_pairs={{0,16},{4,20},{8,24},{12,28},{16,0},{20,4},{24,8},{28,12},{1,17},{... | collective-permute-start | bytes 4325384 | tf_op jit(solution)/shard_map/ppermute | solution.py:616
  400.5 52.2 %collective-permute-start.24 = (f32[128,2048]{1,0:T(8,128)S(1)}, f32[128,2048]{1,0:T(8,128)S(1)}, u32[]{:S(2)}, u32[]{:S(2)}) collective-permute-start(f32[128,2048]{1,0:T(8,128)S(1)} %add.776), channel_id=1, source_target_pairs={{0,1},{1,0},{2,3},{3,2},{4,5},{5,4},{6,7},{7,6},{8,9},{9,8},{10,11... | collective-permute-start | bytes 3145736 | tf_op jit(solution)/shard_map/ppermute | solution.py:331
  422.1 28.0 %collective-permute-start.55 = (f32[512,256]{1,0:T(8,128)S(1)}, f32[512,256]{1,0:T(8,128)S(1)}, u32[]{:S(2)}, u32[]{:S(2)}) collective-permute-start(f32[512,256]{1,0:T(8,128)S(1)} %fusion.60), channel_id=1, source_target_pairs={{0,4},{4,0},{8,12},{12,8},{16,20},{20,16},{24,28},{28,24},{1,5},{5... | collective-permute-start | bytes 1572872 | tf_op jit(solution)/shard_map/ppermute | solution.py:334
  450.1 14.8 %collective-permute-start.61 = (f32[512,256]{1,0:T(8,128)S(1)}, f32[512,256]{1,0:T(8,128)S(1)}, u32[]{:S(2)}, u32[]{:S(2)}) collective-permute-start(f32[512,256]{1,0:T(8,128)S(1)} %fusion.54), channel_id=1, source_target_pairs={{0,4},{4,0},{8,12},{12,8},{16,20},{20,16},{24,28},{28,24},{1,5},{5... | collective-permute-start | bytes 1572872 | tf_op jit(solution)/shard_map/ppermute | solution.py:334
  452.7 66.5 %collective-permute-start.27 = (f32[160,2048]{1,0:T(8,128)S(1)}, f32[160,2048]{1,0:T(8,128)S(1)}, u32[]{:S(2)}, u32[]{:S(2)}) collective-permute-start(f32[160,2048]{1,0:T(8,128)S(1)} %add.783), channel_id=1, source_target_pairs={{0,1},{1,0},{2,3},{3,2},{4,5},{5,4},{6,7},{7,6},{8,9},{9,8},{10,11... | collective-permute-start | bytes 3932168 | tf_op jit(solution)/shard_map/ppermute | solution.py:331
  458.6 56.4 %collective-permute-start.62 = (f32[512,256]{1,0:T(8,128)S(1)}, f32[512,256]{1,0:T(8,128)S(1)}, u32[]{:S(2)}, u32[]{:S(2)}) collective-permute-start(f32[512,256]{1,0:T(8,128)S(1)} %convolution_add_fusion.25), channel_id=1, source_target_pairs={{0,16},{4,20},{8,24},{12,28},{16,0},{20,4},{24,8},{28,12},{1,17},{... | collective-permute-start | bytes 1572872 | tf_op jit(solution)/shard_map/ppermute | solution.py:616
  461.6 59.3 %collective-permute-start.51 = (f32[256,1536]{1,0:T(8,128)S(1)}, f32[256,1536]{1,0:T(8,128)S(1)}, u32[]{:S(2)}, u32[]{:S(2)}) collective-permute-start(f32[256,1536]{1,0:T(8,128)S(1)} %fusion.63), channel_id=1, source_target_pairs={{0,4},{4,0},{8,12},{12,8},{16,20},{20,16},{24,28},{28,24},{1,5},{5... | collective-permute-start | bytes 4718600 | tf_op jit(solution)/shard_map/ppermute | solution.py:334
  464.9 95.2 %collective-permute-start.68 = (f32[256,1408]{1,0:T(8,128)}, f32[256,1408]{1,0:T(8,128)}, u32[]{:S(2)}, u32[]{:S(2)}) collective-permute-start(f32[256,1408]{1,0:T(8,128)} %convolution_add_fusion.2), channel_id=1, source_target_pairs={{0,16},{4,20},{8,24},{12,28},{16,0},{20,4},{24,8},{28,12},{1,17},{... | collective-permute-start | bytes 4325384 | tf_op jit(solution)/shard_map/ppermute | solution.py:616
  515.0 33.0 %collective-permute-start.46 = (f32[160,2048]{1,0:T(8,128)S(1)}, f32[160,2048]{1,0:T(8,128)}, u32[]{:S(2)}, u32[]{:S(2)}) collective-permute-start(f32[160,2048]{1,0:T(8,128)S(1)} %fusion.35), channel_id=1, source_target_pairs={{0,1},{1,0},{2,3},{3,2},{4,5},{5,4},{6,7},{7,6},{8,9},{9,8},{10,11... | collective-permute-start | bytes 3932168 | tf_op jit(solution)/shard_map/ppermute | solution.py:331
  545.9 34.7 %collective-permute-start.63 = (f32[256,1408]{1,0:T(8,128)}, f32[256,1408]{1,0:T(8,128)}, u32[]{:S(2)}, u32[]{:S(2)}) collective-permute-start(f32[256,1408]{1,0:T(8,128)} %fusion.76), channel_id=1, source_target_pairs={{0,4},{4,0},{8,12},{12,8},{16,20},{20,16},{24,28},{28,24},{1,5},{5... | collective-permute-start | bytes 4325384 | tf_op jit(solution)/shard_map/ppermute | solution.py:334
  546.5 65.1 %collective-permute-start.66 = (f32[256,1408]{1,0:T(8,128)}, f32[256,1408]{1,0:T(8,128)}, u32[]{:S(2)}, u32[]{:S(2)}) collective-permute-start(f32[256,1408]{1,0:T(8,128)} %fusion.74), channel_id=1, source_target_pairs={{0,4},{4,0},{8,12},{12,8},{16,20},{20,16},{24,28},{28,24},{1,5},{5... | collective-permute-start | bytes 4325384 | tf_op jit(solution)/shard_map/ppermute | solution.py:334
  556.5 98.5 %collective-permute-start.70 = (f32[1408,256]{1,0:T(8,128)}, f32[1408,256]{1,0:T(8,128)S(1)}, u32[]{:S(2)}, u32[]{:S(2)}) collective-permute-start(f32[1408,256]{1,0:T(8,128)} %convolution_add_fusion), channel_id=1, source_target_pairs={{0,16},{4,20},{8,24},{12,28},{16,0},{20,4},{24,8},{28,12},{1,17},{... | collective-permute-start | bytes 4325384 | tf_op jit(solution)/shard_map/ppermute | solution.py:616
  558.9 96.1 %collective-permute-start.69 = (f32[1408,256]{1,0:T(8,128)}, f32[1408,256]{1,0:T(8,128)S(1)}, u32[]{:S(2)}, u32[]{:S(2)}) collective-permute-start(f32[1408,256]{1,0:T(8,128)} %copy-done.144), channel_id=1, source_target_pairs={{0,4},{4,0},{8,12},{12,8},{16,20},{20,16},{24,28},{28,24},{1,5},{5... | collective-permute-start | bytes 4325384 | tf_op jit(solution)/shard_map/ppermute | solution.py:334
  560.2 115.2 %collective-permute-start.59 = (f32[256,1536]{1,0:T(8,128)}, f32[256,1536]{1,0:T(8,128)S(1)}, u32[]{:S(2)}, u32[]{:S(2)}) collective-permute-start(f32[256,1536]{1,0:T(8,128)} %copy-done.139), channel_id=1, source_target_pairs={{0,4},{4,0},{8,12},{12,8},{16,20},{20,16},{24,28},{28,24},{1,5},{5... | collective-permute-start | bytes 4718600 | tf_op jit(solution)/shard_map/ppermute | solution.py:334
  580.7 107.3 %collective-permute-start.60 = (f32[256,1536]{1,0:T(8,128)}, f32[256,1536]{1,0:T(8,128)S(1)}, u32[]{:S(2)}, u32[]{:S(2)}) collective-permute-start(f32[256,1536]{1,0:T(8,128)} %copy-done.140), channel_id=1, source_target_pairs={{0,16},{4,20},{8,24},{12,28},{16,0},{20,4},{24,8},{28,12},{1,17},{... | collective-permute-start | bytes 4718600 | tf_op jit(solution)/shard_map/ppermute | solution.py:616
  (198 other events, 2220.0 us)

commit v3 on v2

--- a/solution.py
+++ b/solution.py
@@ -7,7 +7,7 @@
 
 LCHUNK = 256
 norm_eps = 1e-06
-FL = {'cot': (0,), 'cot_ready': (0, 1), 'prefix': (0,), 'glu': (), 'branch': (), 'inner': (0,), 'feed': (1,), 'one': (), 'one_ready': (0,), 'gated': (), 'gated_ready': (0,), 'kernel': 0, 'kernel_rec': 0, 'gate': (0,), 'far_down': (0,), 'far_gate': (), 'far_up': (0,), 'joined': (), 'near_branch': (), 'branch_ready': (), 'out': (), 'far_joined': (), 'far_out': (), 'own_down': (2,), 'own_gate': (2,), 'own_up': (2,), 'own_joined': (), 'own_out': (), 'end_down': (1, 2), 'end_gate': (1, 2), 'end_up': (1, 2), 'end_joined': (), 'end_out': (), 'sends': 7, 'direct': 0, 'steps': (1, 2, 4)}
+FL = {'cot': (0,), 'cot_ready': (0, 1), 'prefix': (0,), 'glu': (), 'branch': (), 'inner': (0,), 'feed': (0,), 'one': (), 'one_ready': (0,), 'gated': (), 'gated_ready': (0,), 'kernel': 0, 'kernel_rec': 0, 'gate': (0,), 'far_down': (0,), 'far_gate': (), 'far_up': (0,), 'joined': (0,), 'near_branch': (), 'branch_ready': (), 'out': (0,), 'far_joined': (1,), 'far_out': (), 'own_down': (1,), 'own_gate': (2,), 'own_up': (2,), 'own_joined': (), 'own_out': (2,), 'end_down': (1, 2), 'end_gate': (0,), 'end_up': (1, 2), 'end_joined': (), 'end_out': (1,), 'sends': 2, 'direct': 0, 'steps': (2, 1, 4), 'dn1': (), 'carried': (), 'suffix': ()}
 F32 = jnp.float32
 BF16 = jnp.bfloat16
 
@@ -322,9 +322,9 @@
     side = mine % 2
     chunks = ((LCHUNK, short_rows), (0, LCHUNK))
 
-    def half(value, own, chunk):
+    def half(value, own, chunk, *before):
         first, size = chunk
-        which = core if own else 1 - core
+        which = later(core if own else 1 - core, *before)
         return lax.dynamic_slice_in_dim(value, first + which * (size // 2), size // 2, 0)
 
     def swap_core(value):
@@ -483,6 +483,11 @@
         def part_down(i, y):
             return left_dot(hiddens, columns(cots, 2 * planes[i] + y))
 
+
+        def two(value, *before):
+            y = later(1 - side, *before)
+            return jnp.concatenate([columns(value, 2 * planes[i] + y) for i in (1, 0)], axis=1)
+
         down_sent = part_down(1, 1 - side)
         down_got = swap_y(down_sent)
 
@@ -509,7 +514,20 @@
         inner = after(inner, *pick("inner", (down_got,)))
     d_states = state_scale * (d_normed - normed_state * (inner / width)[:, None])
     back_local, back_decay = scan(decay, d_states, True)
-    carried_in, carry_sent = carry_of(forget[0] * back_decay[0], forget[0] * back_local[0], True)
+    suffix_order = pick("suffix", (down_got,)) if fast else []
+    carried_in, carry_sent = carry_of(
+        forget[0] * back_decay[0], forget[0] * back_local[0], True, *suffix_order
+    )
+    dn1_order = ()
+    if fast:
+
+        def swap_far(value):
+            return lax.ppermute(value, "seq", FAR_PAIRS)
+
+        far_down = part_down(1, later(side, *pick("far_down", (carry_sent, carried_in)))) + down_got
+        far_down_got = swap_far(far_down)
+        dn1_order = pick("dn1", (far_down_got, far_down))
+        carried_in = after(carried_in, *pick("carried", (far_down,)))
     carried = entered(back_local, back_decay, carried_in)
     states_prev = entered(before_local, before_decay, carry_in)
     d_forget = carried * (states_prev - input_act)
@@ -525,7 +543,7 @@
         both = []
         for own in (False, True):
             both.append(
-                right_dot(half(d_input, own, chunk), w_input)
+                right_dot(half(d_input, own, chunk, *dn1_order), w_input)
                 + right_dot(half(d_pforget, own, chunk), w_forget)
                 + right_dot(half(d_rgate, own, chunk), w_rgate)
             )
@@ -612,17 +630,13 @@
         def part_joined(i, y):
             return mm("kernel_rec", both_one, 2 * i + y, joined, None)
 
-        def swap_far(value):
-            return lax.ppermute(value, "seq", FAR_PAIRS)
-
-        gate_sent = part_gate(1, later(1 - side, *pick("gate", (carry_sent,))))
-        up_sent = part_up(1, later(1 - side, *pick("gate", (carry_sent,))))
-        far_down = part_down(1, later(side, *pick("far_down", (carry_sent, carried_in)))) + down_got
-        far_gate = part_gate(1, later(side, *pick("far_gate", (carried_in, joined_wide)))) + swap_y(gate_sent)
-        far_up = part_up(1, later(side, *pick("far_up", (carried_in, joined_wide, far_gate)))) + swap_y(up_sent)
-        far_down_got, far_gate_got, far_up_got = (
-            swap_far(value) for value in (far_down, far_gate, far_up)
-        )
+        gate_sent = left_dot(two(normed, *pick("gate", (carry_sent,))), gates)
+        up_sent = left_dot(two(normed, *pick("gate", (carry_sent,))), ups)
+        gate_both, up_both = swap_y(gate_sent), swap_y(up_sent)
+        own_gate, own_up = gate_both[block:], up_both[block:]
+        far_gate = part_gate(1, later(side, *pick("far_gate", (carried_in, joined_wide)))) + gate_both[:block]
+        far_up = part_up(1, later(side, *pick("far_up", (carried_in, joined_wide, far_gate)))) + up_both[:block]
+        far_gate_got, far_up_got = swap_far(far_gate), swap_far(far_up)
         near_joined = near_whole(
             joined_wide, *pick("joined", (far_down_got, far_gate_got, far_up, far_down))
         )
@@ -642,16 +656,18 @@
         )
         far_out = part_out(1, later(side, *pick("far_out", (far_joined,)))) + swap_y(out_sent)
 
-        def finish(part, got, name):
-            sent = part(0, later(1 - side, *pick("own_" + name, (up_sent, joined_sent, far_joined))))
+        def finish(part, got, name, own=None):
+            if own is None:
+                sent = part(0, later(1 - side, *pick("own_" + name, (up_sent, joined_sent, far_joined))))
+                ends.append(sent)
+                own = swap_y(sent)
             kept = part(0, later(side, *pick("end_" + name, (joined_sent, far_joined, far_out))))
-            ends.append(sent)
-            return kept + swap_y(sent) + got
+            return kept + own + got
 
         ends = [far_joined, far_out]
         grad_w_down = finish(part_down, far_down_got, "down")
-        grad_w_gate = finish(part_gate, far_gate_got, "gate")
-        grad_w_up = finish(part_up, far_up_got, "up")
+        grad_w_gate = finish(part_gate, far_gate_got, "gate", own_gate)
+        grad_w_up = finish(part_up, far_up_got, "up", own_up)
         grad_joined = finish(part_joined, swap_far(far_joined), "joined")
         grad_w_out = finish(part_out, swap_far(far_out), "out")
         sends = ends[: FL["sends"]]

time: 699 us -> 658 us (0.941)
  waiting for transfers between devices: 349 us -> 274 us
  matrix products: 159 us -> 185 us
  other arithmetic: 50.6 us -> 62.4 us
  starting transfers between devices: 68.8 us -> 61.8 us
    ppermute x5, waiting for transfers between devices: 98.1 us -> 26.4 us  [swap_far(): return lax.ppermute(value, 'seq', FAR_PAIRS)]
    ppermute x3, waiting for transfers between devices: 1.71 us -> 51.5 us  [per_device(): lax.ppermute(pieces, 'seq', [(i, i ^ step) for i in range(8)])]
    ppermute x8, waiting for transfers between devices: 114 us -> 82.8 us  [summed_half(): return (value + lax.ppermute(value, 'mp', X_PAIRS), value)]
    ppermute x6, waiting for transfers between devices: 26.4 us -> 0.71 us  [near_rows(): own = after(lax.ppermute(value, 'seq', Z_PAIRS), *ready)]
    dot_general x20 -> x18, matrix products: 52.8 us -> 76.6 us  [left_dot(): lax.dot_general(left, right, (((0,), (0,)), ((), ())), preferred_element_...]
    ppermute x2, waiting for transfers between devices: 4.48 us -> 19.5 us  [near_whole(): near = lax.ppermute(value, 'seq', Z_PAIRS)]
    ppermute x10 -> x8, waiting for transfers between devices: 97.5 us -> 86.7 us  [swap_y(): return lax.ppermute(value, 'seq', Y_PAIRS)]
    unnamed x352 -> x332, local copies, waits for them, and re-layouts: 20.8 us -> 22.2 us
  transfers between devices with their start and end apart: 71 -> 69, of which waited for: 26 -> 21; matrix products, arithmetic and copies ran while one was open for 32% -> 39% of each run, Pallas kernels for 2% -> 2%
where the time goes in v3:
time: 658 us; the launch traced here: 651 us
  waiting for transfers between devices  274 us (42%)
  matrix products  185 us (28%)
  other arithmetic  62.4 us (9%)
  starting transfers between devices  61.8 us (9%)
  local copies, waits for them, and re-layouts  42.8 us (7%)
  between operations  13.8 us (2%)
  Pallas kernels  11.5 us (2%)
    ppermute x8, waiting for transfers between devices, swap_y(): return lax.ppermute(value, 'seq', Y_PAIRS)  86.7 us
    ppermute x8, waiting for transfers between devices, summed_half(): return (value + lax.ppermute(value, 'mp', X_PAIRS), value)  82.8 us
    dot_general x18, matrix products, left_dot(): lax.dot_general(left, right, (((0,), (0,)), ((), ())), preferred_element_...  76.6 us
    dot_general x24, matrix products, right_dot(): lax.dot_general(left, right, (((1,), (1,)), ((), ())), preferred_element_...  57.1 us
    ppermute x3, waiting for transfers between devices, per_device(): lax.ppermute(pieces, 'seq', [(i, i ^ step) for i in range(8)])  51.5 us
    dot_general x19, matrix products, dot(): return jnp.dot(left, right, preferred_element_type=F32)  51.5 us
    ppermute x5, waiting for transfers between devices, swap_far(): return lax.ppermute(value, 'seq', FAR_PAIRS)  26.4 us
    unnamed x332, local copies, waits for them, and re-layouts  22.2 us
  transfers between devices with their start and end apart: 69, of which 21 were waited for; matrix products, arithmetic and copies ran while one was open for 39% of the time, Pallas kernels for 2%

profile of v3, /device:TPU:0, one launch (start us, length us, event | category | flops | bytes accessed | tf_op | source)
XLA Modules:
  0.0 651.4 jit_solution(4027924286388764645)
XLA Ops:
  3.1 3.7 fusion.1
  11.5 4.0 fusion.32
  35.9 4.4 collective-permute-start.5
  62.8 5.6 fusion.10
  70.4 15.7 %collective-permute-done.9 = f32[128,2048]{1,0:T(8,128)S(1)} collective-permute-done((f32[128,2048]{1,0:T(8,128)S(1)}, f32[128,2048]{1,0:T(8,128)S(1)}, u32[]{:S(2)}, u32[]{:S(2)}) %collective-permute-start.9) | collective-permute-done | bytes 1048608 | tf_op jit(solution)/shard_map/ppermute | solution.py:298
  87.8 25.5 %collective-permute-done.17 = f32[160,2048]{1,0:T(8,128)S(1)} collective-permute-done((f32[160,2048]{1,0:T(8,128)S(1)}, f32[160,2048]{1,0:T(8,128)S(1)}, u32[]{:S(2)}, u32[]{:S(2)}) %collective-permute-start.17) | collective-permute-done | bytes 1310752 | tf_op jit(solution)/shard_map/ppermute | solution.py:298
  120.9 4.5 multiply_convert_fusion.11
  142.2 5.6 multiply_convert_fusion.5
  152.0 3.1 convolution_add_fusion.21
  159.3 3.4 fusion.179
  162.7 3.2 fusion.9
  169.5 3.4 multiply_convert_fusion.8
  175.6 4.9 fusion.8
  181.2 4.2 multiply_convert_fusion.2
  185.3 6.6 %collective-permute-done.12 = f32[128,2048]{1,0:T(8,128)S(1)} collective-permute-done((f32[128,2048]{1,0:T(8,128)S(1)}, f32[128,2048]{1,0:T(8,128)S(1)}, u32[]{:S(2)}, u32[]{:S(2)}) %collective-permute-start.12) | collective-permute-done | bytes 1048608 | tf_op jit(solution)/shard_map/ppermute | solution.py:298
  193.7 3.5 fusion.70
  204.1 4.7 fusion.87
  208.8 4.1 fusion.78
  213.5 6.2 collective-permute-done.24
  225.9 4.7 collective-permute-done.36
  232.5 3.4 convolution_add_fusion.17
  241.9 3.2 fusion.162
  264.9 5.1 fusion.47
  270.0 4.6 convolution_add_fusion.4
  274.7 3.9 fusion.48
  298.3 6.5 %collective-permute-done.14 = f32[128,2048]{1,0:T(8,128)S(1)} collective-permute-done((f32[128,2048]{1,0:T(8,128)S(1)}, f32[128,2048]{1,0:T(8,128)S(1)}, u32[]{:S(2)}, u32[]{:S(2)}) %collective-permute-start.14) | collective-permute-done | bytes 1048608 | tf_op jit(solution)/shard_map/ppermute | solution.py:298
  304.8 4.2 collective-permute-start.52
  321.8 3.1 fusion.7
  324.9 5.2 collective-permute-done.20
  339.5 26.4 %collective-permute-done.52 = f32[1408,256]{1,0:T(8,128)} collective-permute-done((f32[1408,256]{1,0:T(8,128)}, f32[1408,256]{1,0:T(8,128)}, u32[]{:S(2)}, u32[]{:S(2)}) %collective-permute-start.52) | collective-permute-done | bytes 1441824 | tf_op jit(solution)/shard_map/ppermute | solution.py:525
  385.7 17.0 %collective-permute-done.45 = f32[160,2048]{1,0:T(8,128)S(1)} collective-permute-done((f32[160,2048]{1,0:T(8,128)S(1)}, f32[160,2048]{1,0:T(8,128)S(1)}, u32[]{:S(2)}, u32[]{:S(2)}) %collective-permute-start.45) | collective-permute-done | bytes 1310752 | tf_op jit(solution)/shard_map/ppermute | solution.py:298
  405.7 4.3 convolution_add_fusion.5
  410.2 48.4 %collective-permute-done.66 = f32[512,1408]{1,0:T(8,128)S(1)} collective-permute-done((f32[512,1408]{1,0:T(8,128)S(1)}, f32[512,1408]{1,0:T(8,128)S(1)}, u32[]{:S(2)}, u32[]{:S(2)}) %collective-permute-start.66) | collective-permute-done | bytes 2883616 | tf_op jit(solution)/shard_map/ppermute | solution.py:334
  458.6 3.9 convolution_add_fusion.1
  462.5 3.6 collective-permute-start.67
  467.6 19.5 %collective-permute-done.53.refs_1_ = f32[576,1536]{1,0:T(8,128)S(1)} collective-permute-done((f32[576,1536]{1,0:T(8,128)S(1)}, f32[576,1536]{1,0:T(8,128)S(1)}, u32[]{:S(2)}, u32[]{:S(2)}) %collective-permute-start.53) | collective-permute-done | bytes 3538976 | tf_op jit(solution)/shard_map/ppermute | solution.py:596
  498.3 4.4 fusion.50
  502.7 11.9 %fusion.59 = f32[256,1536]{1,0:T(8,128)} fusion(bf16[1152,1024]{1,0:T(8,128)(2,1)} %pad_maximum_fusion.10, s32[]{:T(128)S(6)} %select_n.315, bf16[576,1536]{1,0:T(8,128)(2,1)S(1)} %placed.9, bf16[576,512]{1,0:T(8,128)(2,1)S(1)} %copy-done.116, bf16[576,512]{1,0:T(8,128)(2,1)S(1)} %copy-done.70, bf16[576,512]{1,0:T(8,128)(2,1)S(1)} %copy-done.75), kind=kOutput, calls=%fused_computation.172 | convolution fusion | flops 920125440 | bytes 5701636 | tf_op jit(solution)/shard_map/dot_general | solution.py:26
  519.6 22.9 %collective-permute-done.58 = f32[512,256]{1,0:T(8,128)} collective-permute-done((f32[512,256]{1,0:T(8,128)}, f32[512,256]{1,0:T(8,128)}, u32[]{:S(2)}, u32[]{:S(2)}) %collective-permute-start.58) | collective-permute-done | bytes 524320 | tf_op jit(solution)/shard_map/ppermute | solution.py:334
  548.4 4.5 fusion.2
  554.8 3.2 convolution_add_fusion.7
  562.7 10.7 %collective-permute-done.68 = f32[1408,256]{1,0:T(8,128)} collective-permute-done((f32[1408,256]{1,0:T(8,128)}, f32[1408,256]{1,0:T(8,128)}, u32[]{:S(2)}, u32[]{:S(2)}) %collective-permute-start.68) | collective-permute-done | bytes 1441824 | tf_op jit(solution)/shard_map/ppermute | solution.py:334
  573.4 5.2 fusion.4
  579.3 13.0 %collective-permute-done.59 = f32[8,640]{1,0:T(8,128)S(1)} collective-permute-done((f32[8,640]{1,0:T(8,128)S(1)}, f32[8,640]{1,0:T(8,128)S(1)}, u32[]{:S(2)}, u32[]{:S(2)}) %collective-permute-start.59) | collective-permute-done | bytes 20512 | tf_op jit(solution)/shard_map/ppermute | solution.py:705
  596.5 8.7 %collective-permute-done.60 = f32[8,640]{1,0:T(8,128)S(1)} collective-permute-done((f32[8,640]{1,0:T(8,128)S(1)}, f32[8,640]{1,0:T(8,128)S(1)}, u32[]{:S(2)}, u32[]{:S(2)}) %collective-permute-start.60) | collective-permute-done | bytes 20512 | tf_op jit(solution)/shard_map/ppermute | solution.py:705
  607.4 4.1 fusion.3
  611.5 29.8 %collective-permute-done.61 = f32[8,640]{1,0:T(8,128)S(1)} collective-permute-done((f32[8,640]{1,0:T(8,128)S(1)}, f32[8,640]{1,0:T(8,128)S(1)}, u32[]{:S(2)}, u32[]{:S(2)}) %collective-permute-start.61) | collective-permute-done | bytes 20512 | tf_op jit(solution)/shard_map/ppermute | solution.py:705
  645.4 4.3 fusion.5
  (627 shorter events, 231.6 us)
Async XLA Ops:
  8.1 216.7 %collective-permute-start.48 = (f32[288,1024]{1,0:T(8,128)}, f32[288,1024]{1,0:T(8,128)}, u32[]{:S(2)}, u32[]{:S(2)}) collective-permute-start(f32[288,1024]{1,0:T(8,128)} %pad_maximum_fusion.14), channel_id=1, source_target_pairs={{0,8},{4,12},{8,0},{12,4},{16,24},{20,28},{24,16},{28,20},{1,9},{5... | collective-permute-start | bytes 3538952 | tf_op jit(solution)/shard_map/ppermute | solution.py:353
  53.4 63.0 %collective-permute-start.34 = (f32[128,2048]{1,0:T(8,128)}, f32[128,2048]{1,0:T(8,128)S(1)}, u32[]{:S(2)}, u32[]{:S(2)}) collective-permute-start(f32[128,2048]{1,0:T(8,128)} %get-tuple-element.45), channel_id=1, source_target_pairs={{0,8},{4,12},{8,0},{12,4},{16,24},{20,28},{24,16},{28,20},{1,9},{5... | collective-permute-start | bytes 3145736 | tf_op jit(solution)/shard_map/ppermute | solution.py:353
  57.1 59.8 %collective-permute-start.32 = (f32[160,2048]{1,0:T(8,128)S(1)}, f32[160,2048]{1,0:T(8,128)S(1)}, u32[]{:S(2)}, u32[]{:S(2)}) collective-permute-start(f32[160,2048]{1,0:T(8,128)S(1)} %get-tuple-element.47), channel_id=1, source_target_pairs={{0,8},{4,12},{8,0},{12,4},{16,24},{20,28},{24,16},{28,20},{1,9},{5... | collective-permute-start | bytes 3932168 | tf_op jit(solution)/shard_map/ppermute | solution.py:353
  60.0 26.1 %collective-permute-start.9 = (f32[128,2048]{1,0:T(8,128)S(1)}, f32[128,2048]{1,0:T(8,128)S(1)}, u32[]{:S(2)}, u32[]{:S(2)}) collective-permute-start(f32[128,2048]{1,0:T(8,128)S(1)} %convolution_add_fusion.20), channel_id=1, source_target_pairs={{0,2},{1,3},{2,0},{3,1},{4,6},{5,7},{6,4},{7,5},{8,10},{9,11},{10,... | collective-permute-start | bytes 3145736 | tf_op jit(solution)/shard_map/ppermute | solution.py:298
  61.3 52.1 %collective-permute-start.17 = (f32[160,2048]{1,0:T(8,128)S(1)}, f32[160,2048]{1,0:T(8,128)S(1)}, u32[]{:S(2)}, u32[]{:S(2)}) collective-permute-start(f32[160,2048]{1,0:T(8,128)S(1)} %convolution_add_fusion.12), channel_id=1, source_target_pairs={{0,2},{1,3},{2,0},{3,1},{4,6},{5,7},{6,4},{7,5},{8,10},{9,11},{10,... | collective-permute-start | bytes 3932168 | tf_op jit(solution)/shard_map/ppermute | solution.py:298
  87.0 50.5 %collective-permute-start.30 = (f32[128,2048]{1,0:T(8,128)S(1)}, f32[128,2048]{1,0:T(8,128)S(1)}, u32[]{:S(2)}, u32[]{:S(2)}) collective-permute-start(f32[128,2048]{1,0:T(8,128)S(1)} %get-tuple-element.106), channel_id=1, source_target_pairs={{0,8},{4,12},{8,0},{12,4},{16,24},{20,28},{24,16},{28,20},{1,9},{5... | collective-permute-start | bytes 3145736 | tf_op jit(solution)/shard_map/ppermute | solution.py:353
  116.4 40.8 %collective-permute-start.28 = (f32[160,2048]{1,0:T(8,128)S(1)}, f32[160,2048]{1,0:T(8,128)S(1)}, u32[]{:S(2)}, u32[]{:S(2)}) collective-permute-start(f32[160,2048]{1,0:T(8,128)S(1)} %get-tuple-element.110), channel_id=1, source_target_pairs={{0,8},{4,12},{8,0},{12,4},{16,24},{20,28},{24,16},{28,20},{1,9},{5... | collective-permute-start | bytes 3932168 | tf_op jit(solution)/shard_map/ppermute | solution.py:353
  116.9 20.8 %collective-permute-start.18 = (f32[160,2048]{1,0:T(8,128)S(1)}, f32[160,2048]{1,0:T(8,128)S(1)}, u32[]{:S(2)}, u32[]{:S(2)}) collective-permute-start(f32[160,2048]{1,0:T(8,128)S(1)} %get-tuple-element.110), channel_id=1, source_target_pairs={{0,1},{1,0},{2,3},{3,2},{4,5},{5,4},{6,7},{7,6},{8,9},{9,8},{10,11... | collective-permute-start | bytes 3932168 | tf_op jit(solution)/shard_map/ppermute | solution.py:331
  117.3 16.4 %collective-permute-start.35 = (f32[128,2048]{1,0:T(8,128)S(1)}, f32[128,2048]{1,0:T(8,128)S(1)}, u32[]{:S(2)}, u32[]{:S(2)}) collective-permute-start(f32[128,2048]{1,0:T(8,128)S(1)} %broadcast_add_fusion.1.refs_1_), channel_id=1, source_target_pairs={{0,1},{1,0},{2,3},{3,2},{4,5},{5,4},{6,7},{7,6},{8,9},{9,8},{10,11... | collective-permute-start | bytes 3145736 | tf_op jit(solution)/shard_map/ppermute | solution.py:331
  137.4 25.3 %collective-permute-start.11 = (f32[128,2048]{1,0:T(8,128)}, f32[128,2048]{1,0:T(8,128)}, u32[]{:S(2)}, u32[]{:S(2)}) collective-permute-start(f32[128,2048]{1,0:T(8,128)} %convolution_add_fusion.18), channel_id=1, source_target_pairs={{0,1},{1,0},{2,3},{3,2},{4,5},{5,4},{6,7},{7,6},{8,9},{9,8},{10,11... | collective-permute-start | bytes 3145736 | tf_op jit(solution)/shard_map/ppermute | solution.py:297
  137.7 29.6 %collective-permute-start.31 = (f32[128,2048]{1,0:T(8,128)S(1)}, f32[128,2048]{1,0:T(8,128)S(1)}, u32[]{:S(2)}, u32[]{:S(2)}) collective-permute-start(f32[128,2048]{1,0:T(8,128)S(1)} %collective-permute-done.30.refs_0_), channel_id=1, source_target_pairs={{0,1},{1,0},{2,3},{3,2},{4,5},{5,4},{6,7},{7,6},{8,9},{9,8},{10,11... | collective-permute-start | bytes 3145736 | tf_op jit(solution)/shard_map/ppermute | solution.py:331
  156.3 19.3 %collective-permute-start.23 = (f32[160,2048]{1,0:T(8,128)}, f32[160,2048]{1,0:T(8,128)}, u32[]{:S(2)}, u32[]{:S(2)}) collective-permute-start(f32[160,2048]{1,0:T(8,128)} %convolution_add_fusion.21), channel_id=1, source_target_pairs={{0,1},{1,0},{2,3},{3,2},{4,5},{5,4},{6,7},{7,6},{8,9},{9,8},{10,11... | collective-permute-start | bytes 3932168 | tf_op jit(solution)/shard_map/ppermute | solution.py:297
  157.3 15.7 %collective-permute-start.29 = (f32[160,2048]{1,0:T(8,128)S(1)}, f32[160,2048]{1,0:T(8,128)S(1)}, u32[]{:S(2)}, u32[]{:S(2)}) collective-permute-start(f32[160,2048]{1,0:T(8,128)S(1)} %collective-permute-done.28.refs_0_), channel_id=1, source_target_pairs={{0,1},{1,0},{2,3},{3,2},{4,5},{5,4},{6,7},{7,6},{8,9},{9,8},{10,11... | collective-permute-start | bytes 3932168 | tf_op jit(solution)/shard_map/ppermute | solution.py:331
  165.9 26.0 %collective-permute-start.12 = (f32[128,2048]{1,0:T(8,128)S(1)}, f32[128,2048]{1,0:T(8,128)S(1)}, u32[]{:S(2)}, u32[]{:S(2)}) collective-permute-start(f32[128,2048]{1,0:T(8,128)S(1)} %fusion.9), channel_id=1, source_target_pairs={{0,2},{1,3},{2,0},{3,1},{4,6},{5,7},{6,4},{7,5},{8,10},{9,11},{10,... | collective-permute-start | bytes 3145736 | tf_op jit(solution)/shard_map/ppermute | solution.py:298
  180.5 39.3 %collective-permute-start.24 = (f32[160,2048]{1,0:T(8,128)}, f32[160,2048]{1,0:T(8,128)}, u32[]{:S(2)}, u32[]{:S(2)}) collective-permute-start(f32[160,2048]{1,0:T(8,128)} %fusion.8), channel_id=1, source_target_pairs={{0,2},{1,3},{2,0},{3,1},{4,6},{5,7},{6,4},{7,5},{8,10},{9,11},{10,... | collective-permute-start | bytes 3932168 | tf_op jit(solution)/shard_map/ppermute | solution.py:298
  197.2 33.3 %collective-permute-start.36 = (f32[1408,256]{1,0:T(8,128)}, f32[1408,256]{1,0:T(8,128)}, u32[]{:S(2)}, u32[]{:S(2)}) collective-permute-start(f32[1408,256]{1,0:T(8,128)} %fusion.70), channel_id=1, source_target_pairs={{0,4},{4,0},{8,12},{12,8},{16,20},{20,16},{24,28},{28,24},{1,5},{5... | collective-permute-start | bytes 4325384 | tf_op jit(solution)/shard_map/ppermute | solution.py:334
  208.8 23.6 %collective-permute-start.13 = (f32[128,2048]{1,0:T(8,128)}, f32[128,2048]{1,0:T(8,128)}, u32[]{:S(2)}, u32[]{:S(2)}) collective-permute-start(f32[128,2048]{1,0:T(8,128)} %fusion.87), channel_id=1, source_target_pairs={{0,1},{1,0},{2,3},{3,2},{4,5},{5,4},{6,7},{7,6},{8,9},{9,8},{10,11... | collective-permute-start | bytes 3145736 | tf_op jit(solution)/shard_map/ppermute | solution.py:297
  213.0 22.9 %collective-permute-start.19 = (f32[160,2048]{1,0:T(8,128)S(1)}, f32[160,2048]{1,0:T(8,128)S(1)}, u32[]{:S(2)}, u32[]{:S(2)}) collective-permute-start(f32[160,2048]{1,0:T(8,128)S(1)} %fusion.78), channel_id=1, source_target_pairs={{0,1},{1,0},{2,3},{3,2},{4,5},{5,4},{6,7},{7,6},{8,9},{9,8},{10,11... | collective-permute-start | bytes 3932168 | tf_op jit(solution)/shard_map/ppermute | solution.py:297
  224.8 92.3 %collective-permute-start.55 = (f32[576,512]{1,0:T(8,128)}, f32[576,512]{1,0:T(8,128)S(1)}, u32[]{:S(2)}, u32[]{:S(2)}) collective-permute-start(f32[576,512]{1,0:T(8,128)} %pad_maximum_fusion.16), channel_id=1, source_target_pairs={{0,8},{4,12},{8,0},{12,4},{16,24},{20,28},{24,16},{28,20},{1,9},{5... | collective-permute-start | bytes 3538952 | tf_op jit(solution)/shard_map/ppermute | solution.py:596
  230.5 66.4 %collective-permute-start.49 = (f32[288,1024]{1,0:T(8,128)}, f32[288,1024]{1,0:T(8,128)}, u32[]{:S(2)}, u32[]{:S(2)}) collective-permute-start(f32[288,1024]{1,0:T(8,128)} %collective-permute-done.48.refs_1_), channel_id=1, source_target_pairs={{0,1},{1,0},{2,3},{3,2},{4,5},{5,4},{6,7},{7,6},{8,9},{9,8},{10,11... | collective-permute-start | bytes 3538952 | tf_op jit(solution)/shard_map/ppermute | solution.py:331
  259.0 19.7 %collective-permute-start.40 = (f32[2,512]{1,0:T(2,128)S(1)}, f32[2,512]{1,0:T(2,128)S(1)}, u32[]{:S(2)}, u32[]{:S(2)}) collective-permute-start(f32[2,512]{1,0:T(2,128)S(1)} %pad_maximum_fusion.24), channel_id=1, source_target_pairs={{24,0},{28,4},{25,1},{29,5},{26,2},{30,6},{27,3},{31,7}} | collective-permute-start | bytes 12296 | tf_op jit(solution)/shard_map/ppermute | solution.py:285
  260.3 19.8 %collective-permute-start.39 = (f32[2,512]{1,0:T(2,128)S(1)}, f32[2,512]{1,0:T(2,128)S(1)}, u32[]{:S(2)}, u32[]{:S(2)}) collective-permute-start(f32[2,512]{1,0:T(2,128)S(1)} %pad_maximum_fusion.24), channel_id=1, source_target_pairs={{16,0},{20,4},{24,8},{28,12},{17,1},{21,5},{25,9},{29,13},{18,2},{... | collective-permute-start | bytes 12296 | tf_op jit(solution)/shard_map/ppermute | solution.py:285
  261.6 19.2 %collective-permute-start.38 = (f32[2,512]{1,0:T(2,128)S(1)}, f32[2,512]{1,0:T(2,128)S(1)}, u32[]{:S(2)}, u32[]{:S(2)}) collective-permute-start(f32[2,512]{1,0:T(2,128)S(1)} %pad_maximum_fusion.24), channel_id=1, source_target_pairs={{8,0},{12,4},{16,8},{20,12},{24,16},{28,20},{9,1},{13,5},{17,9},{2... | collective-permute-start | bytes 12296 | tf_op jit(solution)/shard_map/ppermute | solution.py:285
  278.6 26.2 %collective-permute-start.14 = (f32[128,2048]{1,0:T(8,128)S(1)}, f32[128,2048]{1,0:T(8,128)S(1)}, u32[]{:S(2)}, u32[]{:S(2)}) collective-permute-start(f32[128,2048]{1,0:T(8,128)S(1)} %copy-done.64), channel_id=1, source_target_pairs={{0,2},{1,3},{2,0},{3,1},{4,6},{5,7},{6,4},{7,5},{8,10},{9,11},{10,... | collective-permute-start | bytes 3145736 | tf_op jit(solution)/shard_map/ppermute | solution.py:298
  280.0 50.1 %collective-permute-start.20 = (f32[160,2048]{1,0:T(8,128)}, f32[160,2048]{1,0:T(8,128)}, u32[]{:S(2)}, u32[]{:S(2)}) collective-permute-start(f32[160,2048]{1,0:T(8,128)} %convolution_add_fusion.23), channel_id=1, source_target_pairs={{0,2},{1,3},{2,0},{3,1},{4,6},{5,7},{6,4},{7,5},{8,10},{9,11},{10,... | collective-permute-start | bytes 3932168 | tf_op jit(solution)/shard_map/ppermute | solution.py:298
  289.4 29.6 %collective-permute-start.41 = (f32[128,2048]{1,0:T(8,128)}, f32[128,2048]{1,0:T(8,128)}, u32[]{:S(2)}, u32[]{:S(2)}) collective-permute-start(f32[128,2048]{1,0:T(8,128)} %convolution_add_fusion.13), channel_id=1, source_target_pairs={{0,1},{1,0},{2,3},{3,2},{4,5},{5,4},{6,7},{7,6},{8,9},{9,8},{10,11... | collective-permute-start | bytes 3145736 | tf_op jit(solution)/shard_map/ppermute | solution.py:297
  297.0 38.2 %collective-permute-start.44 = (f32[160,2048]{1,0:T(8,128)}, f32[160,2048]{1,0:T(8,128)}, u32[]{:S(2)}, u32[]{:S(2)}) collective-permute-start(f32[160,2048]{1,0:T(8,128)} %convolution_add_fusion.8), channel_id=1, source_target_pairs={{0,1},{1,0},{2,3},{3,2},{4,5},{5,4},{6,7},{7,6},{8,9},{9,8},{10,11... | collective-permute-start | bytes 3932168 | tf_op jit(solution)/shard_map/ppermute | solution.py:297
  304.8 61.0 %collective-permute-start.52 = (f32[1408,256]{1,0:T(8,128)}, f32[1408,256]{1,0:T(8,128)}, u32[]{:S(2)}, u32[]{:S(2)}) collective-permute-start(f32[1408,256]{1,0:T(8,128)} %convolution_add_fusion.4), channel_id=1, source_target_pairs={{0,16},{4,20},{8,24},{12,28},{16,0},{20,4},{24,8},{28,12},{1,17},{... | collective-permute-start | bytes 4325384 | tf_op jit(solution)/shard_map/ppermute | solution.py:525
  317.1 52.3 %collective-permute-start.56 = (f32[288,1024]{1,0:T(8,128)}, f32[288,1024]{1,0:T(8,128)}, u32[]{:S(2)}, u32[]{:S(2)}) collective-permute-start(f32[288,1024]{1,0:T(8,128)} %pad_maximum_fusion.18), channel_id=1, source_target_pairs={{0,8},{4,12},{8,0},{12,4},{16,24},{20,28},{24,16},{28,20},{1,9},{5... | collective-permute-start | bytes 3538952 | tf_op jit(solution)/shard_map/ppermute | solution.py:353
  319.1 50.3 %collective-permute-start.15 = (f32[128,2048]{1,0:T(8,128)}, f32[128,2048]{1,0:T(8,128)}, u32[]{:S(2)}, u32[]{:S(2)}) collective-permute-start(f32[128,2048]{1,0:T(8,128)} %add.769), channel_id=1, source_target_pairs={{0,1},{1,0},{2,3},{3,2},{4,5},{5,4},{6,7},{7,6},{8,9},{9,8},{10,11... | collective-permute-start | bytes 3145736 | tf_op jit(solution)/shard_map/ppermute | solution.py:331
  330.1 41.8 %collective-permute-start.42 = (f32[128,2048]{1,0:T(8,128)}, f32[128,2048]{1,0:T(8,128)}, u32[]{:S(2)}, u32[]{:S(2)}) collective-permute-start(f32[128,2048]{1,0:T(8,128)} %fusion.7), channel_id=1, source_target_pairs={{0,2},{1,3},{2,0},{3,1},{4,6},{5,7},{6,4},{7,5},{8,10},{9,11},{10,... | collective-permute-start | bytes 3145736 | tf_op jit(solution)/shard_map/ppermute | solution.py:298
  335.2 70.3 %collective-permute-start.50 = (f32[512,1408]{1,0:T(8,128)}, f32[512,1408]{1,0:T(8,128)S(1)}, u32[]{:S(2)}, u32[]{:S(2)}) collective-permute-start(f32[512,1408]{1,0:T(8,128)} %fusion.48), channel_id=1, source_target_pairs={{0,4},{4,0},{8,12},{12,8},{16,20},{20,16},{24,28},{28,24},{1,5},{5... | collective-permute-start | bytes 8650760 | tf_op jit(solution)/shard_map/ppermute | solution.py:334
  365.8 92.8 %collective-permute-start.66 = (f32[512,1408]{1,0:T(8,128)S(1)}, f32[512,1408]{1,0:T(8,128)S(1)}, u32[]{:S(2)}, u32[]{:S(2)}) collective-permute-start(f32[512,1408]{1,0:T(8,128)S(1)} %copy-done.133), channel_id=1, source_target_pairs={{0,4},{4,0},{8,12},{12,8},{16,20},{20,16},{24,28},{28,24},{1,5},{5... | collective-permute-start | bytes 8650760 | tf_op jit(solution)/shard_map/ppermute | solution.py:334
  371.9 30.7 %collective-permute-start.45 = (f32[160,2048]{1,0:T(8,128)S(1)}, f32[160,2048]{1,0:T(8,128)S(1)}, u32[]{:S(2)}, u32[]{:S(2)}) collective-permute-start(f32[160,2048]{1,0:T(8,128)S(1)} %fusion.6), channel_id=1, source_target_pairs={{0,2},{1,3},{2,0},{3,1},{4,6},{5,7},{6,4},{7,5},{8,10},{9,11},{10,... | collective-permute-start | bytes 3932168 | tf_op jit(solution)/shard_map/ppermute | solution.py:298
  377.9 109.1 %collective-permute-start.53 = (f32[576,1536]{1,0:T(8,128)S(1)}, f32[576,1536]{1,0:T(8,128)S(1)}, u32[]{:S(2)}, u32[]{:S(2)}) collective-permute-start(f32[576,1536]{1,0:T(8,128)S(1)} %copy-done.65), channel_id=1, source_target_pairs={{0,8},{4,12},{8,0},{12,4},{16,24},{20,28},{24,16},{28,20},{1,9},{5... | collective-permute-start | bytes 10616840 | tf_op jit(solution)/shard_map/ppermute | solution.py:596
  382.5 83.6 %collective-permute-start.43 = (f32[128,2048]{1,0:T(8,128)S(1)}, f32[128,2048]{1,0:T(8,128)S(1)}, u32[]{:S(2)}, u32[]{:S(2)}) collective-permute-start(f32[128,2048]{1,0:T(8,128)S(1)} %fusion.44), channel_id=1, source_target_pairs={{0,1},{1,0},{2,3},{3,2},{4,5},{5,4},{6,7},{7,6},{8,9},{9,8},{10,11... | collective-permute-start | bytes 3145736 | tf_op jit(solution)/shard_map/ppermute | solution.py:331
  404.9 109.7 %collective-permute-start.46 = (f32[160,2048]{1,0:T(8,128)}, f32[160,2048]{1,0:T(8,128)}, u32[]{:S(2)}, u32[]{:S(2)}) collective-permute-start(f32[160,2048]{1,0:T(8,128)} %fusion.35), channel_id=1, source_target_pairs={{0,1},{1,0},{2,3},{3,2},{4,5},{5,4},{6,7},{7,6},{8,9},{9,8},{10,11... | collective-permute-start | bytes 3932168 | tf_op jit(solution)/shard_map/ppermute | solution.py:331
  410.1 137.0 %collective-permute-start.51 = (f32[256,1408]{1,0:T(8,128)}, f32[256,1408]{1,0:T(8,128)}, u32[]{:S(2)}, u32[]{:S(2)}) collective-permute-start(f32[256,1408]{1,0:T(8,128)} %convolution_add_fusion.5), channel_id=1, source_target_pairs={{0,16},{4,20},{8,24},{12,28},{16,0},{20,4},{24,8},{28,12},{1,17},{... | collective-permute-start | bytes 4325384 | tf_op jit(solution)/shard_map/ppermute | solution.py:525
  462.5 143.6 %collective-permute-start.67 = (f32[256,1408]{1,0:T(8,128)}, f32[256,1408]{1,0:T(8,128)}, u32[]{:S(2)}, u32[]{:S(2)}) collective-permute-start(f32[256,1408]{1,0:T(8,128)} %convolution_add_fusion.1), channel_id=1, source_target_pairs={{0,16},{4,20},{8,24},{12,28},{16,0},{20,4},{24,8},{28,12},{1,17},{... | collective-permute-start | bytes 4325384 | tf_op jit(solution)/shard_map/ppermute | solution.py:525
  493.6 61.2 %collective-permute-start.54 = (f32[256,1536]{1,0:T(8,128)}, f32[256,1536]{1,0:T(8,128)}, u32[]{:S(2)}, u32[]{:S(2)}) collective-permute-start(f32[256,1536]{1,0:T(8,128)} %copy-done.137), channel_id=1, source_target_pairs={{0,4},{4,0},{8,12},{12,8},{16,20},{20,16},{24,28},{28,24},{1,5},{5... | collective-permute-start | bytes 4718600 | tf_op jit(solution)/shard_map/ppermute | solution.py:334
  497.0 45.5 %collective-permute-start.58 = (f32[512,256]{1,0:T(8,128)}, f32[512,256]{1,0:T(8,128)}, u32[]{:S(2)}, u32[]{:S(2)}) collective-permute-start(f32[512,256]{1,0:T(8,128)} %fusion.62), channel_id=1, source_target_pairs={{0,4},{4,0},{8,12},{12,8},{16,20},{20,16},{24,28},{28,24},{1,5},{5... | collective-permute-start | bytes 1572872 | tf_op jit(solution)/shard_map/ppermute | solution.py:334
  514.6 58.8 %collective-permute-start.68 = (f32[1408,256]{1,0:T(8,128)}, f32[1408,256]{1,0:T(8,128)}, u32[]{:S(2)}, u32[]{:S(2)}) collective-permute-start(f32[1408,256]{1,0:T(8,128)} %fusion.50), channel_id=1, source_target_pairs={{0,4},{4,0},{8,12},{12,8},{16,20},{20,16},{24,28},{28,24},{1,5},{5... | collective-permute-start | bytes 4325384 | tf_op jit(solution)/shard_map/ppermute | solution.py:334
  542.5 102.9 %collective-permute-start.62 = (f32[256,1536]{1,0:T(8,128)}, f32[256,1536]{1,0:T(8,128)}, u32[]{:S(2)}, u32[]{:S(2)}) collective-permute-start(f32[256,1536]{1,0:T(8,128)} %fusion.59), channel_id=1, source_target_pairs={{0,4},{4,0},{8,12},{12,8},{16,20},{20,16},{24,28},{28,24},{1,5},{5... | collective-permute-start | bytes 4718600 | tf_op jit(solution)/shard_map/ppermute | solution.py:334
  547.1 95.4 %collective-permute-start.65 = (f32[512,256]{1,0:T(8,128)}, f32[512,256]{1,0:T(8,128)}, u32[]{:S(2)}, u32[]{:S(2)}) collective-permute-start(f32[512,256]{1,0:T(8,128)} %convolution_add_fusion.25), channel_id=1, source_target_pairs={{0,16},{4,20},{8,24},{12,28},{16,0},{20,4},{24,8},{28,12},{1,17},{... | collective-permute-start | bytes 1572872 | tf_op jit(solution)/shard_map/ppermute | solution.py:525
  561.0 84.4 %collective-permute-start.63 = (f32[256,1536]{1,0:T(8,128)}, f32[256,1536]{1,0:T(8,128)}, u32[]{:S(2)}, u32[]{:S(2)}) collective-permute-start(f32[256,1536]{1,0:T(8,128)} %copy-done.136), channel_id=1, source_target_pairs={{0,16},{4,20},{8,24},{12,28},{16,0},{20,4},{24,8},{28,12},{1,17},{... | collective-permute-start | bytes 4718600 | tf_op jit(solution)/shard_map/ppermute | solution.py:525
  573.4 18.9 %collective-permute-start.59 = (f32[8,640]{1,0:T(8,128)S(1)}, f32[8,640]{1,0:T(8,128)S(1)}, u32[]{:S(2)}, u32[]{:S(2)}) collective-permute-start(f32[8,640]{1,0:T(8,128)S(1)} %maximum_add_fusion), channel_id=1, source_target_pairs={{0,8},{4,12},{8,0},{12,4},{16,24},{20,28},{24,16},{28,20},{1,9},{5... | collective-permute-start | bytes 61448 | tf_op jit(solution)/shard_map/ppermute | solution.py:705
  605.3 37.2 %collective-permute-start.64 = (f32[512,256]{1,0:T(8,128)}, f32[512,256]{1,0:T(8,128)}, u32[]{:S(2)}, u32[]{:S(2)}) collective-permute-start(f32[512,256]{1,0:T(8,128)} %fusion.56), channel_id=1, source_target_pairs={{0,4},{4,0},{8,12},{12,8},{16,20},{20,16},{24,28},{28,24},{1,5},{5... | collective-permute-start | bytes 1572872 | tf_op jit(solution)/shard_map/ppermute | solution.py:334
  606.1 35.2 %collective-permute-start.61 = (f32[8,640]{1,0:T(8,128)S(1)}, f32[8,640]{1,0:T(8,128)S(1)}, u32[]{:S(2)}, u32[]{:S(2)}) collective-permute-start(f32[8,640]{1,0:T(8,128)S(1)} %add.883), channel_id=1, source_target_pairs={{0,16},{4,20},{8,24},{12,28},{16,0},{20,4},{24,8},{28,12},{1,17},{... | collective-permute-start | bytes 61448 | tf_op jit(solution)/shard_map/ppermute | solution.py:705
  (186 other events, 1853.1 us)

commit v4 on v3

--- a/solution.py
+++ b/solution.py
@@ -7,7 +7,7 @@
 
 LCHUNK = 256
 norm_eps = 1e-06
-FL = {'cot': (0,), 'cot_ready': (0, 1), 'prefix': (0,), 'glu': (), 'branch': (), 'inner': (0,), 'feed': (0,), 'one': (), 'one_ready': (0,), 'gated': (), 'gated_ready': (0,), 'kernel': 0, 'kernel_rec': 0, 'gate': (0,), 'far_down': (0,), 'far_gate': (), 'far_up': (0,), 'joined': (0,), 'near_branch': (), 'branch_ready': (), 'out': (0,), 'far_joined': (1,), 'far_out': (), 'own_down': (1,), 'own_gate': (2,), 'own_up': (2,), 'own_joined': (), 'own_out': (2,), 'end_down': (1, 2), 'end_gate': (0,), 'end_up': (1, 2), 'end_joined': (), 'end_out': (1,), 'sends': 2, 'direct': 0, 'steps': (2, 1, 4), 'dn1': (), 'carried': (), 'suffix': ()}
+FL = {'cot': (0,), 'cot_ready': (1,), 'prefix': (0,), 'glu': (), 'branch': (1,), 'inner': (0,), 'feed': (0,), 'one': (), 'one_ready': (0,), 'gated': (), 'gated_ready': (0,), 'kernel': 0, 'kernel_rec': 0, 'gate': (0,), 'far_down': (0,), 'far_gate': (0,), 'far_up': (0,), 'joined': (0,), 'near_branch': (), 'branch_ready': (), 'out': (0,), 'far_joined': (1,), 'far_out': (), 'own_down': (1,), 'own_gate': (2,), 'own_up': (2,), 'own_joined': (), 'own_out': (2,), 'end_down': (1, 2), 'end_gate': (1,), 'end_up': (1, 2), 'end_joined': (), 'end_out': (1,), 'sends': 2, 'direct': 0, 'steps': (2, 1, 4), 'dn1': (), 'carried': (), 'suffix': ()}
 F32 = jnp.float32
 BF16 = jnp.bfloat16
 

time: 658 us -> 652 us (level)
    ppermute x6, waiting for transfers between devices: 0.71 us -> 21.3 us  [near_rows(): own = after(lax.ppermute(value, 'seq', Z_PAIRS), *ready)]
    ppermute x8, waiting for transfers between devices: 82.8 us -> 65.4 us  [summed_half(): return (value + lax.ppermute(value, 'mp', X_PAIRS), value)]
    ppermute x3, waiting for transfers between devices: 51.5 us -> 42.3 us  [per_device(): lax.ppermute(pieces, 'seq', [(i, i ^ step) for i in range(8)])]
    unnamed x332 -> x324, local copies, waits for them, and re-layouts: 22.2 us -> 22.6 us
  transfers between devices with their start and end apart: 69 -> 69, of which waited for: 21 -> 23; matrix products, arithmetic and copies ran while one was open for 39% -> 39% of each run, Pallas kernels for 2% -> 2%
where the time goes in v4:
time: 652 us; the launch traced here: 645 us
  waiting for transfers between devices  278 us (43%)
  matrix products  179 us (27%)
  other arithmetic  61.6 us (9%)
  starting transfers between devices  59.7 us (9%)
  local copies, waits for them, and re-layouts  42.7 us (7%)
  between operations  12.5 us (2%)
  Pallas kernels  11.2 us (2%)
    ppermute x8, waiting for transfers between devices, swap_y(): return lax.ppermute(value, 'seq', Y_PAIRS)  91.1 us
    dot_general x18, matrix products, left_dot(): lax.dot_general(left, right, (((0,), (0,)), ((), ())), preferred_element_...  77.1 us
    ppermute x8, waiting for transfers between devices, summed_half(): return (value + lax.ppermute(value, 'mp', X_PAIRS), value)  65.4 us
    dot_general x24, matrix products, right_dot(): lax.dot_general(left, right, (((1,), (1,)), ((), ())), preferred_element_...  51.8 us
    dot_general x19, matrix products, dot(): return jnp.dot(left, right, preferred_element_type=F32)  50 us
    ppermute x3, waiting for transfers between devices, per_device(): lax.ppermute(pieces, 'seq', [(i, i ^ step) for i in range(8)])  42.3 us
    ppermute x5, waiting for transfers between devices, swap_far(): return lax.ppermute(value, 'seq', FAR_PAIRS)  30.9 us
    unnamed x324, local copies, waits for them, and re-layouts  22.6 us
  transfers between devices with their start and end apart: 69, of which 23 were waited for; matrix products, arithmetic and copies ran while one was open for 39% of the time, Pallas kernels for 2%

profile of v4, /device:TPU:0, one launch (start us, length us, event | category | flops | bytes accessed | tf_op | source)
XLA Modules:
  0.0 644.9 jit_solution(9566525274931787758)
XLA Ops:
  3.1 3.7 fusion.1
  11.5 4.0 fusion.32
  35.8 4.4 collective-permute-start.5
  61.5 5.5 fusion.10
  70.3 15.7 %collective-permute-done.9 = f32[128,2048]{1,0:T(8,128)S(1)} collective-permute-done((f32[128,2048]{1,0:T(8,128)S(1)}, f32[128,2048]{1,0:T(8,128)S(1)}, u32[]{:S(2)}, u32[]{:S(2)}) %collective-permute-start.9) | collective-permute-done | bytes 1048608 | tf_op jit(solution)/shard_map/ppermute | solution.py:298
  88.4 18.2 %collective-permute-done.30 = f32[160,2048]{1,0:T(8,128)S(1)} collective-permute-done((f32[160,2048]{1,0:T(8,128)S(1)}, f32[160,2048]{1,0:T(8,128)S(1)}, u32[]{:S(2)}, u32[]{:S(2)}) %collective-permute-start.30) | collective-permute-done | bytes 1310752 | tf_op jit(solution)/shard_map/ppermute | solution.py:353
  106.7 6.6 %collective-permute-done.17 = f32[160,2048]{1,0:T(8,128)S(1)} collective-permute-done((f32[160,2048]{1,0:T(8,128)S(1)}, f32[160,2048]{1,0:T(8,128)S(1)}, u32[]{:S(2)}, u32[]{:S(2)}) %collective-permute-start.17) | collective-permute-done | bytes 1310752 | tf_op jit(solution)/shard_map/ppermute | solution.py:298
  117.8 4.6 multiply_convert_fusion.11
  137.2 3.4 fusion.179
  145.0 3.8 multiply_convert_fusion.5
  153.0 3.1 collective-permute-done.26.refs_0_
  163.6 3.6 multiply_convert_fusion.8
  173.7 4.1 multiply_convert_fusion.2
  177.8 8.3 %collective-permute-done.12 = f32[128,2048]{1,0:T(8,128)S(1)} collective-permute-done((f32[128,2048]{1,0:T(8,128)S(1)}, f32[128,2048]{1,0:T(8,128)S(1)}, u32[]{:S(2)}, u32[]{:S(2)}) %collective-permute-start.12) | collective-permute-done | bytes 1048608 | tf_op jit(solution)/shard_map/ppermute | solution.py:298
  187.9 3.4 fusion.68
  198.3 4.8 fusion.87
  203.0 4.1 fusion.78
  207.7 6.2 collective-permute-done.24
  219.3 5.3 collective-permute-done.34
  226.5 3.4 convolution_add_fusion.17
  235.6 3.2 fusion.161
  258.5 5.1 fusion.47
  263.7 4.9 convolution_add_fusion.4
  268.7 3.8 fusion.48
  292.2 6.4 collective-permute-done.14
  298.7 4.2 collective-permute-start.52
  315.7 3.1 fusion.7
  318.8 5.2 collective-permute-done.20
  333.3 26.4 %collective-permute-done.52 = f32[1408,256]{1,0:T(8,128)} collective-permute-done((f32[1408,256]{1,0:T(8,128)}, f32[1408,256]{1,0:T(8,128)}, u32[]{:S(2)}, u32[]{:S(2)}) %collective-permute-start.52) | collective-permute-done | bytes 1441824 | tf_op jit(solution)/shard_map/ppermute | solution.py:525
  379.6 17.0 %collective-permute-done.45 = f32[160,2048]{1,0:T(8,128)S(1)} collective-permute-done((f32[160,2048]{1,0:T(8,128)S(1)}, f32[160,2048]{1,0:T(8,128)S(1)}, u32[]{:S(2)}, u32[]{:S(2)}) %collective-permute-start.45) | collective-permute-done | bytes 1310752 | tf_op jit(solution)/shard_map/ppermute | solution.py:298
  399.6 4.3 convolution_add_fusion.5
  404.1 48.3 %collective-permute-done.66 = f32[512,1408]{1,0:T(8,128)S(1)} collective-permute-done((f32[512,1408]{1,0:T(8,128)S(1)}, f32[512,1408]{1,0:T(8,128)S(1)}, u32[]{:S(2)}, u32[]{:S(2)}) %collective-permute-start.66) | collective-permute-done | bytes 2883616 | tf_op jit(solution)/shard_map/ppermute | solution.py:334
  452.4 3.9 convolution_add_fusion.1
  456.2 3.6 collective-permute-start.67
  461.3 19.6 %collective-permute-done.53.refs_1_ = f32[576,1536]{1,0:T(8,128)S(1)} collective-permute-done((f32[576,1536]{1,0:T(8,128)S(1)}, f32[576,1536]{1,0:T(8,128)S(1)}, u32[]{:S(2)}, u32[]{:S(2)}) %collective-permute-start.53) | collective-permute-done | bytes 3538976 | tf_op jit(solution)/shard_map/ppermute | solution.py:596
  492.2 4.4 fusion.50
  496.6 11.9 %fusion.58 = f32[256,1536]{1,0:T(8,128)} fusion(bf16[1152,1024]{1,0:T(8,128)(2,1)} %pad_maximum_fusion.9, s32[]{:T(128)S(6)} %select_n.315, bf16[576,1536]{1,0:T(8,128)(2,1)S(1)} %placed.9, bf16[576,512]{1,0:T(8,128)(2,1)S(1)} %copy-done.111, bf16[576,512]{1,0:T(8,128)(2,1)S(1)} %copy-done.67, bf16[576,512]{1,0:T(8,128)(2,1)S(1)} %copy-done.72), kind=kOutput, calls=%fused_computation.171 | convolution fusion | flops 920125440 | bytes 5701636 | tf_op jit(solution)/shard_map/dot_general | solution.py:26
  513.4 23.0 %collective-permute-done.58 = f32[512,256]{1,0:T(8,128)} collective-permute-done((f32[512,256]{1,0:T(8,128)}, f32[512,256]{1,0:T(8,128)}, u32[]{:S(2)}, u32[]{:S(2)}) %collective-permute-start.58) | collective-permute-done | bytes 524320 | tf_op jit(solution)/shard_map/ppermute | solution.py:334
  544.0 3.2 convolution_add_fusion.7
  552.8 14.5 %collective-permute-done.68 = f32[1408,256]{1,0:T(8,128)} collective-permute-done((f32[1408,256]{1,0:T(8,128)}, f32[1408,256]{1,0:T(8,128)}, u32[]{:S(2)}, u32[]{:S(2)}) %collective-permute-start.68) | collective-permute-done | bytes 1441824 | tf_op jit(solution)/shard_map/ppermute | solution.py:334
  567.3 5.3 fusion.4
  575.2 8.1 %collective-permute-done.59 = f32[8,640]{1,0:T(8,128)S(1)} collective-permute-done((f32[8,640]{1,0:T(8,128)S(1)}, f32[8,640]{1,0:T(8,128)S(1)}, u32[]{:S(2)}, u32[]{:S(2)}) %collective-permute-start.59) | collective-permute-done | bytes 20512 | tf_op jit(solution)/shard_map/ppermute | solution.py:705
  585.0 4.6 collective-permute-done.67
  589.9 4.4 fusion.3
  594.4 16.0 %collective-permute-done.60 = f32[8,640]{1,0:T(8,128)S(1)} collective-permute-done((f32[8,640]{1,0:T(8,128)S(1)}, f32[8,640]{1,0:T(8,128)S(1)}, u32[]{:S(2)}, u32[]{:S(2)}) %collective-permute-start.60) | collective-permute-done | bytes 20512 | tf_op jit(solution)/shard_map/ppermute | solution.py:705
  612.0 5.0 fusion.2
  617.0 18.2 %collective-permute-done.61 = f32[8,640]{1,0:T(8,128)S(1)} collective-permute-done((f32[8,640]{1,0:T(8,128)S(1)}, f32[8,640]{1,0:T(8,128)S(1)}, u32[]{:S(2)}, u32[]{:S(2)}) %collective-permute-start.61) | collective-permute-done | bytes 20512 | tf_op jit(solution)/shard_map/ppermute | solution.py:705
  639.1 4.3 fusion.5
  (617 shorter events, 234.4 us)
Async XLA Ops:
  8.1 210.8 %collective-permute-start.48 = (f32[288,1024]{1,0:T(8,128)}, f32[288,1024]{1,0:T(8,128)}, u32[]{:S(2)}, u32[]{:S(2)}) collective-permute-start(f32[288,1024]{1,0:T(8,128)} %pad_maximum_fusion.13), channel_id=1, source_target_pairs={{0,8},{4,12},{8,0},{12,4},{16,24},{20,28},{24,16},{28,20},{1,9},{5... | collective-permute-start | bytes 3538952 | tf_op jit(solution)/shard_map/ppermute | solution.py:353
  47.4 21.6 %collective-permute-start.16 = (f32[160,2048]{1,0:T(8,128)}, f32[160,2048]{1,0:T(8,128)S(1)}, u32[]{:S(2)}, u32[]{:S(2)}) collective-permute-start(f32[160,2048]{1,0:T(8,128)} %copy-done.81), channel_id=1, source_target_pairs={{0,1},{1,0},{2,3},{3,2},{4,5},{5,4},{6,7},{7,6},{8,9},{9,8},{10,11... | collective-permute-start | bytes 3932168 | tf_op jit(solution)/shard_map/ppermute | solution.py:297
  52.4 35.8 %collective-permute-start.32 = (f32[128,2048]{1,0:T(8,128)S(1)}, f32[128,2048]{1,0:T(8,128)S(1)}, u32[]{:S(2)}, u32[]{:S(2)}) collective-permute-start(f32[128,2048]{1,0:T(8,128)S(1)} %get-tuple-element.47), channel_id=1, source_target_pairs={{0,8},{4,12},{8,0},{12,4},{16,24},{20,28},{24,16},{28,20},{1,9},{5... | collective-permute-start | bytes 3145736 | tf_op jit(solution)/shard_map/ppermute | solution.py:353
  57.1 49.5 %collective-permute-start.30 = (f32[160,2048]{1,0:T(8,128)S(1)}, f32[160,2048]{1,0:T(8,128)S(1)}, u32[]{:S(2)}, u32[]{:S(2)}) collective-permute-start(f32[160,2048]{1,0:T(8,128)S(1)} %get-tuple-element.49), channel_id=1, source_target_pairs={{0,8},{4,12},{8,0},{12,4},{16,24},{20,28},{24,16},{28,20},{1,9},{5... | collective-permute-start | bytes 3932168 | tf_op jit(solution)/shard_map/ppermute | solution.py:353
  60.0 26.1 %collective-permute-start.9 = (f32[128,2048]{1,0:T(8,128)S(1)}, f32[128,2048]{1,0:T(8,128)S(1)}, u32[]{:S(2)}, u32[]{:S(2)}) collective-permute-start(f32[128,2048]{1,0:T(8,128)S(1)} %convolution_add_fusion.20), channel_id=1, source_target_pairs={{0,2},{1,3},{2,0},{3,1},{4,6},{5,7},{6,4},{7,5},{8,10},{9,11},{10,... | collective-permute-start | bytes 3145736 | tf_op jit(solution)/shard_map/ppermute | solution.py:298
  69.6 43.8 %collective-permute-start.17 = (f32[160,2048]{1,0:T(8,128)S(1)}, f32[160,2048]{1,0:T(8,128)S(1)}, u32[]{:S(2)}, u32[]{:S(2)}) collective-permute-start(f32[160,2048]{1,0:T(8,128)S(1)} %convolution_add_fusion.12), channel_id=1, source_target_pairs={{0,2},{1,3},{2,0},{3,1},{4,6},{5,7},{6,4},{7,5},{8,10},{9,11},{10,... | collective-permute-start | bytes 3932168 | tf_op jit(solution)/shard_map/ppermute | solution.py:298
  86.9 46.7 %collective-permute-start.28 = (f32[128,2048]{1,0:T(8,128)S(1)}, f32[128,2048]{1,0:T(8,128)S(1)}, u32[]{:S(2)}, u32[]{:S(2)}) collective-permute-start(f32[128,2048]{1,0:T(8,128)S(1)} %get-tuple-element.108), channel_id=1, source_target_pairs={{0,8},{4,12},{8,0},{12,4},{16,24},{20,28},{24,16},{28,20},{1,9},{5... | collective-permute-start | bytes 3145736 | tf_op jit(solution)/shard_map/ppermute | solution.py:353
  88.2 26.0 %collective-permute-start.10 = (f32[128,2048]{1,0:T(8,128)S(1)}, f32[128,2048]{1,0:T(8,128)S(1)}, u32[]{:S(2)}, u32[]{:S(2)}) collective-permute-start(f32[128,2048]{1,0:T(8,128)S(1)} %get-tuple-element.108), channel_id=1, source_target_pairs={{0,1},{1,0},{2,3},{3,2},{4,5},{5,4},{6,7},{7,6},{8,9},{9,8},{10,11... | collective-permute-start | bytes 3145736 | tf_op jit(solution)/shard_map/ppermute | solution.py:331
  106.6 21.1 %collective-permute-start.33 = (f32[128,2048]{1,0:T(8,128)S(1)}, f32[128,2048]{1,0:T(8,128)S(1)}, u32[]{:S(2)}, u32[]{:S(2)}) collective-permute-start(f32[128,2048]{1,0:T(8,128)S(1)} %broadcast_add_fusion.1.refs_1_), channel_id=1, source_target_pairs={{0,1},{1,0},{2,3},{3,2},{4,5},{5,4},{6,7},{7,6},{8,9},{9,8},{10,11... | collective-permute-start | bytes 3145736 | tf_op jit(solution)/shard_map/ppermute | solution.py:331
  113.3 20.4 %collective-permute-start.31 = (f32[160,2048]{1,0:T(8,128)S(1)}, f32[160,2048]{1,0:T(8,128)S(1)}, u32[]{:S(2)}, u32[]{:S(2)}) collective-permute-start(f32[160,2048]{1,0:T(8,128)S(1)} %broadcast_add_fusion.refs_1_), channel_id=1, source_target_pairs={{0,1},{1,0},{2,3},{3,2},{4,5},{5,4},{6,7},{7,6},{8,9},{9,8},{10,11... | collective-permute-start | bytes 3932168 | tf_op jit(solution)/shard_map/ppermute | solution.py:331
  114.3 41.8 %collective-permute-start.26 = (f32[160,2048]{1,0:T(8,128)S(1)}, f32[160,2048]{1,0:T(8,128)S(1)}, u32[]{:S(2)}, u32[]{:S(2)}) collective-permute-start(f32[160,2048]{1,0:T(8,128)S(1)} %get-tuple-element.112), channel_id=1, source_target_pairs={{0,8},{4,12},{8,0},{12,4},{16,24},{20,28},{24,16},{28,20},{1,9},{5... | collective-permute-start | bytes 3932168 | tf_op jit(solution)/shard_map/ppermute | solution.py:353
  133.6 24.5 %collective-permute-start.11 = (f32[128,2048]{1,0:T(8,128)}, f32[128,2048]{1,0:T(8,128)S(1)}, u32[]{:S(2)}, u32[]{:S(2)}) collective-permute-start(f32[128,2048]{1,0:T(8,128)} %convolution_add_fusion.18), channel_id=1, source_target_pairs={{0,1},{1,0},{2,3},{3,2},{4,5},{5,4},{6,7},{7,6},{8,9},{9,8},{10,11... | collective-permute-start | bytes 3145736 | tf_op jit(solution)/shard_map/ppermute | solution.py:297
  133.7 27.8 %collective-permute-start.29 = (f32[128,2048]{1,0:T(8,128)S(1)}, f32[128,2048]{1,0:T(8,128)S(1)}, u32[]{:S(2)}, u32[]{:S(2)}) collective-permute-start(f32[128,2048]{1,0:T(8,128)S(1)} %collective-permute-done.28.refs_0_), channel_id=1, source_target_pairs={{0,1},{1,0},{2,3},{3,2},{4,5},{5,4},{6,7},{7,6},{8,9},{9,8},{10,11... | collective-permute-start | bytes 3145736 | tf_op jit(solution)/shard_map/ppermute | solution.py:331
  160.1 26.0 %collective-permute-start.12 = (f32[128,2048]{1,0:T(8,128)S(1)}, f32[128,2048]{1,0:T(8,128)S(1)}, u32[]{:S(2)}, u32[]{:S(2)}) collective-permute-start(f32[128,2048]{1,0:T(8,128)S(1)} %fusion.9), channel_id=1, source_target_pairs={{0,2},{1,3},{2,0},{3,1},{4,6},{5,7},{6,4},{7,5},{8,10},{9,11},{10,... | collective-permute-start | bytes 3145736 | tf_op jit(solution)/shard_map/ppermute | solution.py:298
  173.0 40.9 %collective-permute-start.24 = (f32[160,2048]{1,0:T(8,128)}, f32[160,2048]{1,0:T(8,128)}, u32[]{:S(2)}, u32[]{:S(2)}) collective-permute-start(f32[160,2048]{1,0:T(8,128)} %fusion.8), channel_id=1, source_target_pairs={{0,2},{1,3},{2,0},{3,1},{4,6},{5,7},{6,4},{7,5},{8,10},{9,11},{10,... | collective-permute-start | bytes 3932168 | tf_op jit(solution)/shard_map/ppermute | solution.py:298
  191.3 33.3 %collective-permute-start.34 = (f32[1408,256]{1,0:T(8,128)}, f32[1408,256]{1,0:T(8,128)}, u32[]{:S(2)}, u32[]{:S(2)}) collective-permute-start(f32[1408,256]{1,0:T(8,128)} %fusion.68), channel_id=1, source_target_pairs={{0,4},{4,0},{8,12},{12,8},{16,20},{20,16},{24,28},{28,24},{1,5},{5... | collective-permute-start | bytes 4325384 | tf_op jit(solution)/shard_map/ppermute | solution.py:334
  203.0 23.4 %collective-permute-start.13 = (f32[128,2048]{1,0:T(8,128)}, f32[128,2048]{1,0:T(8,128)}, u32[]{:S(2)}, u32[]{:S(2)}) collective-permute-start(f32[128,2048]{1,0:T(8,128)} %fusion.87), channel_id=1, source_target_pairs={{0,1},{1,0},{2,3},{3,2},{4,5},{5,4},{6,7},{7,6},{8,9},{9,8},{10,11... | collective-permute-start | bytes 3145736 | tf_op jit(solution)/shard_map/ppermute | solution.py:297
  207.2 22.8 %collective-permute-start.19 = (f32[160,2048]{1,0:T(8,128)S(1)}, f32[160,2048]{1,0:T(8,128)S(1)}, u32[]{:S(2)}, u32[]{:S(2)}) collective-permute-start(f32[160,2048]{1,0:T(8,128)S(1)} %fusion.78), channel_id=1, source_target_pairs={{0,1},{1,0},{2,3},{3,2},{4,5},{5,4},{6,7},{7,6},{8,9},{9,8},{10,11... | collective-permute-start | bytes 3932168 | tf_op jit(solution)/shard_map/ppermute | solution.py:297
  218.9 92.0 %collective-permute-start.55 = (f32[576,512]{1,0:T(8,128)}, f32[576,512]{1,0:T(8,128)S(1)}, u32[]{:S(2)}, u32[]{:S(2)}) collective-permute-start(f32[576,512]{1,0:T(8,128)} %pad_maximum_fusion.15), channel_id=1, source_target_pairs={{0,8},{4,12},{8,0},{12,4},{16,24},{20,28},{24,16},{28,20},{1,9},{5... | collective-permute-start | bytes 3538952 | tf_op jit(solution)/shard_map/ppermute | solution.py:596
  224.6 66.3 %collective-permute-start.49 = (f32[288,1024]{1,0:T(8,128)}, f32[288,1024]{1,0:T(8,128)}, u32[]{:S(2)}, u32[]{:S(2)}) collective-permute-start(f32[288,1024]{1,0:T(8,128)} %collective-permute-done.48.refs_1_), channel_id=1, source_target_pairs={{0,1},{1,0},{2,3},{3,2},{4,5},{5,4},{6,7},{7,6},{8,9},{9,8},{10,11... | collective-permute-start | bytes 3538952 | tf_op jit(solution)/shard_map/ppermute | solution.py:331
  252.6 19.9 %collective-permute-start.40 = (f32[2,512]{1,0:T(2,128)S(1)}, f32[2,512]{1,0:T(2,128)S(1)}, u32[]{:S(2)}, u32[]{:S(2)}) collective-permute-start(f32[2,512]{1,0:T(2,128)S(1)} %pad_maximum_fusion.23), channel_id=1, source_target_pairs={{24,0},{28,4},{25,1},{29,5},{26,2},{30,6},{27,3},{31,7}} | collective-permute-start | bytes 12296 | tf_op jit(solution)/shard_map/ppermute | solution.py:285
  253.9 20.0 %collective-permute-start.39 = (f32[2,512]{1,0:T(2,128)S(1)}, f32[2,512]{1,0:T(2,128)S(1)}, u32[]{:S(2)}, u32[]{:S(2)}) collective-permute-start(f32[2,512]{1,0:T(2,128)S(1)} %pad_maximum_fusion.23), channel_id=1, source_target_pairs={{16,0},{20,4},{24,8},{28,12},{17,1},{21,5},{25,9},{29,13},{18,2},{... | collective-permute-start | bytes 12296 | tf_op jit(solution)/shard_map/ppermute | solution.py:285
  255.2 19.4 %collective-permute-start.38 = (f32[2,512]{1,0:T(2,128)S(1)}, f32[2,512]{1,0:T(2,128)S(1)}, u32[]{:S(2)}, u32[]{:S(2)}) collective-permute-start(f32[2,512]{1,0:T(2,128)S(1)} %pad_maximum_fusion.23), channel_id=1, source_target_pairs={{8,0},{12,4},{16,8},{20,12},{24,16},{28,20},{9,1},{13,5},{17,9},{2... | collective-permute-start | bytes 12296 | tf_op jit(solution)/shard_map/ppermute | solution.py:285
  272.5 26.2 %collective-permute-start.14 = (f32[128,2048]{1,0:T(8,128)S(1)}, f32[128,2048]{1,0:T(8,128)S(1)}, u32[]{:S(2)}, u32[]{:S(2)}) collective-permute-start(f32[128,2048]{1,0:T(8,128)S(1)} %copy-done.61), channel_id=1, source_target_pairs={{0,2},{1,3},{2,0},{3,1},{4,6},{5,7},{6,4},{7,5},{8,10},{9,11},{10,... | collective-permute-start | bytes 3145736 | tf_op jit(solution)/shard_map/ppermute | solution.py:298
  273.9 50.0 %collective-permute-start.20 = (f32[160,2048]{1,0:T(8,128)}, f32[160,2048]{1,0:T(8,128)}, u32[]{:S(2)}, u32[]{:S(2)}) collective-permute-start(f32[160,2048]{1,0:T(8,128)} %convolution_add_fusion.23), channel_id=1, source_target_pairs={{0,2},{1,3},{2,0},{3,1},{4,6},{5,7},{6,4},{7,5},{8,10},{9,11},{10,... | collective-permute-start | bytes 3932168 | tf_op jit(solution)/shard_map/ppermute | solution.py:298
  283.4 29.6 %collective-permute-start.41 = (f32[128,2048]{1,0:T(8,128)}, f32[128,2048]{1,0:T(8,128)}, u32[]{:S(2)}, u32[]{:S(2)}) collective-permute-start(f32[128,2048]{1,0:T(8,128)} %convolution_add_fusion.13), channel_id=1, source_target_pairs={{0,1},{1,0},{2,3},{3,2},{4,5},{5,4},{6,7},{7,6},{8,9},{9,8},{10,11... | collective-permute-start | bytes 3145736 | tf_op jit(solution)/shard_map/ppermute | solution.py:297
  290.9 38.0 %collective-permute-start.44 = (f32[160,2048]{1,0:T(8,128)}, f32[160,2048]{1,0:T(8,128)}, u32[]{:S(2)}, u32[]{:S(2)}) collective-permute-start(f32[160,2048]{1,0:T(8,128)} %convolution_add_fusion.8), channel_id=1, source_target_pairs={{0,1},{1,0},{2,3},{3,2},{4,5},{5,4},{6,7},{7,6},{8,9},{9,8},{10,11... | collective-permute-start | bytes 3932168 | tf_op jit(solution)/shard_map/ppermute | solution.py:297
  298.7 60.9 %collective-permute-start.52 = (f32[1408,256]{1,0:T(8,128)}, f32[1408,256]{1,0:T(8,128)}, u32[]{:S(2)}, u32[]{:S(2)}) collective-permute-start(f32[1408,256]{1,0:T(8,128)} %convolution_add_fusion.4), channel_id=1, source_target_pairs={{0,16},{4,20},{8,24},{12,28},{16,0},{20,4},{24,8},{28,12},{1,17},{... | collective-permute-start | bytes 4325384 | tf_op jit(solution)/shard_map/ppermute | solution.py:525
  310.9 52.3 %collective-permute-start.56 = (f32[288,1024]{1,0:T(8,128)}, f32[288,1024]{1,0:T(8,128)}, u32[]{:S(2)}, u32[]{:S(2)}) collective-permute-start(f32[288,1024]{1,0:T(8,128)} %pad_maximum_fusion.17), channel_id=1, source_target_pairs={{0,8},{4,12},{8,0},{12,4},{16,24},{20,28},{24,16},{28,20},{1,9},{5... | collective-permute-start | bytes 3538952 | tf_op jit(solution)/shard_map/ppermute | solution.py:353
  312.9 50.4 %collective-permute-start.15 = (f32[128,2048]{1,0:T(8,128)}, f32[128,2048]{1,0:T(8,128)}, u32[]{:S(2)}, u32[]{:S(2)}) collective-permute-start(f32[128,2048]{1,0:T(8,128)} %add.765), channel_id=1, source_target_pairs={{0,1},{1,0},{2,3},{3,2},{4,5},{5,4},{6,7},{7,6},{8,9},{9,8},{10,11... | collective-permute-start | bytes 3145736 | tf_op jit(solution)/shard_map/ppermute | solution.py:331
  323.9 41.9 %collective-permute-start.42 = (f32[128,2048]{1,0:T(8,128)}, f32[128,2048]{1,0:T(8,128)}, u32[]{:S(2)}, u32[]{:S(2)}) collective-permute-start(f32[128,2048]{1,0:T(8,128)} %fusion.7), channel_id=1, source_target_pairs={{0,2},{1,3},{2,0},{3,1},{4,6},{5,7},{6,4},{7,5},{8,10},{9,11},{10,... | collective-permute-start | bytes 3145736 | tf_op jit(solution)/shard_map/ppermute | solution.py:298
  329.0 70.4 %collective-permute-start.50 = (f32[512,1408]{1,0:T(8,128)}, f32[512,1408]{1,0:T(8,128)S(1)}, u32[]{:S(2)}, u32[]{:S(2)}) collective-permute-start(f32[512,1408]{1,0:T(8,128)} %fusion.48), channel_id=1, source_target_pairs={{0,4},{4,0},{8,12},{12,8},{16,20},{20,16},{24,28},{28,24},{1,5},{5... | collective-permute-start | bytes 8650760 | tf_op jit(solution)/shard_map/ppermute | solution.py:334
  359.6 92.7 %collective-permute-start.66 = (f32[512,1408]{1,0:T(8,128)S(1)}, f32[512,1408]{1,0:T(8,128)S(1)}, u32[]{:S(2)}, u32[]{:S(2)}) collective-permute-start(f32[512,1408]{1,0:T(8,128)S(1)} %copy-done.131), channel_id=1, source_target_pairs={{0,4},{4,0},{8,12},{12,8},{16,20},{20,16},{24,28},{28,24},{1,5},{5... | collective-permute-start | bytes 8650760 | tf_op jit(solution)/shard_map/ppermute | solution.py:334
  365.8 30.7 %collective-permute-start.45 = (f32[160,2048]{1,0:T(8,128)S(1)}, f32[160,2048]{1,0:T(8,128)S(1)}, u32[]{:S(2)}, u32[]{:S(2)}) collective-permute-start(f32[160,2048]{1,0:T(8,128)S(1)} %fusion.6), channel_id=1, source_target_pairs={{0,2},{1,3},{2,0},{3,1},{4,6},{5,7},{6,4},{7,5},{8,10},{9,11},{10,... | collective-permute-start | bytes 3932168 | tf_op jit(solution)/shard_map/ppermute | solution.py:298
  371.8 109.1 %collective-permute-start.53 = (f32[576,1536]{1,0:T(8,128)S(1)}, f32[576,1536]{1,0:T(8,128)S(1)}, u32[]{:S(2)}, u32[]{:S(2)}) collective-permute-start(f32[576,1536]{1,0:T(8,128)S(1)} %copy-done.62), channel_id=1, source_target_pairs={{0,8},{4,12},{8,0},{12,4},{16,24},{20,28},{24,16},{28,20},{1,9},{5... | collective-permute-start | bytes 10616840 | tf_op jit(solution)/shard_map/ppermute | solution.py:596
  376.4 83.5 %collective-permute-start.43 = (f32[128,2048]{1,0:T(8,128)S(1)}, f32[128,2048]{1,0:T(8,128)S(1)}, u32[]{:S(2)}, u32[]{:S(2)}) collective-permute-start(f32[128,2048]{1,0:T(8,128)S(1)} %fusion.44), channel_id=1, source_target_pairs={{0,1},{1,0},{2,3},{3,2},{4,5},{5,4},{6,7},{7,6},{8,9},{9,8},{10,11... | collective-permute-start | bytes 3145736 | tf_op jit(solution)/shard_map/ppermute | solution.py:331
  398.8 109.7 %collective-permute-start.46 = (f32[160,2048]{1,0:T(8,128)}, f32[160,2048]{1,0:T(8,128)}, u32[]{:S(2)}, u32[]{:S(2)}) collective-permute-start(f32[160,2048]{1,0:T(8,128)} %fusion.35), channel_id=1, source_target_pairs={{0,1},{1,0},{2,3},{3,2},{4,5},{5,4},{6,7},{7,6},{8,9},{9,8},{10,11... | collective-permute-start | bytes 3932168 | tf_op jit(solution)/shard_map/ppermute | solution.py:331
  404.0 137.0 %collective-permute-start.51 = (f32[256,1408]{1,0:T(8,128)}, f32[256,1408]{1,0:T(8,128)}, u32[]{:S(2)}, u32[]{:S(2)}) collective-permute-start(f32[256,1408]{1,0:T(8,128)} %convolution_add_fusion.5), channel_id=1, source_target_pairs={{0,16},{4,20},{8,24},{12,28},{16,0},{20,4},{24,8},{28,12},{1,17},{... | collective-permute-start | bytes 4325384 | tf_op jit(solution)/shard_map/ppermute | solution.py:525
  456.2 133.3 %collective-permute-start.67 = (f32[256,1408]{1,0:T(8,128)}, f32[256,1408]{1,0:T(8,128)}, u32[]{:S(2)}, u32[]{:S(2)}) collective-permute-start(f32[256,1408]{1,0:T(8,128)} %convolution_add_fusion.1), channel_id=1, source_target_pairs={{0,16},{4,20},{8,24},{12,28},{16,0},{20,4},{24,8},{28,12},{1,17},{... | collective-permute-start | bytes 4325384 | tf_op jit(solution)/shard_map/ppermute | solution.py:525
  487.5 56.5 %collective-permute-start.54 = (f32[256,1536]{1,0:T(8,128)}, f32[256,1536]{1,0:T(8,128)}, u32[]{:S(2)}, u32[]{:S(2)}) collective-permute-start(f32[256,1536]{1,0:T(8,128)} %copy-done.133), channel_id=1, source_target_pairs={{0,4},{4,0},{8,12},{12,8},{16,20},{20,16},{24,28},{28,24},{1,5},{5... | collective-permute-start | bytes 4718600 | tf_op jit(solution)/shard_map/ppermute | solution.py:334
  490.9 45.5 %collective-permute-start.58 = (f32[512,256]{1,0:T(8,128)}, f32[512,256]{1,0:T(8,128)}, u32[]{:S(2)}, u32[]{:S(2)}) collective-permute-start(f32[512,256]{1,0:T(8,128)} %fusion.61), channel_id=1, source_target_pairs={{0,4},{4,0},{8,12},{12,8},{16,20},{20,16},{24,28},{28,24},{1,5},{5... | collective-permute-start | bytes 1572872 | tf_op jit(solution)/shard_map/ppermute | solution.py:334
  508.4 58.9 %collective-permute-start.68 = (f32[1408,256]{1,0:T(8,128)}, f32[1408,256]{1,0:T(8,128)}, u32[]{:S(2)}, u32[]{:S(2)}) collective-permute-start(f32[1408,256]{1,0:T(8,128)} %fusion.50), channel_id=1, source_target_pairs={{0,4},{4,0},{8,12},{12,8},{16,20},{20,16},{24,28},{28,24},{1,5},{5... | collective-permute-start | bytes 4325384 | tf_op jit(solution)/shard_map/ppermute | solution.py:334
  536.4 102.7 %collective-permute-start.62 = (f32[256,1536]{1,0:T(8,128)}, f32[256,1536]{1,0:T(8,128)}, u32[]{:S(2)}, u32[]{:S(2)}) collective-permute-start(f32[256,1536]{1,0:T(8,128)} %fusion.58), channel_id=1, source_target_pairs={{0,4},{4,0},{8,12},{12,8},{16,20},{20,16},{24,28},{28,24},{1,5},{5... | collective-permute-start | bytes 4718600 | tf_op jit(solution)/shard_map/ppermute | solution.py:334
  541.0 95.3 %collective-permute-start.65 = (f32[512,256]{1,0:T(8,128)}, f32[512,256]{1,0:T(8,128)}, u32[]{:S(2)}, u32[]{:S(2)}) collective-permute-start(f32[512,256]{1,0:T(8,128)} %convolution_add_fusion.25), channel_id=1, source_target_pairs={{0,16},{4,20},{8,24},{12,28},{16,0},{20,4},{24,8},{28,12},{1,17},{... | collective-permute-start | bytes 1572872 | tf_op jit(solution)/shard_map/ppermute | solution.py:525
  550.9 88.2 %collective-permute-start.63 = (f32[256,1536]{1,0:T(8,128)}, f32[256,1536]{1,0:T(8,128)}, u32[]{:S(2)}, u32[]{:S(2)}) collective-permute-start(f32[256,1536]{1,0:T(8,128)} %copy-done.132), channel_id=1, source_target_pairs={{0,16},{4,20},{8,24},{12,28},{16,0},{20,4},{24,8},{28,12},{1,17},{... | collective-permute-start | bytes 4718600 | tf_op jit(solution)/shard_map/ppermute | solution.py:525
  583.3 53.1 %collective-permute-start.64 = (f32[512,256]{1,0:T(8,128)}, f32[512,256]{1,0:T(8,128)}, u32[]{:S(2)}, u32[]{:S(2)}) collective-permute-start(f32[512,256]{1,0:T(8,128)} %fusion.55), channel_id=1, source_target_pairs={{0,4},{4,0},{8,12},{12,8},{16,20},{20,16},{24,28},{28,24},{1,5},{5... | collective-permute-start | bytes 1572872 | tf_op jit(solution)/shard_map/ppermute | solution.py:334
  589.6 20.8 %collective-permute-start.60 = (f32[8,640]{1,0:T(8,128)S(1)}, f32[8,640]{1,0:T(8,128)S(1)}, u32[]{:S(2)}, u32[]{:S(2)}) collective-permute-start(f32[8,640]{1,0:T(8,128)S(1)} %add.883), channel_id=1, source_target_pairs={{0,4},{4,0},{8,12},{12,8},{16,20},{20,16},{24,28},{28,24},{1,5},{5... | collective-permute-start | bytes 61448 | tf_op jit(solution)/shard_map/ppermute | solution.py:705
  610.4 24.8 %collective-permute-start.61 = (f32[8,640]{1,0:T(8,128)S(1)}, f32[8,640]{1,0:T(8,128)S(1)}, u32[]{:S(2)}, u32[]{:S(2)}) collective-permute-start(f32[8,640]{1,0:T(8,128)S(1)} %add.884), channel_id=1, source_target_pairs={{0,16},{4,20},{8,24},{12,28},{16,0},{20,4},{24,8},{28,12},{1,17},{... | collective-permute-start | bytes 61448 | tf_op jit(solution)/shard_map/ppermute | solution.py:705
  (182 other events, 1858.7 us)

commit v5 on v4

--- a/solution.py
+++ b/solution.py
@@ -7,7 +7,7 @@
 
 LCHUNK = 256
 norm_eps = 1e-06
-FL = {'cot': (0,), 'cot_ready': (1,), 'prefix': (0,), 'glu': (), 'branch': (1,), 'inner': (0,), 'feed': (0,), 'one': (), 'one_ready': (0,), 'gated': (), 'gated_ready': (0,), 'kernel': 0, 'kernel_rec': 0, 'gate': (0,), 'far_down': (0,), 'far_gate': (0,), 'far_up': (0,), 'joined': (0,), 'near_branch': (), 'branch_ready': (), 'out': (0,), 'far_joined': (1,), 'far_out': (), 'own_down': (1,), 'own_gate': (2,), 'own_up': (2,), 'own_joined': (), 'own_out': (2,), 'end_down': (1, 2), 'end_gate': (1,), 'end_up': (1, 2), 'end_joined': (), 'end_out': (1,), 'sends': 2, 'direct': 0, 'steps': (2, 1, 4), 'dn1': (), 'carried': (), 'suffix': ()}
+FL = {'cot': (1,), 'cot_ready': (1,), 'prefix': (0,), 'glu': (), 'branch': (1,), 'inner': (0,), 'feed': (0,), 'one': (), 'one_ready': (0,), 'gated': (), 'gated_ready': (0,), 'kernel': 0, 'kernel_rec': 0, 'gate': (0,), 'far_down': (0,), 'far_gate': (0,), 'far_up': (0,), 'joined': (0,), 'near_branch': (), 'branch_ready': (), 'out': (0,), 'far_joined': (1,), 'far_out': (), 'own_down': (1,), 'own_gate': (2,), 'own_up': (2,), 'own_joined': (), 'own_out': (2,), 'end_down': (1, 2), 'end_gate': (1,), 'end_up': (1, 2), 'end_joined': (), 'end_out': (1,), 'sends': 2, 'direct': 0, 'steps': (2, 1, 4), 'dn1': (), 'carried': (), 'suffix': ()}
 F32 = jnp.float32
 BF16 = jnp.bfloat16
 

time: 652 us -> 652 us (level)
    unnamed x324 -> x328, local copies, waits for them, and re-layouts: 22.6 us -> 23.2 us
  transfers between devices with their start and end apart: 69 -> 69, of which waited for: 23 -> 24; matrix products, arithmetic and copies ran while one was open for 39% -> 38% of each run, Pallas kernels for 2% -> 2%
where the time goes in v5:
time: 652 us; the launch traced here: 645 us
  waiting for transfers between devices  277 us (42%)
  matrix products  178 us (27%)
  starting transfers between devices  62.6 us (10%)
  other arithmetic  61.8 us (9%)
  local copies, waits for them, and re-layouts  42.8 us (7%)
  between operations  12 us (2%)
  Pallas kernels  11.2 us (2%)
    ppermute x8, waiting for transfers between devices, swap_y(): return lax.ppermute(value, 'seq', Y_PAIRS)  91.9 us
    dot_general x18, matrix products, left_dot(): lax.dot_general(left, right, (((0,), (0,)), ((), ())), preferred_element_...  77.1 us
    ppermute x8, waiting for transfers between devices, summed_half(): return (value + lax.ppermute(value, 'mp', X_PAIRS), value)  64.9 us
    dot_general x24, matrix products, right_dot(): lax.dot_general(left, right, (((1,), (1,)), ((), ())), preferred_element_...  50.8 us
    dot_general x19, matrix products, dot(): return jnp.dot(left, right, preferred_element_type=F32)  50 us
    ppermute x3, waiting for transfers between devices, per_device(): lax.ppermute(pieces, 'seq', [(i, i ^ step) for i in range(8)])  42.3 us
    ppermute x5, waiting for transfers between devices, swap_far(): return lax.ppermute(value, 'seq', FAR_PAIRS)  30.9 us
    unnamed x328, local copies, waits for them, and re-layouts  23.2 us
  transfers between devices with their start and end apart: 69, of which 24 were waited for; matrix products, arithmetic and copies ran while one was open for 38% of the time, Pallas kernels for 2%

profile of v5, /device:TPU:0, one launch (start us, length us, event | category | flops | bytes accessed | tf_op | source)
XLA Modules:
  0.0 645.4 jit_solution(7372979542010558524)
XLA Ops:
  3.1 3.7 fusion.1
  11.5 4.0 fusion.32
  35.8 4.4 collective-permute-start.5
  60.8 5.5 fusion.10
  70.2 15.3 %collective-permute-done.9 = f32[128,2048]{1,0:T(8,128)S(1)} collective-permute-done((f32[128,2048]{1,0:T(8,128)S(1)}, f32[128,2048]{1,0:T(8,128)S(1)}, u32[]{:S(2)}, u32[]{:S(2)}) %collective-permute-start.9) | collective-permute-done | bytes 1048608 | tf_op jit(solution)/shard_map/ppermute | solution.py:298
  88.9 18.1 %collective-permute-done.30 = f32[160,2048]{1,0:T(8,128)S(1)} collective-permute-done((f32[160,2048]{1,0:T(8,128)S(1)}, f32[160,2048]{1,0:T(8,128)S(1)}, u32[]{:S(2)}, u32[]{:S(2)}) %collective-permute-start.30) | collective-permute-done | bytes 1310752 | tf_op jit(solution)/shard_map/ppermute | solution.py:353
  107.2 5.6 collective-permute-done.17
  117.5 4.6 multiply_convert_fusion.11
  136.7 3.5 fusion.179
  144.5 3.8 multiply_convert_fusion.5
  152.6 3.9 collective-permute-done.26.refs_0_
  164.1 3.7 multiply_convert_fusion.8
  173.2 4.1 multiply_convert_fusion.2
  177.3 9.3 %collective-permute-done.12 = f32[128,2048]{1,0:T(8,128)S(1)} collective-permute-done((f32[128,2048]{1,0:T(8,128)S(1)}, f32[128,2048]{1,0:T(8,128)S(1)}, u32[]{:S(2)}, u32[]{:S(2)}) %collective-permute-start.12) | collective-permute-done | bytes 1048608 | tf_op jit(solution)/shard_map/ppermute | solution.py:298
  188.4 3.4 fusion.68
  198.8 4.7 fusion.87
  203.6 4.1 fusion.78
  208.3 6.2 collective-permute-done.24
  219.1 6.1 collective-permute-done.34
  227.0 3.4 convolution_add_fusion.17
  236.1 3.2 fusion.161
  259.1 5.1 fusion.47
  264.2 4.9 convolution_add_fusion.4
  269.2 3.8 fusion.48
  292.8 6.4 collective-permute-done.14
  299.2 4.2 collective-permute-start.52
  316.2 3.1 fusion.7
  319.3 5.2 collective-permute-done.20
  333.8 26.4 %collective-permute-done.52 = f32[1408,256]{1,0:T(8,128)} collective-permute-done((f32[1408,256]{1,0:T(8,128)}, f32[1408,256]{1,0:T(8,128)}, u32[]{:S(2)}, u32[]{:S(2)}) %collective-permute-start.52) | collective-permute-done | bytes 1441824 | tf_op jit(solution)/shard_map/ppermute | solution.py:525
  380.1 17.0 %collective-permute-done.45 = f32[160,2048]{1,0:T(8,128)S(1)} collective-permute-done((f32[160,2048]{1,0:T(8,128)S(1)}, f32[160,2048]{1,0:T(8,128)S(1)}, u32[]{:S(2)}, u32[]{:S(2)}) %collective-permute-start.45) | collective-permute-done | bytes 1310752 | tf_op jit(solution)/shard_map/ppermute | solution.py:298
  400.1 4.3 convolution_add_fusion.5
  404.6 48.3 %collective-permute-done.66 = f32[512,1408]{1,0:T(8,128)S(1)} collective-permute-done((f32[512,1408]{1,0:T(8,128)S(1)}, f32[512,1408]{1,0:T(8,128)S(1)}, u32[]{:S(2)}, u32[]{:S(2)}) %collective-permute-start.66) | collective-permute-done | bytes 2883616 | tf_op jit(solution)/shard_map/ppermute | solution.py:334
  452.9 3.9 convolution_add_fusion.1
  456.8 3.6 collective-permute-start.67
  461.9 19.6 %collective-permute-done.53.refs_1_ = f32[576,1536]{1,0:T(8,128)S(1)} collective-permute-done((f32[576,1536]{1,0:T(8,128)S(1)}, f32[576,1536]{1,0:T(8,128)S(1)}, u32[]{:S(2)}, u32[]{:S(2)}) %collective-permute-start.53) | collective-permute-done | bytes 3538976 | tf_op jit(solution)/shard_map/ppermute | solution.py:596
  492.7 4.4 fusion.50
  497.1 11.9 %fusion.58 = f32[256,1536]{1,0:T(8,128)} fusion(bf16[1152,1024]{1,0:T(8,128)(2,1)} %pad_maximum_fusion.9, s32[]{:T(128)S(6)} %select_n.309, bf16[576,1536]{1,0:T(8,128)(2,1)S(1)} %placed.9, bf16[576,512]{1,0:T(8,128)(2,1)S(1)} %copy-done.113, bf16[576,512]{1,0:T(8,128)(2,1)S(1)} %copy-done.68, bf16[576,512]{1,0:T(8,128)(2,1)S(1)} %copy-done.73), kind=kOutput, calls=%fused_computation.171 | convolution fusion | flops 920125440 | bytes 5701636 | tf_op jit(solution)/shard_map/dot_general | solution.py:26
  514.0 23.0 %collective-permute-done.58 = f32[512,256]{1,0:T(8,128)} collective-permute-done((f32[512,256]{1,0:T(8,128)}, f32[512,256]{1,0:T(8,128)}, u32[]{:S(2)}, u32[]{:S(2)}) %collective-permute-start.58) | collective-permute-done | bytes 524320 | tf_op jit(solution)/shard_map/ppermute | solution.py:334
  544.6 3.2 convolution_add_fusion.7
  553.3 14.5 %collective-permute-done.68 = f32[1408,256]{1,0:T(8,128)} collective-permute-done((f32[1408,256]{1,0:T(8,128)}, f32[1408,256]{1,0:T(8,128)}, u32[]{:S(2)}, u32[]{:S(2)}) %collective-permute-start.68) | collective-permute-done | bytes 1441824 | tf_op jit(solution)/shard_map/ppermute | solution.py:334
  567.8 5.3 fusion.4
  575.7 8.2 %collective-permute-done.59 = f32[8,640]{1,0:T(8,128)S(1)} collective-permute-done((f32[8,640]{1,0:T(8,128)S(1)}, f32[8,640]{1,0:T(8,128)S(1)}, u32[]{:S(2)}, u32[]{:S(2)}) %collective-permute-start.59) | collective-permute-done | bytes 20512 | tf_op jit(solution)/shard_map/ppermute | solution.py:705
  585.5 4.6 collective-permute-done.67
  590.5 4.4 fusion.3
  595.0 15.9 %collective-permute-done.60 = f32[8,640]{1,0:T(8,128)S(1)} collective-permute-done((f32[8,640]{1,0:T(8,128)S(1)}, f32[8,640]{1,0:T(8,128)S(1)}, u32[]{:S(2)}, u32[]{:S(2)}) %collective-permute-start.60) | collective-permute-done | bytes 20512 | tf_op jit(solution)/shard_map/ppermute | solution.py:705
  612.5 5.0 fusion.2
  617.5 18.2 %collective-permute-done.61 = f32[8,640]{1,0:T(8,128)S(1)} collective-permute-done((f32[8,640]{1,0:T(8,128)S(1)}, f32[8,640]{1,0:T(8,128)S(1)}, u32[]{:S(2)}, u32[]{:S(2)}) %collective-permute-start.61) | collective-permute-done | bytes 20512 | tf_op jit(solution)/shard_map/ppermute | solution.py:705
  639.6 4.3 fusion.5
  (619 shorter events, 234.5 us)
Async XLA Ops:
  8.1 210.6 %collective-permute-start.48 = (f32[288,1024]{1,0:T(8,128)}, f32[288,1024]{1,0:T(8,128)}, u32[]{:S(2)}, u32[]{:S(2)}) collective-permute-start(f32[288,1024]{1,0:T(8,128)} %pad_maximum_fusion.13), channel_id=1, source_target_pairs={{0,8},{4,12},{8,0},{12,4},{16,24},{20,28},{24,16},{28,20},{1,9},{5... | collective-permute-start | bytes 3538952 | tf_op jit(solution)/shard_map/ppermute | solution.py:353
  49.9 18.4 %collective-permute-start.16 = (f32[160,2048]{1,0:T(8,128)}, f32[160,2048]{1,0:T(8,128)S(1)}, u32[]{:S(2)}, u32[]{:S(2)}) collective-permute-start(f32[160,2048]{1,0:T(8,128)} %copy-done.82), channel_id=1, source_target_pairs={{0,1},{1,0},{2,3},{3,2},{4,5},{5,4},{6,7},{7,6},{8,9},{9,8},{10,11... | collective-permute-start | bytes 3932168 | tf_op jit(solution)/shard_map/ppermute | solution.py:297
  52.9 36.0 %collective-permute-start.32 = (f32[128,2048]{1,0:T(8,128)S(1)}, f32[128,2048]{1,0:T(8,128)S(1)}, u32[]{:S(2)}, u32[]{:S(2)}) collective-permute-start(f32[128,2048]{1,0:T(8,128)S(1)} %get-tuple-element.47), channel_id=1, source_target_pairs={{0,8},{4,12},{8,0},{12,4},{16,24},{20,28},{24,16},{28,20},{1,9},{5... | collective-permute-start | bytes 3145736 | tf_op jit(solution)/shard_map/ppermute | solution.py:353
  57.6 49.4 %collective-permute-start.30 = (f32[160,2048]{1,0:T(8,128)S(1)}, f32[160,2048]{1,0:T(8,128)S(1)}, u32[]{:S(2)}, u32[]{:S(2)}) collective-permute-start(f32[160,2048]{1,0:T(8,128)S(1)} %get-tuple-element.49), channel_id=1, source_target_pairs={{0,8},{4,12},{8,0},{12,4},{16,24},{20,28},{24,16},{28,20},{1,9},{5... | collective-permute-start | bytes 3932168 | tf_op jit(solution)/shard_map/ppermute | solution.py:353
  59.4 26.1 %collective-permute-start.9 = (f32[128,2048]{1,0:T(8,128)S(1)}, f32[128,2048]{1,0:T(8,128)S(1)}, u32[]{:S(2)}, u32[]{:S(2)}) collective-permute-start(f32[128,2048]{1,0:T(8,128)S(1)} %convolution_add_fusion.20), channel_id=1, source_target_pairs={{0,2},{1,3},{2,0},{3,1},{4,6},{5,7},{6,4},{7,5},{8,10},{9,11},{10,... | collective-permute-start | bytes 3145736 | tf_op jit(solution)/shard_map/ppermute | solution.py:298
  68.8 43.9 %collective-permute-start.17 = (f32[160,2048]{1,0:T(8,128)S(1)}, f32[160,2048]{1,0:T(8,128)S(1)}, u32[]{:S(2)}, u32[]{:S(2)}) collective-permute-start(f32[160,2048]{1,0:T(8,128)S(1)} %convolution_add_fusion.12), channel_id=1, source_target_pairs={{0,2},{1,3},{2,0},{3,1},{4,6},{5,7},{6,4},{7,5},{8,10},{9,11},{10,... | collective-permute-start | bytes 3932168 | tf_op jit(solution)/shard_map/ppermute | solution.py:298
  86.4 46.7 %collective-permute-start.28 = (f32[128,2048]{1,0:T(8,128)S(1)}, f32[128,2048]{1,0:T(8,128)S(1)}, u32[]{:S(2)}, u32[]{:S(2)}) collective-permute-start(f32[128,2048]{1,0:T(8,128)S(1)} %get-tuple-element.106), channel_id=1, source_target_pairs={{0,8},{4,12},{8,0},{12,4},{16,24},{20,28},{24,16},{28,20},{1,9},{5... | collective-permute-start | bytes 3145736 | tf_op jit(solution)/shard_map/ppermute | solution.py:353
  88.8 24.9 %collective-permute-start.10 = (f32[128,2048]{1,0:T(8,128)S(1)}, f32[128,2048]{1,0:T(8,128)S(1)}, u32[]{:S(2)}, u32[]{:S(2)}) collective-permute-start(f32[128,2048]{1,0:T(8,128)S(1)} %get-tuple-element.106), channel_id=1, source_target_pairs={{0,1},{1,0},{2,3},{3,2},{4,5},{5,4},{6,7},{7,6},{8,9},{9,8},{10,11... | collective-permute-start | bytes 3145736 | tf_op jit(solution)/shard_map/ppermute | solution.py:331
  107.1 20.3 %collective-permute-start.33 = (f32[128,2048]{1,0:T(8,128)S(1)}, f32[128,2048]{1,0:T(8,128)S(1)}, u32[]{:S(2)}, u32[]{:S(2)}) collective-permute-start(f32[128,2048]{1,0:T(8,128)S(1)} %broadcast_add_fusion.1.refs_1_), channel_id=1, source_target_pairs={{0,1},{1,0},{2,3},{3,2},{4,5},{5,4},{6,7},{7,6},{8,9},{9,8},{10,11... | collective-permute-start | bytes 3145736 | tf_op jit(solution)/shard_map/ppermute | solution.py:331
  112.8 20.6 %collective-permute-start.31 = (f32[160,2048]{1,0:T(8,128)S(1)}, f32[160,2048]{1,0:T(8,128)S(1)}, u32[]{:S(2)}, u32[]{:S(2)}) collective-permute-start(f32[160,2048]{1,0:T(8,128)S(1)} %broadcast_add_fusion.refs_1_), channel_id=1, source_target_pairs={{0,1},{1,0},{2,3},{3,2},{4,5},{5,4},{6,7},{7,6},{8,9},{9,8},{10,11... | collective-permute-start | bytes 3932168 | tf_op jit(solution)/shard_map/ppermute | solution.py:331
  113.8 42.8 %collective-permute-start.26 = (f32[160,2048]{1,0:T(8,128)S(1)}, f32[160,2048]{1,0:T(8,128)S(1)}, u32[]{:S(2)}, u32[]{:S(2)}) collective-permute-start(f32[160,2048]{1,0:T(8,128)S(1)} %get-tuple-element.110), channel_id=1, source_target_pairs={{0,8},{4,12},{8,0},{12,4},{16,24},{20,28},{24,16},{28,20},{1,9},{5... | collective-permute-start | bytes 3932168 | tf_op jit(solution)/shard_map/ppermute | solution.py:353
  133.1 25.5 %collective-permute-start.11 = (f32[128,2048]{1,0:T(8,128)}, f32[128,2048]{1,0:T(8,128)S(1)}, u32[]{:S(2)}, u32[]{:S(2)}) collective-permute-start(f32[128,2048]{1,0:T(8,128)} %convolution_add_fusion.18), channel_id=1, source_target_pairs={{0,1},{1,0},{2,3},{3,2},{4,5},{5,4},{6,7},{7,6},{8,9},{9,8},{10,11... | collective-permute-start | bytes 3145736 | tf_op jit(solution)/shard_map/ppermute | solution.py:297
  133.4 28.6 %collective-permute-start.29 = (f32[128,2048]{1,0:T(8,128)S(1)}, f32[128,2048]{1,0:T(8,128)S(1)}, u32[]{:S(2)}, u32[]{:S(2)}) collective-permute-start(f32[128,2048]{1,0:T(8,128)S(1)} %collective-permute-done.28.refs_0_), channel_id=1, source_target_pairs={{0,1},{1,0},{2,3},{3,2},{4,5},{5,4},{6,7},{7,6},{8,9},{9,8},{10,11... | collective-permute-start | bytes 3145736 | tf_op jit(solution)/shard_map/ppermute | solution.py:331
  160.6 26.0 %collective-permute-start.12 = (f32[128,2048]{1,0:T(8,128)S(1)}, f32[128,2048]{1,0:T(8,128)S(1)}, u32[]{:S(2)}, u32[]{:S(2)}) collective-permute-start(f32[128,2048]{1,0:T(8,128)S(1)} %fusion.9), channel_id=1, source_target_pairs={{0,2},{1,3},{2,0},{3,1},{4,6},{5,7},{6,4},{7,5},{8,10},{9,11},{10,... | collective-permute-start | bytes 3145736 | tf_op jit(solution)/shard_map/ppermute | solution.py:298
  172.5 42.0 %collective-permute-start.24 = (f32[160,2048]{1,0:T(8,128)S(1)}, f32[160,2048]{1,0:T(8,128)}, u32[]{:S(2)}, u32[]{:S(2)}) collective-permute-start(f32[160,2048]{1,0:T(8,128)S(1)} %fusion.8), channel_id=1, source_target_pairs={{0,2},{1,3},{2,0},{3,1},{4,6},{5,7},{6,4},{7,5},{8,10},{9,11},{10,... | collective-permute-start | bytes 3932168 | tf_op jit(solution)/shard_map/ppermute | solution.py:298
  191.8 33.3 %collective-permute-start.34 = (f32[1408,256]{1,0:T(8,128)}, f32[1408,256]{1,0:T(8,128)}, u32[]{:S(2)}, u32[]{:S(2)}) collective-permute-start(f32[1408,256]{1,0:T(8,128)} %fusion.68), channel_id=1, source_target_pairs={{0,4},{4,0},{8,12},{12,8},{16,20},{20,16},{24,28},{28,24},{1,5},{5... | collective-permute-start | bytes 4325384 | tf_op jit(solution)/shard_map/ppermute | solution.py:334
  203.6 23.4 %collective-permute-start.13 = (f32[128,2048]{1,0:T(8,128)}, f32[128,2048]{1,0:T(8,128)}, u32[]{:S(2)}, u32[]{:S(2)}) collective-permute-start(f32[128,2048]{1,0:T(8,128)} %fusion.87), channel_id=1, source_target_pairs={{0,1},{1,0},{2,3},{3,2},{4,5},{5,4},{6,7},{7,6},{8,9},{9,8},{10,11... | collective-permute-start | bytes 3145736 | tf_op jit(solution)/shard_map/ppermute | solution.py:297
  207.7 22.7 %collective-permute-start.19 = (f32[160,2048]{1,0:T(8,128)S(1)}, f32[160,2048]{1,0:T(8,128)S(1)}, u32[]{:S(2)}, u32[]{:S(2)}) collective-permute-start(f32[160,2048]{1,0:T(8,128)S(1)} %fusion.78), channel_id=1, source_target_pairs={{0,1},{1,0},{2,3},{3,2},{4,5},{5,4},{6,7},{7,6},{8,9},{9,8},{10,11... | collective-permute-start | bytes 3932168 | tf_op jit(solution)/shard_map/ppermute | solution.py:297
  218.7 92.7 %collective-permute-start.55 = (f32[576,512]{1,0:T(8,128)}, f32[576,512]{1,0:T(8,128)S(1)}, u32[]{:S(2)}, u32[]{:S(2)}) collective-permute-start(f32[576,512]{1,0:T(8,128)} %pad_maximum_fusion.15), channel_id=1, source_target_pairs={{0,8},{4,12},{8,0},{12,4},{16,24},{20,28},{24,16},{28,20},{1,9},{5... | collective-permute-start | bytes 3538952 | tf_op jit(solution)/shard_map/ppermute | solution.py:596
  225.1 66.3 %collective-permute-start.49 = (f32[288,1024]{1,0:T(8,128)}, f32[288,1024]{1,0:T(8,128)}, u32[]{:S(2)}, u32[]{:S(2)}) collective-permute-start(f32[288,1024]{1,0:T(8,128)} %collective-permute-done.48.refs_1_), channel_id=1, source_target_pairs={{0,1},{1,0},{2,3},{3,2},{4,5},{5,4},{6,7},{7,6},{8,9},{9,8},{10,11... | collective-permute-start | bytes 3538952 | tf_op jit(solution)/shard_map/ppermute | solution.py:331
  253.1 19.9 %collective-permute-start.40 = (f32[2,512]{1,0:T(2,128)S(1)}, f32[2,512]{1,0:T(2,128)S(1)}, u32[]{:S(2)}, u32[]{:S(2)}) collective-permute-start(f32[2,512]{1,0:T(2,128)S(1)} %pad_maximum_fusion.23), channel_id=1, source_target_pairs={{24,0},{28,4},{25,1},{29,5},{26,2},{30,6},{27,3},{31,7}} | collective-permute-start | bytes 12296 | tf_op jit(solution)/shard_map/ppermute | solution.py:285
  254.4 20.0 %collective-permute-start.39 = (f32[2,512]{1,0:T(2,128)S(1)}, f32[2,512]{1,0:T(2,128)S(1)}, u32[]{:S(2)}, u32[]{:S(2)}) collective-permute-start(f32[2,512]{1,0:T(2,128)S(1)} %pad_maximum_fusion.23), channel_id=1, source_target_pairs={{16,0},{20,4},{24,8},{28,12},{17,1},{21,5},{25,9},{29,13},{18,2},{... | collective-permute-start | bytes 12296 | tf_op jit(solution)/shard_map/ppermute | solution.py:285
  255.7 19.4 %collective-permute-start.38 = (f32[2,512]{1,0:T(2,128)S(1)}, f32[2,512]{1,0:T(2,128)S(1)}, u32[]{:S(2)}, u32[]{:S(2)}) collective-permute-start(f32[2,512]{1,0:T(2,128)S(1)} %pad_maximum_fusion.23), channel_id=1, source_target_pairs={{8,0},{12,4},{16,8},{20,12},{24,16},{28,20},{9,1},{13,5},{17,9},{2... | collective-permute-start | bytes 12296 | tf_op jit(solution)/shard_map/ppermute | solution.py:285
  273.0 26.2 %collective-permute-start.14 = (f32[128,2048]{1,0:T(8,128)S(1)}, f32[128,2048]{1,0:T(8,128)S(1)}, u32[]{:S(2)}, u32[]{:S(2)}) collective-permute-start(f32[128,2048]{1,0:T(8,128)S(1)} %copy-done.62), channel_id=1, source_target_pairs={{0,2},{1,3},{2,0},{3,1},{4,6},{5,7},{6,4},{7,5},{8,10},{9,11},{10,... | collective-permute-start | bytes 3145736 | tf_op jit(solution)/shard_map/ppermute | solution.py:298
  274.4 50.1 %collective-permute-start.20 = (f32[160,2048]{1,0:T(8,128)}, f32[160,2048]{1,0:T(8,128)}, u32[]{:S(2)}, u32[]{:S(2)}) collective-permute-start(f32[160,2048]{1,0:T(8,128)} %convolution_add_fusion.23), channel_id=1, source_target_pairs={{0,2},{1,3},{2,0},{3,1},{4,6},{5,7},{6,4},{7,5},{8,10},{9,11},{10,... | collective-permute-start | bytes 3932168 | tf_op jit(solution)/shard_map/ppermute | solution.py:298
  283.9 29.5 %collective-permute-start.41 = (f32[128,2048]{1,0:T(8,128)}, f32[128,2048]{1,0:T(8,128)}, u32[]{:S(2)}, u32[]{:S(2)}) collective-permute-start(f32[128,2048]{1,0:T(8,128)} %convolution_add_fusion.13), channel_id=1, source_target_pairs={{0,1},{1,0},{2,3},{3,2},{4,5},{5,4},{6,7},{7,6},{8,9},{9,8},{10,11... | collective-permute-start | bytes 3145736 | tf_op jit(solution)/shard_map/ppermute | solution.py:297
  291.4 38.1 %collective-permute-start.44 = (f32[160,2048]{1,0:T(8,128)}, f32[160,2048]{1,0:T(8,128)}, u32[]{:S(2)}, u32[]{:S(2)}) collective-permute-start(f32[160,2048]{1,0:T(8,128)} %convolution_add_fusion.8), channel_id=1, source_target_pairs={{0,1},{1,0},{2,3},{3,2},{4,5},{5,4},{6,7},{7,6},{8,9},{9,8},{10,11... | collective-permute-start | bytes 3932168 | tf_op jit(solution)/shard_map/ppermute | solution.py:297
  299.2 61.0 %collective-permute-start.52 = (f32[1408,256]{1,0:T(8,128)}, f32[1408,256]{1,0:T(8,128)}, u32[]{:S(2)}, u32[]{:S(2)}) collective-permute-start(f32[1408,256]{1,0:T(8,128)} %convolution_add_fusion.4), channel_id=1, source_target_pairs={{0,16},{4,20},{8,24},{12,28},{16,0},{20,4},{24,8},{28,12},{1,17},{... | collective-permute-start | bytes 4325384 | tf_op jit(solution)/shard_map/ppermute | solution.py:525
  311.4 52.3 %collective-permute-start.56 = (f32[288,1024]{1,0:T(8,128)}, f32[288,1024]{1,0:T(8,128)}, u32[]{:S(2)}, u32[]{:S(2)}) collective-permute-start(f32[288,1024]{1,0:T(8,128)} %pad_maximum_fusion.17), channel_id=1, source_target_pairs={{0,8},{4,12},{8,0},{12,4},{16,24},{20,28},{24,16},{28,20},{1,9},{5... | collective-permute-start | bytes 3538952 | tf_op jit(solution)/shard_map/ppermute | solution.py:353
  313.5 50.3 %collective-permute-start.15 = (f32[128,2048]{1,0:T(8,128)}, f32[128,2048]{1,0:T(8,128)}, u32[]{:S(2)}, u32[]{:S(2)}) collective-permute-start(f32[128,2048]{1,0:T(8,128)} %add.757), channel_id=1, source_target_pairs={{0,1},{1,0},{2,3},{3,2},{4,5},{5,4},{6,7},{7,6},{8,9},{9,8},{10,11... | collective-permute-start | bytes 3145736 | tf_op jit(solution)/shard_map/ppermute | solution.py:331
  324.5 41.8 %collective-permute-start.42 = (f32[128,2048]{1,0:T(8,128)}, f32[128,2048]{1,0:T(8,128)}, u32[]{:S(2)}, u32[]{:S(2)}) collective-permute-start(f32[128,2048]{1,0:T(8,128)} %fusion.7), channel_id=1, source_target_pairs={{0,2},{1,3},{2,0},{3,1},{4,6},{5,7},{6,4},{7,5},{8,10},{9,11},{10,... | collective-permute-start | bytes 3145736 | tf_op jit(solution)/shard_map/ppermute | solution.py:298
  329.5 70.3 %collective-permute-start.50 = (f32[512,1408]{1,0:T(8,128)}, f32[512,1408]{1,0:T(8,128)S(1)}, u32[]{:S(2)}, u32[]{:S(2)}) collective-permute-start(f32[512,1408]{1,0:T(8,128)} %fusion.48), channel_id=1, source_target_pairs={{0,4},{4,0},{8,12},{12,8},{16,20},{20,16},{24,28},{28,24},{1,5},{5... | collective-permute-start | bytes 8650760 | tf_op jit(solution)/shard_map/ppermute | solution.py:334
  360.2 92.7 %collective-permute-start.66 = (f32[512,1408]{1,0:T(8,128)S(1)}, f32[512,1408]{1,0:T(8,128)S(1)}, u32[]{:S(2)}, u32[]{:S(2)}) collective-permute-start(f32[512,1408]{1,0:T(8,128)S(1)} %copy-done.133), channel_id=1, source_target_pairs={{0,4},{4,0},{8,12},{12,8},{16,20},{20,16},{24,28},{28,24},{1,5},{5... | collective-permute-start | bytes 8650760 | tf_op jit(solution)/shard_map/ppermute | solution.py:334
  366.3 30.7 %collective-permute-start.45 = (f32[160,2048]{1,0:T(8,128)S(1)}, f32[160,2048]{1,0:T(8,128)S(1)}, u32[]{:S(2)}, u32[]{:S(2)}) collective-permute-start(f32[160,2048]{1,0:T(8,128)S(1)} %fusion.6), channel_id=1, source_target_pairs={{0,2},{1,3},{2,0},{3,1},{4,6},{5,7},{6,4},{7,5},{8,10},{9,11},{10,... | collective-permute-start | bytes 3932168 | tf_op jit(solution)/shard_map/ppermute | solution.py:298
  372.3 109.1 %collective-permute-start.53 = (f32[576,1536]{1,0:T(8,128)S(1)}, f32[576,1536]{1,0:T(8,128)S(1)}, u32[]{:S(2)}, u32[]{:S(2)}) collective-permute-start(f32[576,1536]{1,0:T(8,128)S(1)} %copy-done.63), channel_id=1, source_target_pairs={{0,8},{4,12},{8,0},{12,4},{16,24},{20,28},{24,16},{28,20},{1,9},{5... | collective-permute-start | bytes 10616840 | tf_op jit(solution)/shard_map/ppermute | solution.py:596
  376.9 83.5 %collective-permute-start.43 = (f32[128,2048]{1,0:T(8,128)S(1)}, f32[128,2048]{1,0:T(8,128)S(1)}, u32[]{:S(2)}, u32[]{:S(2)}) collective-permute-start(f32[128,2048]{1,0:T(8,128)S(1)} %fusion.44), channel_id=1, source_target_pairs={{0,1},{1,0},{2,3},{3,2},{4,5},{5,4},{6,7},{7,6},{8,9},{9,8},{10,11... | collective-permute-start | bytes 3145736 | tf_op jit(solution)/shard_map/ppermute | solution.py:331
  399.3 109.7 %collective-permute-start.46 = (f32[160,2048]{1,0:T(8,128)}, f32[160,2048]{1,0:T(8,128)}, u32[]{:S(2)}, u32[]{:S(2)}) collective-permute-start(f32[160,2048]{1,0:T(8,128)} %fusion.35), channel_id=1, source_target_pairs={{0,1},{1,0},{2,3},{3,2},{4,5},{5,4},{6,7},{7,6},{8,9},{9,8},{10,11... | collective-permute-start | bytes 3932168 | tf_op jit(solution)/shard_map/ppermute | solution.py:331
  404.5 137.0 %collective-permute-start.51 = (f32[256,1408]{1,0:T(8,128)}, f32[256,1408]{1,0:T(8,128)}, u32[]{:S(2)}, u32[]{:S(2)}) collective-permute-start(f32[256,1408]{1,0:T(8,128)} %convolution_add_fusion.5), channel_id=1, source_target_pairs={{0,16},{4,20},{8,24},{12,28},{16,0},{20,4},{24,8},{28,12},{1,17},{... | collective-permute-start | bytes 4325384 | tf_op jit(solution)/shard_map/ppermute | solution.py:525
  456.8 133.3 %collective-permute-start.67 = (f32[256,1408]{1,0:T(8,128)}, f32[256,1408]{1,0:T(8,128)}, u32[]{:S(2)}, u32[]{:S(2)}) collective-permute-start(f32[256,1408]{1,0:T(8,128)} %convolution_add_fusion.1), channel_id=1, source_target_pairs={{0,16},{4,20},{8,24},{12,28},{16,0},{20,4},{24,8},{28,12},{1,17},{... | collective-permute-start | bytes 4325384 | tf_op jit(solution)/shard_map/ppermute | solution.py:525
  488.0 56.6 %collective-permute-start.54 = (f32[256,1536]{1,0:T(8,128)}, f32[256,1536]{1,0:T(8,128)}, u32[]{:S(2)}, u32[]{:S(2)}) collective-permute-start(f32[256,1536]{1,0:T(8,128)} %copy-done.135), channel_id=1, source_target_pairs={{0,4},{4,0},{8,12},{12,8},{16,20},{20,16},{24,28},{28,24},{1,5},{5... | collective-permute-start | bytes 4718600 | tf_op jit(solution)/shard_map/ppermute | solution.py:334
  491.4 45.5 %collective-permute-start.58 = (f32[512,256]{1,0:T(8,128)}, f32[512,256]{1,0:T(8,128)}, u32[]{:S(2)}, u32[]{:S(2)}) collective-permute-start(f32[512,256]{1,0:T(8,128)} %fusion.61), channel_id=1, source_target_pairs={{0,4},{4,0},{8,12},{12,8},{16,20},{20,16},{24,28},{28,24},{1,5},{5... | collective-permute-start | bytes 1572872 | tf_op jit(solution)/shard_map/ppermute | solution.py:334
  509.0 58.9 %collective-permute-start.68 = (f32[1408,256]{1,0:T(8,128)}, f32[1408,256]{1,0:T(8,128)}, u32[]{:S(2)}, u32[]{:S(2)}) collective-permute-start(f32[1408,256]{1,0:T(8,128)} %fusion.50), channel_id=1, source_target_pairs={{0,4},{4,0},{8,12},{12,8},{16,20},{20,16},{24,28},{28,24},{1,5},{5... | collective-permute-start | bytes 4325384 | tf_op jit(solution)/shard_map/ppermute | solution.py:334
  536.9 102.7 %collective-permute-start.62 = (f32[256,1536]{1,0:T(8,128)}, f32[256,1536]{1,0:T(8,128)}, u32[]{:S(2)}, u32[]{:S(2)}) collective-permute-start(f32[256,1536]{1,0:T(8,128)} %fusion.58), channel_id=1, source_target_pairs={{0,4},{4,0},{8,12},{12,8},{16,20},{20,16},{24,28},{28,24},{1,5},{5... | collective-permute-start | bytes 4718600 | tf_op jit(solution)/shard_map/ppermute | solution.py:334
  541.5 95.4 %collective-permute-start.65 = (f32[512,256]{1,0:T(8,128)}, f32[512,256]{1,0:T(8,128)}, u32[]{:S(2)}, u32[]{:S(2)}) collective-permute-start(f32[512,256]{1,0:T(8,128)} %convolution_add_fusion.25), channel_id=1, source_target_pairs={{0,16},{4,20},{8,24},{12,28},{16,0},{20,4},{24,8},{28,12},{1,17},{... | collective-permute-start | bytes 1572872 | tf_op jit(solution)/shard_map/ppermute | solution.py:525
  551.5 88.2 %collective-permute-start.63 = (f32[256,1536]{1,0:T(8,128)}, f32[256,1536]{1,0:T(8,128)}, u32[]{:S(2)}, u32[]{:S(2)}) collective-permute-start(f32[256,1536]{1,0:T(8,128)} %copy-done.134), channel_id=1, source_target_pairs={{0,16},{4,20},{8,24},{12,28},{16,0},{20,4},{24,8},{28,12},{1,17},{... | collective-permute-start | bytes 4718600 | tf_op jit(solution)/shard_map/ppermute | solution.py:525
  583.9 53.0 %collective-permute-start.64 = (f32[512,256]{1,0:T(8,128)}, f32[512,256]{1,0:T(8,128)}, u32[]{:S(2)}, u32[]{:S(2)}) collective-permute-start(f32[512,256]{1,0:T(8,128)} %fusion.55), channel_id=1, source_target_pairs={{0,4},{4,0},{8,12},{12,8},{16,20},{20,16},{24,28},{28,24},{1,5},{5... | collective-permute-start | bytes 1572872 | tf_op jit(solution)/shard_map/ppermute | solution.py:334
  590.1 20.8 %collective-permute-start.60 = (f32[8,640]{1,0:T(8,128)S(1)}, f32[8,640]{1,0:T(8,128)S(1)}, u32[]{:S(2)}, u32[]{:S(2)}) collective-permute-start(f32[8,640]{1,0:T(8,128)S(1)} %add.872), channel_id=1, source_target_pairs={{0,4},{4,0},{8,12},{12,8},{16,20},{20,16},{24,28},{28,24},{1,5},{5... | collective-permute-start | bytes 61448 | tf_op jit(solution)/shard_map/ppermute | solution.py:705
  610.9 24.8 %collective-permute-start.61 = (f32[8,640]{1,0:T(8,128)S(1)}, f32[8,640]{1,0:T(8,128)S(1)}, u32[]{:S(2)}, u32[]{:S(2)}) collective-permute-start(f32[8,640]{1,0:T(8,128)S(1)} %add.873), channel_id=1, source_target_pairs={{0,16},{4,20},{8,24},{12,28},{16,0},{20,4},{24,8},{28,12},{1,17},{... | collective-permute-start | bytes 61448 | tf_op jit(solution)/shard_map/ppermute | solution.py:705
  (184 other events, 1802.8 us)
